TPU v7x, 128 devices: a whole 4x4x4 slice. The times are simulated.
128 devices in a mesh: pipe: 4 (over x_hi, core), expert: 32 (over x_lo, y, z).
Axes of the slice: x: 4 (x_hi: 2, x_lo: 2; x = x_hi * 2 + x_lo), y: 4, z: 4, core: 2. Of those that a mesh axis runs over, the one named last changes fastest.
Arguments:
- tokens: bfloat16 [4096, 7168], P('expert'), may hold values from -6 to 6
- cotangent: bfloat16 [4096, 7168], P('expert'), may hold values from -6 to 6
- norm_gain: float32 [7168], replicated, may hold values from 0.1 to 1.9
- expert_ids: int32 [4096, 2], P('expert'), may hold values from 0 to 31, all different within a row; in each aligned block of 128 rows (0 to 127, 128 to 255, ...) at most 12 rows name the same one
- gate_weights: float32 [4096, 2], P('expert'), may hold values from 0.1 to 1
- w_gate: bfloat16 [32, 7168, 2048], P('expert', None, 'pipe'), may hold values from -0.0625 to 0.0625
- w_up: bfloat16 [32, 7168, 2048], P('expert', None, 'pipe'), may hold values from -0.0625 to 0.0625
- w_down: bfloat16 [32, 2048, 7168], P('expert', 'pipe'), may hold values from -0.125 to 0.125
Outputs:
- input_grad: bfloat16 [4096, 7168], P('expert', 'pipe')
Inputs may be any that keep to these rules, and one draw needn't show every extreme that they name: `expert_ids`: each row names 2 different experts. Among the rows of one device no expert is named by more than 12 rows, and in some devices' rows one expert is named by exactly 12.
All inputs are finite; a program needn't handle non-finite values.
Results may differ from a plain program's by a relative error of at most 0.0054.
Values may be sent and summed in bfloat16 or wider, within the bound.
No kernel may reach another device: no remote copies, remote signals or barrier semaphores. Data moves between devices by JAX's collectives and lax.ppermute only.
A program may use at most 128 MiB of HBM per device.

v0:
```python
import jax
import jax.numpy as jnp
from jax import lax
from jax.sharding import PartitionSpec as P

EPSILON = 1e-06


def slot_layout(block_ids, experts, capacity):
    pairs = block_ids.reshape(-1)
    count = pairs.shape[0]
    onehot = (pairs[:, None] == jnp.arange(experts, dtype=jnp.int32)[None, :]).astype(jnp.int32)
    earlier = jnp.cumsum(onehot, axis=0) - onehot
    rank_in = jnp.sum(earlier * onehot, axis=1)
    slot_of = pairs * capacity + rank_in
    matches = (slot_of[None, :] == jnp.arange(experts * capacity, dtype=jnp.int32)[:, None]).astype(
        jnp.int32
    )
    source_pair = jnp.sum(matches * jnp.arange(count, dtype=jnp.int32)[None, :], axis=1)
    filled = jnp.sum(matches, axis=1)
    return (slot_of, source_pair, filled)


def expert_backward(normed_rows, routed_rows, gate_mat, up_mat, down_mat):
    pre_gate = jnp.dot(normed_rows, gate_mat, preferred_element_type=jnp.float32)
    pre_up = jnp.dot(normed_rows, up_mat, preferred_element_type=jnp.float32)
    contract = (((1,), (1,)), ((), ()))
    hidden_grad = lax.dot_general(
        routed_rows, down_mat, contract, preferred_element_type=jnp.float32
    )
    sigma = jax.nn.sigmoid(pre_gate)
    grad_gate = (hidden_grad * pre_up * sigma * (1.0 + pre_gate * (1.0 - sigma))).astype(
        jnp.bfloat16
    )
    grad_up = (hidden_grad * pre_gate * sigma).astype(jnp.bfloat16)
    back = lax.dot_general(grad_gate, gate_mat, contract, preferred_element_type=jnp.float32)
    return back + lax.dot_general(grad_up, up_mat, contract, preferred_element_type=jnp.float32)


def body(tokens, cotangent, norm_gain, expert_ids, gate_weights, w_gate, w_up, w_down):
    experts = lax.axis_size("expert")
    ranks = lax.axis_size("pipe")
    token_count, width = tokens.shape
    top_count = expert_ids.shape[1]
    capacity = token_count * top_count * 3 // (2 * experts)
    columns = width // ranks
    values = tokens.astype(jnp.float32)
    inverse = lax.rsqrt(jnp.mean(values * values, axis=1, keepdims=True) + EPSILON)
    normed = (values * inverse * norm_gain).astype(jnp.bfloat16)
    routed = (gate_weights[:, :, None] * cotangent.astype(jnp.float32)[:, None, :]).astype(
        jnp.bfloat16
    )
    routed = routed.reshape(token_count * top_count, width)
    slot_of, source_pair, filled = slot_layout(expert_ids, experts, capacity)
    mask = filled.astype(jnp.bfloat16)[:, None]
    send_normed = (jnp.take(normed, source_pair // top_count, axis=0) * mask).reshape(
        experts, capacity, width
    )
    send_routed = (jnp.take(routed, source_pair, axis=0) * mask).reshape(experts, capacity, width)
    normed_rows = lax.all_to_all(send_normed, "expert", split_axis=0, concat_axis=0, tiled=True)
    routed_rows = lax.all_to_all(send_routed, "expert", split_axis=0, concat_axis=0, tiled=True)
    sources, items, _ = normed_rows.shape
    back = expert_backward(
        normed_rows.reshape(sources * items, width),
        routed_rows.reshape(sources * items, width),
        w_gate[0],
        w_up[0],
        w_down[0],
    )
    back = back.reshape(sources, items, width)
    returned = lax.all_to_all(back, "expert", split_axis=0, concat_axis=0, tiled=True)
    gathered = jnp.take(returned.reshape(experts * capacity, -1), slot_of, axis=0)
    summed = gathered.reshape(token_count, top_count, -1).sum(axis=1)
    normed_grad = lax.psum_scatter(summed, "pipe", scatter_dimension=1, tiled=True)
    start = lax.axis_index("pipe") * columns
    value_part = lax.dynamic_slice_in_dim(values, start, columns, 1)
    gain_part = lax.dynamic_slice_in_dim(norm_gain, start, columns, 0)
    cotangent_part = lax.dynamic_slice_in_dim(cotangent, start, columns, 1).astype(jnp.float32)
    row_product = lax.psum(
        jnp.sum(normed_grad * gain_part * value_part, axis=1, keepdims=True), "pipe"
    )
    cubed = inverse * inverse * inverse
    input_grad = (
        cotangent_part
        + inverse * gain_part * normed_grad
        - value_part * cubed * row_product / width
    ).astype(jnp.bfloat16)
    return input_grad


def solution(mesh):
    in_specs = (
        P("expert", None),
        P("expert", None),
        P(),
        P("expert", None),
        P("expert", None),
        P("expert", None, "pipe"),
        P("expert", None, "pipe"),
        P("expert", "pipe", None),
    )
    out_specs = P("expert", "pipe")
    return jax.shard_map(body, mesh=mesh, in_specs=in_specs, out_specs=out_specs, check_vma=False)
```

profile of v0, /device:TPU:0, one launch (start us, length us, event | category | flops | bytes accessed | tf_op | source)
XLA Modules:
  0.0 671.5 jit_solution(3540839591152490209)
XLA Ops:
  13.4 6.5 gather_fusion.1
  19.9 8.2 %gather.21 = bf16[32,12,7168]{2,1,0:T(8,128)(2,1)} reshape(bf16[384,7168]{1,0:T(8,128)(2,1)} %gather_fusion.1) | data formatting | bytes 11010048 | tf_op jit(solution)/shard_map/jit(_take)/gather | solution.py:56
  33.2 9.6 %mul.186 = f32[256,7168]{1,0:T(8,128)} reshape(f32[128,2,7168]{2,1,0:T(2,128)} %mul.185) | data formatting | bytes 14680064 | tf_op jit(solution)/shard_map/mul | solution.py:50
  43.1 5.7 multiply_convert_fusion
  48.8 15.9 %gather_fusion = bf16[384,7168]{1,0:T(8,128)(2,1)} fusion(bf16[256,7168]{1,0:T(8,128)(2,1)} %multiply_convert_fusion, s32[1024]{0:T(1024)S(1)} %get-tuple-element.16), kind=kCustom, calls=%fused_computation | custom fusion | bytes 11011584 | tf_op jit(solution)/shard_map/jit(_take)/gather | solution.py:59
  64.7 8.0 %gather.19 = bf16[32,12,7168]{2,1,0:T(8,128)(2,1)} reshape(bf16[384,7168]{1,0:T(8,128)(2,1)} %gather_fusion) | data formatting | bytes 11010048 | tf_op jit(solution)/shard_map/jit(_take)/gather | solution.py:59
  72.9 8.6 %select_multiply_fusion = (bf16[32,12,7168]{2,1,0:T(8,128)(2,1)S(1)}, bf16[32,12,7168]{2,1,0:T(8,128)(2,1)}) fusion(bf16[32,12,7168]{2,1,0:T(8,128)(2,1)} %gather.21, pred[32,12]{1,0:T(8,128)(4,1)S(1)} %get-tuple-element.9, bf16[32,12]{1,0:T(8,128)(2,1)S(1)} %convert_element_type.53, bf16[32,12,7168]{2,1,0:T(8,128)(2,1)} %gather.19, ...), kind=kLoop, calls=%fused_computation.14 | loop fusion | flops 11010048 | bytes 22021632 | tf_op jit(solution)/shard_map/mul | solution.py:56
  81.5 94.9 %all_to_all.15 = bf16[32,12,7168]{2,1,0:T(8,128)(2,1)} all-to-all(bf16[32,12,7168]{2,1,0:T(8,128)(2,1)S(1)} %get-tuple-element.11), channel_id=1, replica_groups=mesh['pipe'=4,'expert'=32] {'expert'}, dimensions={0} | all-to-all | bytes 11010048 | tf_op jit(solution)/shard_map/all_to_all | solution.py:60
  181.5 8.3 %reshape.214 = bf16[384,7168]{1,0:T(8,128)(2,1)} reshape(bf16[32,12,7168]{2,1,0:T(8,128)(2,1)} %all_to_all.15) | data formatting | bytes 11010048 | tf_op jit(solution)/shard_map/reshape | solution.py:64
  189.8 8.6 %fusion.2 = f32[384,512]{1,0:T(8,128)} fusion(bf16[384,7168]{1,0:T(8,128)(2,1)} %reshape.214, bf16[1,7168,512]{2,1,0:T(8,128)(2,1)} %param.13), kind=kOutput, calls=%fused_computation.6 | convolution fusion | flops 2818572288 | bytes 13631488 | tf_op jit(solution)/shard_map/dot_general | solution.py:25
  198.4 77.6 %all-to-all-done = bf16[32,12,7168]{2,1,0:T(8,128)(2,1)} async-done(((bf16[32,12,7168]{2,1,0:T(8,128)(2,1)}), bf16[32,12,7168]{2,1,0:T(8,128)(2,1)}, u32[]{:S(2)}, u32[]{:S(2)}) %all-to-all-start) | async-done | bytes 5505056 | tf_op jit(solution)/shard_map/all_to_all | solution.py:61
  276.1 8.4 %reshape.213 = bf16[384,7168]{1,0:T(8,128)(2,1)} reshape(bf16[32,12,7168]{2,1,0:T(8,128)(2,1)} %all-to-all-done) | data formatting | bytes 11010048 | tf_op jit(solution)/shard_map/reshape | solution.py:65
  284.5 7.1 %fusion.7 = f32[384,512]{1,0:T(8,128)S(1)} fusion(bf16[384,7168]{1,0:T(8,128)(2,1)} %reshape.213, bf16[1,512,7168]{2,1,0:T(8,128)(2,1)} %param.15), kind=kOutput, calls=%fused_computation.11 | convolution fusion | flops 2818572288 | bytes 13631488 | tf_op jit(solution)/shard_map/dot_general | solution.py:28
  292.6 5.8 fusion.18
  301.5 11.0 %convolution_add_fusion = f32[384,7168]{1,0:T(8,128)} fusion(f32[384,7168]{1,0:T(8,128)S(1)} %fusion, bf16[1,7168,512]{2,1,0:T(8,128)(2,1)} %param.14, f32[384,512]{1,0:T(8,128)} %copy-done.3, f32[384,512]{1,0:T(8,128)} %fusion.2), kind=kOutput, calls=%fused_computation.3 | convolution fusion | flops 2822504448 | bytes 30932992 | tf_op jit(solution)/shard_map/dot_general | solution.py:37
  312.5 11.2 %reshape.215 = f32[32,12,7168]{2,1,0:T(8,128)} reshape(f32[384,7168]{1,0:T(8,128)} %convolution_add_fusion) | data formatting | bytes 22020096 | tf_op jit(solution)/shard_map/reshape | solution.py:70
  323.7 11.3 %all-to-all-start.2 = ((f32[32,12,7168]{2,1,0:T(8,128)}), f32[32,12,7168]{2,1,0:T(8,128)}, u32[]{:S(2)}, u32[]{:S(2)}) async-start(f32[32,12,7168]{2,1,0:T(8,128)} %reshape.215), calls=%async_computation.2 | async-start | bytes 29360128 | tf_op jit(solution)/shard_map/all_to_all | solution.py:71
  335.7 210.9 %all-to-all-done.2 = f32[32,12,7168]{2,1,0:T(8,128)} async-done(((f32[32,12,7168]{2,1,0:T(8,128)}), f32[32,12,7168]{2,1,0:T(8,128)}, u32[]{:S(2)}, u32[]{:S(2)}) %all-to-all-start.2) | async-done | bytes 11010080 | tf_op jit(solution)/shard_map/all_to_all | solution.py:71
  546.6 11.5 %reshape.216 = f32[384,7168]{1,0:T(8,128)} reshape(f32[32,12,7168]{2,1,0:T(8,128)} %all-to-all-done.2) | data formatting | bytes 22020096 | tf_op jit(solution)/shard_map/reshape | solution.py:72
  558.1 13.0 %gather_fusion.2 = f32[256,7168]{1,0:T(8,128)} fusion(f32[384,7168]{1,0:T(8,128)} %reshape.216, s32[1024]{0:T(1024)S(1)} %pad_clamp_fusion), kind=kCustom, calls=%fused_computation.2 | custom fusion | bytes 14681088 | tf_op jit(solution)/shard_map/jit(_take)/gather | solution.py:72
  571.1 9.3 %gather.23 = f32[128,2,7168]{2,1,0:T(2,128)} reshape(f32[256,7168]{1,0:T(8,128)} %gather_fusion.2) | data formatting | bytes 14680064 | tf_op jit(solution)/shard_map/jit(_take)/gather | solution.py:72
  580.3 13.4 %select_reduce_fusion = f32[128,7168]{1,0:T(8,128)} fusion(f32[128,2,7168]{2,1,0:T(2,128)} %gather.23, pred[128,2]{1,0:T(8,128)(4,1)S(1)} %copy.24), kind=kLoop, calls=%fused_computation.13 | loop fusion | flops 2752512 | bytes 11010304 | tf_op jit(solution)/shard_map/reduce_sum | solution.py:73
  596.8 56.3 %reduce-scatter.2.cloned.1.call-done = f32[128,1792]{1,0:T(8,128)} async-done(((f32[128,7168]{1,0:T(8,128)}), f32[128,1792]{1,0:T(8,128)}) %reduce-scatter.2.cloned.1.call-update) | async-done | bytes 917520 | tf_op jit(solution)/shard_map/reduce_scatter | solution.py:74
  654.7 7.3 %psum.7 = f32[128]{0:T(128)S(1)} all-reduce(f32[128]{0:T(128)S(1)} %multiply_reduce_fusion.1), channel_id=1, replica_groups=mesh['pipe'=4,'expert'=32] {'pipe'}, use_global_device_ids=true, to_apply=%region_9.10 | all-reduce | flops 128 | bytes 1024 | tf_op jit(solution)/shard_map/psum | solution.py:79
  (68 shorter events, 29.5 us)
Async XLA Ops:
  11.4 8.5 %copy-start.5 = (f32[128]{0:T(128)}, f32[128]{0:T(128)S(1)}, u32[]{:S(2)}) copy-start(f32[128]{0:T(128)S(1)} %get-tuple-element.14) | copy-start | bytes 1540
  19.9 8.2 %copy-start.1 = (bf16[128,7168]{1,0:T(8,128)(2,1)S(1)}, bf16[128,7168]{1,0:T(8,128)(2,1)}, u32[]{:S(2)}) copy-start(bf16[128,7168]{1,0:T(8,128)(2,1)} %param.9) | copy-start | bytes 5505028
  33.2 9.6 %copy-start.7 = (f32[128,2]{0,1:T(2,128)S(1)}, f32[128,2]{0,1:T(2,128)}, u32[]{:S(2)}) copy-start(f32[128,2]{0,1:T(2,128)} %param.12) | copy-start | bytes 3076
  176.4 99.7 %all-to-all-start = ((bf16[32,12,7168]{2,1,0:T(8,128)(2,1)}), bf16[32,12,7168]{2,1,0:T(8,128)(2,1)}, u32[]{:S(2)}, u32[]{:S(2)}) async-start(bf16[32,12,7168]{2,1,0:T(8,128)(2,1)} %get-tuple-element.12), calls=%async_computation | async-start | bytes 14680064 | tf_op jit(solution)/shard_map/all_to_all | solution.py:61
  276.1 16.5 %slice-start.2 = ((s8[7340032]{0:T(1024)(128)(4,1)}), s8[3145728]{0:T(1024)(128)(4,1)S(1)}, s32[]{:S(2)}) async-start(s8[7340032]{0:T(1024)(128)(4,1)} %bitcast.48), calls=%async_computation.7 | async-start | bytes 6291456
  284.5 8.1 %slice-start.3 = ((s8[7340032]{0:T(1024)(128)(4,1)}), s8[4194304]{0:T(1024)(128)(4,1)S(1)}, s32[]{:S(2)}) async-start(s8[7340032]{0:T(1024)(128)(4,1)} %bitcast.48), calls=%async_computation.8 | async-start | bytes 8388608
  284.5 8.1 %copy-start.2 = (f32[384,512]{1,0:T(8,128)S(1)}, f32[384,512]{1,0:T(8,128)}, u32[]{:S(2)}) copy-start(f32[384,512]{1,0:T(8,128)} %fusion.2) | copy-start | bytes 2359300
  284.5 13.9 %slice-start = ((s8[7340032]{0:T(1024)(128)(4,1)}), s8[4194304]{0:T(1024)(128)(4,1)S(1)}, s32[]{:S(2)}) async-start(s8[7340032]{0:T(1024)(128)(4,1)} %bitcast.46), calls=%async_computation.5 | async-start | bytes 8388608
  291.6 0.9 copy-start.3
  292.6 5.9 slice-start.1
  323.7 11.5 %copy-start.4 = (s32[128,2]{0,1:T(2,128)S(1)}, s32[128,2]{0,1:T(2,128)}, u32[]{:S(2)}) copy-start(s32[128,2]{0,1:T(2,128)} %param.11) | copy-start | bytes 3076
  323.7 222.9 %all-to-all-start.2 = ((f32[32,12,7168]{2,1,0:T(8,128)}), f32[32,12,7168]{2,1,0:T(8,128)}, u32[]{:S(2)}, u32[]{:S(2)}) async-start(f32[32,12,7168]{2,1,0:T(8,128)} %reshape.215), calls=%async_computation.2 | async-start | bytes 29360128 | tf_op jit(solution)/shard_map/all_to_all | solution.py:71
  335.0 318.1 %reduce-scatter.2.cloned.1.call-start = ((), (), s32[]{:S(2)}) async-start(), calls=%async_computation.4 | async-start | bytes 4587520 | tf_op jit(solution)/shard_map/reduce_scatter | solution.py:74
  580.3 13.5 %copy-start = (bf16[128,7168]{1,0:T(8,128)(2,1)S(1)}, bf16[128,7168]{1,0:T(8,128)(2,1)}, u32[]{:S(2)}) copy-start(bf16[128,7168]{1,0:T(8,128)(2,1)} %param.8) | copy-start | bytes 5505028
  593.8 68.2 %copy-start.6 = (f32[128]{0:T(128)S(1)}, f32[128]{0:T(128)}, u32[]{:S(2)}) copy-start(f32[128]{0:T(128)} %copy-done.5) | copy-start | bytes 1540
  593.8 68.2 %copy-start.8 = (f32[128]{0:T(128)S(1)}, f32[128]{0:T(128)}, u32[]{:S(2)}) copy-start(f32[128]{0:T(128)} %get-tuple-element.13) | copy-start | bytes 1540
Sparse Core Ops, SparseCore 0:
  593.9 59.1 reduce-scatter.1
where the time goes:
time: 674 us; the launch traced here: 672 us
  waiting for transfers between devices  345 us (51%)
  local copies, waits for them, and re-layouts  119 us (18%)
  blocking collectives  102 us (15%)
  other arithmetic  39.9 us (6%)
  matrix products  35.6 us (5%)
  starting transfers between devices  16.5 us (2%)
  between operations  13.6 us (2%)
    all_to_all x1, waiting for transfers between devices, body(): lax.all_to_all(back, 'expert', split_axis=0, concat_axis=0, tiled=True)  211 us
    all_to_all x1, blocking collectives, body(): lax.all_to_all(send_normed, 'expert', split_axis=0, concat_axis=0, tiled=...  94.9 us
    all_to_all x1, waiting for transfers between devices, body(): lax.all_to_all(send_routed, 'expert', split_axis=0, concat_axis=0, tiled=...  77.6 us
    reduce_scatter x1, waiting for transfers between devices, body(): lax.psum_scatter(summed, 'pipe', scatter_dimension=1, tiled=True)  56.3 us
    gather x2, local copies, waits for them, and re-layouts, body(): jnp.take(routed, source_pair, axis=0) * mask  23.9 us
    gather x2, local copies, waits for them, and re-layouts, body(): jnp.take(returned.reshape(experts * capacity, -1), slot_of, axis=0)  22.2 us
    mul x3, local copies, waits for them, and re-layouts, body(): gate_weights[:, :, None] * cotangent.astype(jnp.float32)[:, None, :]  14.9 us
    gather x2, local copies, waits for them, and re-layouts, body(): jnp.take(normed, source_pair // top_count, axis=0) * mask  14.6 us
  transfers between devices with their start and end apart: 3, of which 3 were waited for; matrix products, arithmetic and copies ran while one was open for 3% of the time, Pallas kernels for 0%

commit v1 on v0

v1 whole, which is shorter than its diff:
```python
import functools

import jax
import jax.numpy as jnp
from jax import lax
from jax.experimental import pallas as pl
from jax.experimental.pallas import tpu as pltpu
from jax.sharding import PartitionSpec as P

EPSILON = 1e-06
BF16 = jnp.bfloat16
F32 = jnp.float32
VMEM_LIMIT = 48 * 1024 * 1024
FILL = 512
DEPTH = 1792
BACK = 896
LANES = 128
LAST = (((1,), (1,)), ((), ()))
CORE_SWAP = [(0, 1), (1, 0), (2, 3), (3, 2)]


def params():
    return pltpu.CompilerParams(vmem_limit_bytes=VMEM_LIMIT)


def whole(shape):
    return pl.BlockSpec(shape, lambda *_: (0,) * len(shape))


def grid_of(grid, in_specs, out_specs, scratch=()):
    return pltpu.PrefetchScalarGridSpec(
        num_scalar_prefetch=1, grid=grid, in_specs=in_specs, out_specs=out_specs, scratch_shapes=scratch
    )


def same_plane(group):
    return [[x * group + k for k in range(group)] for x in range(lax.axis_size("expert") // group)]


def ring_permute(array, steps):
    plane = lax.axis_size("expert") // 2
    moves = []
    for x in range(4):
        for core in range(2):
            to = (x + steps[core]) % 4
            for k in range(plane):
                source = (2 * (x // 2) + core) * 2 * plane + (x % 2) * plane + k
                target = (2 * (to // 2) + core) * 2 * plane + (to % 2) * plane + k
                moves.append((source, target))
    return lax.ppermute(array, ("pipe", "expert"), moves)


def core_swap(array):
    return lax.ppermute(array, "pipe", CORE_SWAP)


def plane_exchange(rows):
    plane = lax.axis_size("expert") // 2
    shaped = rows.reshape(plane, rows.shape[0] // plane, rows.shape[1])
    out = lax.all_to_all(
        shaped, "expert", split_axis=0, concat_axis=0, tiled=True, axis_index_groups=same_plane(plane)
    )
    return out.reshape(rows.shape)


def message_kernel(capacity, other, first, place, *refs):
    tokens, cotangent, gain, ids, weights = refs[:5]
    if first:
        all_tokens, rows, inverse, select = refs[5:]
    else:
        inverse, rows, select = refs[5:]
    top, count = ids.shape

    @pl.when(pl.program_id(0) == 0)
    def _():
        height = select.shape[0]
        plane = height // (2 * capacity)
        expert_of = lax.broadcasted_iota(jnp.int32, (2 * plane, count), 0)
        earlier_of = lax.broadcasted_iota(jnp.int32, (count, count), 0)
        later_of = lax.broadcasted_iota(jnp.int32, (count, count), 1)
        before = (earlier_of < later_of).astype(F32).astype(BF16)
        row = lax.broadcasted_iota(jnp.int32, (height, count), 0)
        taken = jnp.zeros((2 * plane, 1), F32)
        normed_part = jnp.zeros(row.shape, F32)
        base = plane * (1 - place[1] if other else place[1])
        for k in range(top):
            expert = ids[k : k + 1, :]
            named = (expert_of == expert).astype(F32)
            earlier = jnp.dot(named.astype(BF16), before, preferred_element_type=F32) + taken
            rank = jnp.sum(earlier * named, axis=0, keepdims=True).astype(jnp.int32)
            taken = taken + jnp.sum(named, axis=1, keepdims=True)
            local = expert - base
            at = jnp.where((local >= 0) & (local < plane), local * (2 * capacity) + rank, -2 * capacity)
            normed_part = normed_part + (row == at).astype(F32)
            select[:, (k + 1) * count : (k + 2) * count] = (row == at + capacity).astype(F32).astype(BF16)
        select[:, :count] = normed_part.astype(BF16)
        if first:
            values = all_tokens[...].astype(F32)
            inverse[...] = lax.rsqrt(jnp.mean(values * values, axis=1, keepdims=True) + EPSILON)

    normed = (tokens[...].astype(F32) * inverse[...] * gain[...]).astype(BF16)
    values = cotangent[...].astype(F32)
    parts = [normed] + [(weights[:, k : k + 1] * values).astype(BF16) for k in range(top)]
    rows[...] = jnp.dot(select[...], jnp.concatenate(parts, axis=0), preferred_element_type=F32).astype(BF16)


def make_message(place, tokens, cotangent, gain, ids, weights, inverse, capacity, plane, other):
    count, width = tokens.shape
    half = width // 2
    height = plane * 2 * capacity
    steps = half // FILL
    first = inverse is None
    column = lambda i, place: (0, place[0] * steps + i)
    split = [pl.BlockSpec((count, FILL), column), pl.BlockSpec((count, FILL), column), pl.BlockSpec((1, FILL), column)]
    last = (count, width) if first else (count, 1)
    message = jax.ShapeDtypeStruct((height, half), BF16)
    message_spec = pl.BlockSpec((height, FILL), lambda i, place: (0, i))
    out = pl.pallas_call(
        functools.partial(message_kernel, capacity, other, first),
        out_shape=(message, jax.ShapeDtypeStruct((count, 1), F32)) if first else message,
        grid_spec=grid_of(
            (steps,),
            split + [whole(ids.shape), whole(weights.shape), whole(last)],
            (message_spec, whole((count, 1))) if first else message_spec,
            [pltpu.VMEM((height, 3 * count), BF16)],
        ),
        compiler_params=params(),
        name="message",
    )(place, tokens, cotangent, gain, ids, weights, tokens if first else inverse)
    return out


def gather_kernel(capacity, place, ids, out):
    count, top = ids.shape
    rows = out.shape[1]
    plane = rows // (2 * capacity)
    expert_of = lax.broadcasted_iota(jnp.int32, (count, 2 * plane), 1)
    later_of = lax.broadcasted_iota(jnp.int32, (count, count), 0)
    earlier_of = lax.broadcasted_iota(jnp.int32, (count, count), 1)
    before = (earlier_of < later_of).astype(F32).astype(BF16)
    row = lax.broadcasted_iota(jnp.int32, (count, rows), 1)
    taken = jnp.zeros((1, 2 * plane), F32)
    first = jnp.zeros(row.shape, F32)
    second = jnp.zeros(row.shape, F32)
    for k in range(top):
        expert = ids[:, k : k + 1]
        named = (expert_of == expert).astype(F32)
        earlier = jnp.dot(before, named.astype(BF16), preferred_element_type=F32) + taken
        rank = jnp.sum(earlier * named, axis=1, keepdims=True).astype(jnp.int32)
        taken = taken + jnp.sum(named, axis=0, keepdims=True)
        local = expert - place[1] * plane
        at = jnp.where((local >= 0) & (local < plane), local * (2 * capacity) + rank, -2 * capacity)
        first = first + (row == at).astype(F32)
        second = second + (row == at + capacity).astype(F32)
    out[:count, :] = first.astype(BF16)
    out[count:, :] = second.astype(BF16)


def gather_matrix(place, ids, capacity, plane):
    count = ids.shape[0]
    rows = plane * 2 * capacity
    return pl.pallas_call(
        functools.partial(gather_kernel, capacity),
        out_shape=jax.ShapeDtypeStruct((2 * count, rows), BF16),
        grid_spec=grid_of((1,), [whole(ids.shape)], whole((2 * count, rows))),
        compiler_params=params(),
        name="gather_matrix",
    )(place, ids)


def tiles(x, group):
    return x.reshape(x.shape[0] // (8 * group), group, 8, x.shape[1])


def upper(shape):
    return lax.broadcasted_iota(jnp.int32, shape, 1) < 4


def compact(x):
    rows, columns = x.shape
    a, b = tiles(x, 6), tiles(pltpu.roll(x, 4, 0), 6)
    shape = (rows // 48, 8, columns)
    parts = [a[:, 0], jnp.where(upper(shape), a[:, 1], b[:, 3]), b[:, 4]]
    return jnp.concatenate([p[:, None] for p in parts], axis=1).reshape(rows // 2, columns)


def interleave(x, y):
    rows, columns = x.shape
    x0, x1, x2 = tiles(x, 3), tiles(pltpu.roll(x, 4, 0), 3), tiles(pltpu.roll(x, rows - 4, 0), 3)
    y0, y1 = tiles(y, 3), tiles(pltpu.roll(y, 4, 0), 3)
    shape = (rows // 24, 8, columns)
    parts = [
        x0[:, 0],
        jnp.where(upper(shape), x0[:, 1], y1[:, 0]),
        y1[:, 1],
        x1[:, 2],
        jnp.where(upper(shape), x2[:, 2], y0[:, 1]),
        y0[:, 2],
    ]
    return jnp.concatenate([p[:, None] for p in parts], axis=1).reshape(2 * rows, columns)


def project_kernel(capacity, blocks, first, last, place, *refs):
    own, other, gate, up, down = refs[:5]
    rest = list(refs[5:])
    previous = [] if first else [rest.pop(0) for _ in range(3)]
    outs = [rest.pop(0) for _ in range(3)]
    accs = rest if last else outs
    step = pl.program_id(0)

    @pl.when(step == 0)
    def _():
        for number, acc in enumerate(accs):
            acc[...] = jnp.zeros_like(acc) if first else previous[number][...]

    def add(rows):
        x = rows[...]
        accs[0][...] += jnp.dot(x, gate[...], preferred_element_type=F32)
        accs[1][...] += jnp.dot(x, up[...], preferred_element_type=F32)
        accs[2][...] += lax.dot_general(x, down[...], LAST, preferred_element_type=F32)

    @pl.when(step < blocks)
    def _():
        add(own)

    @pl.when(step >= blocks)
    def _():
        add(other)

    if last:

        @pl.when(step == 2 * blocks - 1)
        def _():
            rows = accs[2].shape[0]
            pre_gate = compact(accs[0][...])
            pre_up = compact(accs[1][...])
            hidden = compact(pltpu.roll(accs[2][...], rows - capacity, 0))
            sigma = jax.nn.sigmoid(pre_gate)
            grad_gate = hidden * pre_up * sigma * (1.0 + pre_gate * (1.0 - sigma))
            grad_up = hidden * pre_gate * sigma
            outs[0][...] = grad_gate.astype(BF16)
            outs[1][...] = grad_up.astype(BF16)
            product = jnp.sum(grad_gate * pre_gate + grad_up * pre_up, axis=1, keepdims=True)
            outs[2][...] = jnp.broadcast_to(product, outs[2].shape)


def project(place, own, other, weights, at, previous, last, capacity):
    gate, up, down = weights
    rows, columns = own.shape
    width, hidden = gate.shape
    blocks = columns // DEPTH if columns % DEPTH == 0 else columns // 256
    depth = columns // blocks
    per_half = width // 2 // depth
    start = at // depth

    def at_block(i, place):
        side = jnp.where(i < blocks, place[0], 1 - place[0])
        return side * per_half + start + lax.rem(i, blocks)

    acc = jax.ShapeDtypeStruct((rows, hidden), F32)
    grad = jax.ShapeDtypeStruct((rows // 2, hidden), BF16)
    product = jax.ShapeDtypeStruct((rows // 2, LANES), F32)
    outs = (grad, grad, product) if last else (acc,) * 3
    return pl.pallas_call(
        functools.partial(project_kernel, capacity, blocks, not previous, last),
        out_shape=outs,
        grid_spec=grid_of(
            (2 * blocks,),
            [
                pl.BlockSpec((rows, depth), lambda i, place: (0, jnp.minimum(i, blocks - 1))),
                pl.BlockSpec((rows, depth), lambda i, place: (0, jnp.maximum(i - blocks, 0))),
                pl.BlockSpec((depth, hidden), lambda i, place: (at_block(i, place), 0)),
                pl.BlockSpec((depth, hidden), lambda i, place: (at_block(i, place), 0)),
                pl.BlockSpec((hidden, depth), lambda i, place: (0, at_block(i, place))),
            ]
            + [whole((rows, hidden))] * len(previous),
            tuple(whole(o.shape) for o in outs),
            [pltpu.VMEM((rows, hidden), F32)] * 3 if last else [],
        ),
        compiler_params=params(),
        name="project",
    )(place, own, other, gate, up, down, *previous)


def back_kernel(place, *refs):
    grad_gate, grad_up, product, gate_0, gate_1, up_0, up_1 = refs[:7]
    out = refs[-1]
    other = refs[7] if len(refs) == 9 else None
    columns = out.shape[1] - LANES

    def one(gate, up):
        total = lax.dot_general(grad_gate[...], gate[...], LAST, preferred_element_type=F32)
        return total + lax.dot_general(grad_up[...], up[...], LAST, preferred_element_type=F32)

    def put(rows, at):
        if other is not None:
            rows = rows + other[:, at].astype(F32)
        out[:, at] = rows.astype(BF16)

    step = pl.program_id(0)
    put(interleave(one(gate_0, up_0), one(gate_1, up_1)), pl.ds(pl.multiple_of(step * BACK, LANES), BACK))

    @pl.when(step == 0)
    def _():
        put(interleave(product[...], product[...]), pl.ds(columns, LANES))


def back(place, grads, weights, other):
    gate, up, _ = weights
    rows, hidden = grads[0].shape
    columns = gate.shape[0] // 4
    steps = columns // BACK

    def quarter(high):
        def index(i, place):
            side = 1 - place[0] if other is None else place[0]
            return ((2 * high + side) * steps + i, 0)

        return pl.BlockSpec((BACK, hidden), index)

    shape = (2 * rows, columns + LANES)
    extra = [] if other is None else [other]
    return pl.pallas_call(
        back_kernel,
        out_shape=jax.ShapeDtypeStruct(shape, BF16),
        grid_spec=grid_of(
            (steps,),
            [whole(g.shape) for g in grads]
            + [quarter(0), quarter(1), quarter(0), quarter(1)]
            + [whole(shape)] * len(extra),
            whole(shape),
        ),
        compiler_params=params(),
        name="back",
    )(place, *grads, gate, gate, up, up, *extra)


def combine_kernel(place, gather, rows, first, second):
    count = first.shape[0]
    total = jnp.dot(gather[...], rows[...], preferred_element_type=F32)
    low, high = total[:count], total[count:]
    flip = place[2] == 1
    first[...] = jnp.where(flip, high, low).astype(first.dtype)
    second[...] = jnp.where(flip, low, high).astype(second.dtype)


def combine(place, gather, rows, first_type):
    count = gather.shape[0] // 2
    columns = rows.shape[1]
    part = columns // 3
    block = pl.BlockSpec((count, part), lambda i, place: (0, i))
    return pl.pallas_call(
        combine_kernel,
        out_shape=(
            jax.ShapeDtypeStruct((count, columns), first_type),
            jax.ShapeDtypeStruct((count, columns), BF16),
        ),
        grid_spec=grid_of(
            (3,),
            [whole(gather.shape), pl.BlockSpec((rows.shape[0], part), lambda i, place: (0, i))],
            (block, block),
        ),
        compiler_params=params(),
        name="combine",
    )(place, gather, rows)


def body(tokens, cotangent, norm_gain, expert_ids, gate_weights, w_gate, w_up, w_down):
    experts = lax.axis_size("expert")
    plane = experts // 2
    token_count, width = tokens.shape
    top_count = expert_ids.shape[1]
    capacity = token_count * top_count * 3 // (2 * experts)
    columns = width // lax.axis_size("pipe")
    pipe = lax.axis_index("pipe")
    core, high = lax.rem(pipe, 2), pipe // 2
    low = lax.axis_index("expert") // plane
    after = lax.rem(2 * high + low + 1, 4) // 2
    place = jnp.stack([core, low, high]).astype(jnp.int32)
    place_after = jnp.stack([core, low, after]).astype(jnp.int32)
    weights = (w_gate[0], w_up[0], w_down[0])

    gain = norm_gain.reshape(1, width)
    make = functools.partial(
        make_message, place, tokens, cotangent, gain, expert_ids.T, gate_weights, capacity=capacity, plane=plane
    )
    other, inverse = make(inverse=None, other=True)
    own = make(inverse=inverse, other=False)
    other_ids = lax.ppermute(expert_ids, "expert", [(k, (k + plane) % experts) for k in range(experts)])
    gathers = [gather_matrix(place, ids, capacity, plane) for ids in (expert_ids, other_ids)]

    other = ring_permute(other, (1, 3))
    own = plane_exchange(own)
    other = plane_exchange(other)

    grads = project(place, own, core_swap(own), weights, 0, (), True, capacity)
    theirs = core_swap(back(place, grads, weights, None))
    mine = back(place, grads, weights, theirs)

    mine, other = lax.optimization_barrier((mine, other))
    own_back = plane_exchange(mine)
    grads = project(place, other, core_swap(other), weights, 0, (), True, capacity)
    theirs = core_swap(back(place, grads, weights, None))
    mine = back(place, grads, weights, theirs)
    other_back = plane_exchange(mine)

    kept, sent = combine(place, gathers[0], own_back, F32)
    from_far = ring_permute(sent, (2, 2))
    forth, back_ = combine(place_after, gathers[1], other_back, BF16)
    from_before = ring_permute(forth, (1, 1))
    from_after = ring_permute(back_, (3, 3))

    def own_columns(array):
        return lax.dynamic_slice_in_dim(array, pipe * columns, columns, array.ndim - 1)

    total = kept + from_far.astype(F32) + from_before.astype(F32) + from_after.astype(F32)
    normed_grad, product = total[:, :columns], total[:, columns : columns + 1]
    value_part = own_columns(tokens).astype(F32)
    cotangent_part = own_columns(cotangent).astype(F32)
    return (
        cotangent_part
        + inverse * own_columns(norm_gain) * normed_grad
        - value_part * (inverse * inverse * product / width)
    ).astype(BF16)


def solution(mesh):
    in_specs = (
        P("expert", None),
        P("expert", None),
        P(),
        P("expert", None),
        P("expert", None),
        P("expert", None, "pipe"),
        P("expert", None, "pipe"),
        P("expert", "pipe", None),
    )
    out_specs = P("expert", "pipe")
    return jax.shard_map(body, mesh=mesh, in_specs=in_specs, out_specs=out_specs, check_vma=False)
```

time: 674 us -> 209 us (0.31)
  waiting for transfers between devices: 345 us -> 89.1 us
  local copies, waits for them, and re-layouts: 119 us -> 7.08 us
  blocking collectives: 102 us -> 0 us
  Pallas kernels: 0 us -> 72.5 us
  other arithmetic: 39.9 us -> 3.74 us
  matrix products: 35.6 us -> 0 us
  starting transfers between devices: 16.5 us -> 36.3 us
  between operations: 13.6 us -> 0.12 us
    all_to_all x2 -> x4, waiting for transfers between devices: 289 us -> 71.7 us  [plane_exchange(): lax.all_to_all(shaped, 'expert', split_axis=0, concat_axis=0, tiled=True,...]
    all_to_all x1 -> x0, blocking collectives: 94.9 us -> none  [body(): lax.all_to_all(send_normed, 'expert', split_axis=0, concat_axis=0, tiled=...]
    pallas_call x0 -> x12, Pallas kernels: none -> 72.5 us  [the longest x2 28.2 us: project(): pl.pallas_call(functools.partial(project_kernel, capacity, blocks, not pr...]
    gather x6 -> x0, local copies, waits for them, and re-layouts: 60.8 us -> none  [the longest x2 23.9 us: body(): jnp.take(routed, source_pair, axis=0) * mask]
    reduce_scatter x1 -> x0, waiting for transfers between devices: 56.3 us -> none  [body(): lax.psum_scatter(summed, 'pipe', scatter_dimension=1, tiled=True)]
    reshape x5 -> x0, local copies, waits for them, and re-layouts: 39.5 us -> none  [the longest x1 11.5 us: body(): returned.reshape(experts * capacity, -1)]
    dot_general x5 -> x0, matrix products: 35.6 us -> none  [the longest x1 11 us: expert_backward(): lax.dot_general(grad_up, up_mat, contract, preferred_element_type=jnp.flo...]
    ppermute x0 -> x9, waiting for transfers between devices: none -> 17.4 us  [the longest x4 8.59 us: core_swap(): return lax.ppermute(array, 'pipe', CORE_SWAP)]
  transfers between devices with their start and end apart: 3 -> 13, of which waited for: 3 -> 9; matrix products, arithmetic and copies ran while one was open for 3% -> 0% of each run, Pallas kernels for 0% -> 19%
where the time goes in v1:
time: 209 us
  waiting for transfers between devices  89.1 us (43%)
  Pallas kernels  72.5 us (35%)
  starting transfers between devices  36.3 us (17%)
  local copies, waits for them, and re-layouts  7.08 us (3%)
  other arithmetic  3.74 us (2%)
    all_to_all x4, waiting for transfers between devices, plane_exchange(): lax.all_to_all(shaped, 'expert', split_axis=0, concat_axis=0, tiled=True,...  71.7 us
    pallas_call x2, Pallas kernels, project(): pl.pallas_call(functools.partial(project_kernel, capacity, blocks, not pr...  28.2 us
    all_to_all x4, starting transfers between devices, plane_exchange(): lax.all_to_all(shaped, 'expert', split_axis=0, concat_axis=0, tiled=True,...  26.6 us
    pallas_call x4, Pallas kernels, back(): pl.pallas_call(back_kernel, out_shape=jax.ShapeDtypeStruct(shape, BF16),...  24.5 us
    pallas_call x2, Pallas kernels, make_message(): pl.pallas_call(functools.partial(message_kernel, capacity, other, first),...  12.2 us
    ppermute x4, waiting for transfers between devices, core_swap(): return lax.ppermute(array, 'pipe', CORE_SWAP)  8.59 us
    ppermute x4, starting transfers between devices, ring_permute(): return lax.ppermute(array, ('pipe', 'expert'), moves)  7.81 us
    ppermute x4, waiting for transfers between devices, ring_permute(): return lax.ppermute(array, ('pipe', 'expert'), moves)  7.12 us
  transfers between devices with their start and end apart: 13, of which 9 were waited for; matrix products, arithmetic and copies ran while one was open for 0% of the time, Pallas kernels for 19%

profile of v1, /device:TPU:0, one launch (start us, length us, event | category | flops | bytes accessed | tf_op | source)
XLA Modules:
  0.0 208.8 jit_solution(9920861206914020095)
XLA Ops:
  5.3 6.3 %message.2 = (bf16[384,3584]{1,0:T(8,128)(2,1)}, f32[128,1]{1,0:T(8,128)S(1)}) custom-call(s32[3]{0:T(128)S(1)} %pad_add_fusion.place, bf16[128,7168]{1,0:T(8,128)(2,1)S(1)} %copy-done, bf16[128,7168]{1,0:T(8,128)(2,1)S(1)} %copy-done.1, f32[1,7168]{1,0:T(1,128)S(1)} %bitcast.21, s32[2,128]{1,0:T(2,128)S(1)} %bitcast.23, f32[128,2]{1,0:T(8,128)S(1)} %copy.13.refs_4_, ...), custom_call_target="tpu_custom_call" | custom-call | tf_op jit(solution)/shard_map/message/pallas_call | solution.py:118
  11.6 5.9 %message.3 = bf16[384,3584]{1,0:T(8,128)(2,1)} custom-call(s32[3]{0:T(128)S(1)} %pad_add_fusion.place, bf16[128,7168]{1,0:T(8,128)(2,1)S(1)} %copy-done, bf16[128,7168]{1,0:T(8,128)(2,1)S(1)} %copy-done.1, f32[1,7168]{1,0:T(1,128)S(1)} %bitcast.22, s32[2,128]{1,0:T(2,128)S(1)} %bitcast.24, f32[128,2]{1,0:T(8,128)S(1)} %copy.13.refs_4_, ...), custom_call_target="tpu_custom_call" | custom-call | tf_op jit(solution)/shard_map/message/pallas_call | solution.py:118
  17.5 8.4 %all-to-all-start = ((bf16[16,24,3584]{2,1,0:T(8,128)(2,1)}), bf16[16,24,3584]{2,1,0:T(8,128)(2,1)}, u32[]{:S(2)}, u32[]{:S(2)}) async-start(bf16[16,24,3584]{2,1,0:T(8,128)(2,1)} %bitcast.47), calls=%async_computation | async-start | bytes 5505024 | tf_op jit(solution)/shard_map/all_to_all | solution.py:60
  27.5 37.0 %all-to-all-done = bf16[16,24,3584]{2,1,0:T(8,128)(2,1)} async-done(((bf16[16,24,3584]{2,1,0:T(8,128)(2,1)}), bf16[16,24,3584]{2,1,0:T(8,128)(2,1)}, u32[]{:S(2)}, u32[]{:S(2)}) %all-to-all-start) | async-done | bytes 2752544 | tf_op jit(solution)/shard_map/all_to_all | solution.py:60
  64.6 5.1 %all-to-all-start.1 = ((bf16[16,24,3584]{2,1,0:T(8,128)(2,1)}), bf16[16,24,3584]{2,1,0:T(8,128)(2,1)S(1)}, u32[]{:S(2)}, u32[]{:S(2)}) async-start(bf16[16,24,3584]{2,1,0:T(8,128)(2,1)} %bitcast.10), calls=%async_computation.1 | async-start | bytes 5505024 | tf_op jit(solution)/shard_map/all_to_all | solution.py:60
  70.0 14.6 %project.2 = (bf16[192,512]{1,0:T(8,128)(2,1)S(1)}, bf16[192,512]{1,0:T(8,128)(2,1)S(1)}, f32[192,128]{1,0:T(8,128)S(1)}) custom-call(s32[3]{0:T(128)S(1)} %pad_add_fusion.place, bf16[384,3584]{1,0:T(8,128)(2,1)} %bitcast.6.refs_0_, bf16[384,3584]{1,0:T(8,128)(2,1)} %collective-permute-done.refs_1_, bf16[7168,512]{1,0:T(8,128)(2,1)} %bitcast.25, ...), custom_call_target="tpu_custom_call" | custom-call | tf_op jit(solution)/shard_map/project/pallas_call | solution.py:264
  84.6 5.3 %back.4 = bf16[384,1920]{1,0:T(8,128)(2,1)S(1)} custom-call(s32[3]{0:T(128)S(1)} %pad_add_fusion.place, bf16[192,512]{1,0:T(8,128)(2,1)S(1)} %get-tuple-element.20.refs_0_, bf16[192,512]{1,0:T(8,128)(2,1)S(1)} %get-tuple-element.21.refs_1_, f32[192,128]{1,0:T(8,128)S(1)} %get-tuple-element.22.refs_2_, bf16[7168,512]{1,0:T(8,128)(2,1)} %bitcast.26, ...), custom_call_target="tpu_custom_call" | custom-call | tf_op jit(solution)/shard_map/back/pallas_call | solution.py:323
  90.1 3.1 %collective-permute-done.1.refs_7_ = bf16[384,1920]{1,0:T(8,128)(2,1)S(1)} collective-permute-done((bf16[384,1920]{1,0:T(8,128)(2,1)S(1)}, bf16[384,1920]{1,0:T(8,128)(2,1)S(1)}, u32[]{:S(2)}, u32[]{:S(2)}) %collective-permute-start.1) | collective-permute-done | bytes 1474592 | tf_op jit(solution)/shard_map/ppermute | solution.py:54
  93.2 6.4 %back.5 = bf16[384,1920]{1,0:T(8,128)(2,1)} custom-call(s32[3]{0:T(128)S(1)} %pad_add_fusion.place, bf16[192,512]{1,0:T(8,128)(2,1)S(1)} %get-tuple-element.20.refs_0_, bf16[192,512]{1,0:T(8,128)(2,1)S(1)} %get-tuple-element.21.refs_1_, f32[192,128]{1,0:T(8,128)S(1)} %get-tuple-element.22.refs_2_, bf16[7168,512]{1,0:T(8,128)(2,1)} %bitcast.28, ...), custom_call_target="tpu_custom_call" | custom-call | tf_op jit(solution)/shard_map/back/pallas_call | solution.py:323
  99.6 8.2 %all-to-all-done.1 = bf16[16,24,3584]{2,1,0:T(8,128)(2,1)S(1)} async-done(((bf16[16,24,3584]{2,1,0:T(8,128)(2,1)}), bf16[16,24,3584]{2,1,0:T(8,128)(2,1)S(1)}, u32[]{:S(2)}, u32[]{:S(2)}) %all-to-all-start.1) | async-done | bytes 2752544 | tf_op jit(solution)/shard_map/all_to_all | solution.py:60
  107.9 5.1 %collective-permute-done.5.refs_1_ = bf16[384,3584]{1,0:T(8,128)(2,1)S(1)} collective-permute-done((bf16[384,3584]{1,0:T(8,128)(2,1)S(1)}, bf16[384,3584]{1,0:T(8,128)(2,1)S(1)}, u32[]{:S(2)}, u32[]{:S(2)}) %collective-permute-start.5) | collective-permute-done | bytes 2752544 | tf_op jit(solution)/shard_map/ppermute | solution.py:54
  113.0 13.7 %project.3 = (bf16[192,512]{1,0:T(8,128)(2,1)S(1)}, bf16[192,512]{1,0:T(8,128)(2,1)S(1)}, f32[192,128]{1,0:T(8,128)S(1)}) custom-call(s32[3]{0:T(128)S(1)} %pad_add_fusion.place, bf16[384,3584]{1,0:T(8,128)(2,1)S(1)} %bitcast.18, bf16[384,3584]{1,0:T(8,128)(2,1)S(1)} %collective-permute-done.5.refs_1_, bf16[7168,512]{1,0:T(8,128)(2,1)} %bitcast.30, ...), custom_call_target="tpu_custom_call" | custom-call | tf_op jit(solution)/shard_map/project/pallas_call | solution.py:264
  126.6 6.4 %back.6 = bf16[384,1920]{1,0:T(8,128)(2,1)} custom-call(s32[3]{0:T(128)S(1)} %pad_add_fusion.place, bf16[192,512]{1,0:T(8,128)(2,1)S(1)} %get-tuple-element.28.refs_0_, bf16[192,512]{1,0:T(8,128)(2,1)S(1)} %get-tuple-element.29.refs_1_, f32[192,128]{1,0:T(8,128)S(1)} %get-tuple-element.30.refs_2_, bf16[7168,512]{1,0:T(8,128)(2,1)} %bitcast.31, ...), custom_call_target="tpu_custom_call" | custom-call | tf_op jit(solution)/shard_map/back/pallas_call | solution.py:323
  133.2 9.4 %all-to-all-start.2 = ((bf16[16,24,1920]{2,1,0:T(8,128)(2,1)}), bf16[16,24,1920]{2,1,0:T(8,128)(2,1)S(1)}, u32[]{:S(2)}, u32[]{:S(2)}) async-start(bf16[16,24,1920]{2,1,0:T(8,128)(2,1)} %bitcast.12), calls=%async_computation.2 | async-start | bytes 2949120 | tf_op jit(solution)/shard_map/all_to_all | solution.py:60
  142.5 6.4 %back.7 = bf16[384,1920]{1,0:T(8,128)(2,1)} custom-call(s32[3]{0:T(128)S(1)} %pad_add_fusion.place, bf16[192,512]{1,0:T(8,128)(2,1)S(1)} %get-tuple-element.28.refs_0_, bf16[192,512]{1,0:T(8,128)(2,1)S(1)} %get-tuple-element.29.refs_1_, f32[192,128]{1,0:T(8,128)S(1)} %get-tuple-element.30.refs_2_, bf16[7168,512]{1,0:T(8,128)(2,1)} %bitcast.33, ...), custom_call_target="tpu_custom_call" | custom-call | tf_op jit(solution)/shard_map/back/pallas_call | solution.py:323
  149.0 17.1 %all-to-all-done.2 = bf16[16,24,1920]{2,1,0:T(8,128)(2,1)S(1)} async-done(((bf16[16,24,1920]{2,1,0:T(8,128)(2,1)}), bf16[16,24,1920]{2,1,0:T(8,128)(2,1)S(1)}, u32[]{:S(2)}, u32[]{:S(2)}) %all-to-all-start.2) | async-done | bytes 1474592 | tf_op jit(solution)/shard_map/all_to_all | solution.py:60
  166.0 3.7 %all-to-all-start.3 = ((bf16[16,24,1920]{2,1,0:T(8,128)(2,1)}), bf16[16,24,1920]{2,1,0:T(8,128)(2,1)S(1)}, u32[]{:S(2)}, u32[]{:S(2)}) async-start(bf16[16,24,1920]{2,1,0:T(8,128)(2,1)} %bitcast.15), calls=%async_computation.3 | async-start | bytes 2949120 | tf_op jit(solution)/shard_map/all_to_all | solution.py:60
  175.2 2.8 %combine.2 = (f32[128,1920]{1,0:T(8,128)S(1)}, bf16[128,1920]{1,0:T(8,128)(2,1)}) custom-call(s32[3]{0:T(128)S(1)} %pad_add_fusion.place, bf16[256,384]{1,0:T(8,128)(2,1)S(1)} %gather_matrix.2.gather, bf16[384,1920]{1,0:T(8,128)(2,1)S(1)} %bitcast.19), custom_call_target="tpu_custom_call" | custom-call | tf_op jit(solution)/shard_map/combine/pallas_call | solution.py:352
  179.0 3.0 %collective-permute-start.3 = (bf16[128,1920]{1,0:T(8,128)(2,1)}, bf16[128,1920]{1,0:T(8,128)(2,1)}, u32[]{:S(2)}, u32[]{:S(2)}) collective-permute-start(bf16[128,1920]{1,0:T(8,128)(2,1)} %get-tuple-element.26), channel_id=1, source_target_pairs={{0,64},{1,65},{2,66},{3,67},{4,68},{5,69},{6,70},{7,71},{8,72},{9,... | collective-permute-start | bytes 1474568 | tf_op jit(solution)/shard_map/ppermute | solution.py:50
  182.0 9.4 %all-to-all-done.3 = bf16[16,24,1920]{2,1,0:T(8,128)(2,1)S(1)} async-done(((bf16[16,24,1920]{2,1,0:T(8,128)(2,1)}), bf16[16,24,1920]{2,1,0:T(8,128)(2,1)S(1)}, u32[]{:S(2)}, u32[]{:S(2)}) %all-to-all-start.3) | async-done | bytes 1474592 | tf_op jit(solution)/shard_map/all_to_all | solution.py:60
  191.4 2.7 %combine.3 = (bf16[128,1920]{1,0:T(8,128)(2,1)}, bf16[128,1920]{1,0:T(8,128)(2,1)S(1)}) custom-call(s32[3]{0:T(128)S(1)} %pad_add_fusion.2.place, bf16[256,384]{1,0:T(8,128)(2,1)S(1)} %gather_matrix.3.gather, bf16[384,1920]{1,0:T(8,128)(2,1)S(1)} %bitcast.20), custom_call_target="tpu_custom_call" | custom-call | tf_op jit(solution)/shard_map/combine/pallas_call | solution.py:352
  195.6 1.7 collective-permute-start.8
  198.1 7.1 %collective-permute-done.7 = bf16[128,1920]{1,0:T(8,128)(2,1)S(1)} collective-permute-done((bf16[128,1920]{1,0:T(8,128)(2,1)}, bf16[128,1920]{1,0:T(8,128)(2,1)S(1)}, u32[]{:S(2)}, u32[]{:S(2)}) %collective-permute-start.7) | collective-permute-done | bytes 491552 | tf_op jit(solution)/shard_map/ppermute | solution.py:50
  206.6 2.2 %fusion.2 = bf16[128,1792]{1,0:T(8,128)(2,1)} fusion(f32[128,1920]{1,0:T(8,128)S(1)} %convert_add_fusion, f32[128]{0:T(128)S(1)} %get-tuple-element.34, bf16[128,7168]{1,0:T(8,128)(2,1)} %refs_0_.3, s32[]{:T(128)S(6)} %select_n.16, f32[1792]{0:T(1024)S(1)} %dynamic_slice.10, f32[128]{0:T(128)S(1)} %get-tuple-element.33, bf16[128,7168]{1,0:T(8,128)(2,1)} %refs_1_.3), kind=kLoop, calls=%fused_computation.4 | loop fusion | flops 1835008 | bytes 2301956 | tf_op jit(solution)/shard_map/convert_element_type | solution.py:424
  (38 shorter events, 17.6 us)
Async XLA Ops:
  0.9 1.5 copy-start
  2.4 1.5 copy-start.1
  3.9 0.7 copy-start.4
  4.6 0.7 copy-start.5
  17.5 8.5 %copy-start.7 = (bf16[384,3584]{1,0:T(8,128)(2,1)S(1)}, bf16[384,3584]{1,0:T(8,128)(2,1)}, u32[]{:S(2)}) copy-start(bf16[384,3584]{1,0:T(8,128)(2,1)} %get-tuple-element.23) | copy-start | bytes 8257540
  17.5 47.0 %all-to-all-start = ((bf16[16,24,3584]{2,1,0:T(8,128)(2,1)}), bf16[16,24,3584]{2,1,0:T(8,128)(2,1)}, u32[]{:S(2)}, u32[]{:S(2)}) async-start(bf16[16,24,3584]{2,1,0:T(8,128)(2,1)} %bitcast.47), calls=%async_computation | async-start | bytes 5505024 | tf_op jit(solution)/shard_map/all_to_all | solution.py:60
  26.0 38.6 %collective-permute-start.2 = (bf16[384,3584]{1,0:T(8,128)(2,1)S(1)}, bf16[384,3584]{1,0:T(8,128)(2,1)}, u32[]{:S(2)}, u32[]{:S(2)}) collective-permute-start(bf16[384,3584]{1,0:T(8,128)(2,1)S(1)} %copy-done.7), channel_id=1, source_target_pairs={{0,16},{1,17},{2,18},{3,19},{4,20},{5,21},{6,22},{7,23},{8,24},{9,... | collective-permute-start | bytes 8257544 | tf_op jit(solution)/shard_map/ppermute | solution.py:50
  64.6 5.4 %collective-permute-start = (bf16[384,3584]{1,0:T(8,128)(2,1)}, bf16[384,3584]{1,0:T(8,128)(2,1)}, u32[]{:S(2)}, u32[]{:S(2)}) collective-permute-start(bf16[384,3584]{1,0:T(8,128)(2,1)} %bitcast.6.refs_0_), channel_id=1, source_target_pairs={{0,32},{32,0},{64,96},{96,64},{1,33},{33,1},{65,97},{97,65},{2,34}... | collective-permute-start | bytes 8257544 | tf_op jit(solution)/shard_map/ppermute | solution.py:54
  64.6 43.3 %all-to-all-start.1 = ((bf16[16,24,3584]{2,1,0:T(8,128)(2,1)}), bf16[16,24,3584]{2,1,0:T(8,128)(2,1)S(1)}, u32[]{:S(2)}, u32[]{:S(2)}) async-start(bf16[16,24,3584]{2,1,0:T(8,128)(2,1)} %bitcast.10), calls=%async_computation.1 | async-start | bytes 5505024 | tf_op jit(solution)/shard_map/all_to_all | solution.py:60
  89.9 3.3 %collective-permute-start.1 = (bf16[384,1920]{1,0:T(8,128)(2,1)S(1)}, bf16[384,1920]{1,0:T(8,128)(2,1)S(1)}, u32[]{:S(2)}, u32[]{:S(2)}) collective-permute-start(bf16[384,1920]{1,0:T(8,128)(2,1)S(1)} %back.4), channel_id=1, source_target_pairs={{0,32},{32,0},{64,96},{96,64},{1,33},{33,1},{65,97},{97,65},{2,34}... | collective-permute-start | bytes 4423688 | tf_op jit(solution)/shard_map/ppermute | solution.py:54
  107.9 5.1 %collective-permute-start.5 = (bf16[384,3584]{1,0:T(8,128)(2,1)S(1)}, bf16[384,3584]{1,0:T(8,128)(2,1)S(1)}, u32[]{:S(2)}, u32[]{:S(2)}) collective-permute-start(bf16[384,3584]{1,0:T(8,128)(2,1)S(1)} %bitcast.17), channel_id=1, source_target_pairs={{0,32},{32,0},{64,96},{96,64},{1,33},{33,1},{65,97},{97,65},{2,34}... | collective-permute-start | bytes 8257544 | tf_op jit(solution)/shard_map/ppermute | solution.py:54
  133.0 9.5 %collective-permute-start.6 = (bf16[384,1920]{1,0:T(8,128)(2,1)}, bf16[384,1920]{1,0:T(8,128)(2,1)S(1)}, u32[]{:S(2)}, u32[]{:S(2)}) collective-permute-start(bf16[384,1920]{1,0:T(8,128)(2,1)} %back.6), channel_id=1, source_target_pairs={{0,32},{32,0},{64,96},{96,64},{1,33},{33,1},{65,97},{97,65},{2,34}... | collective-permute-start | bytes 4423688 | tf_op jit(solution)/shard_map/ppermute | solution.py:54
  133.2 32.9 %all-to-all-start.2 = ((bf16[16,24,1920]{2,1,0:T(8,128)(2,1)}), bf16[16,24,1920]{2,1,0:T(8,128)(2,1)S(1)}, u32[]{:S(2)}, u32[]{:S(2)}) async-start(bf16[16,24,1920]{2,1,0:T(8,128)(2,1)} %bitcast.12), calls=%async_computation.2 | async-start | bytes 2949120 | tf_op jit(solution)/shard_map/all_to_all | solution.py:60
  149.0 20.8 %copy-start.6 = (s32[128,2]{0,1:T(2,128)S(1)}, s32[128,2]{0,1:T(2,128)}, u32[]{:S(2)}) copy-start(s32[128,2]{0,1:T(2,128)} %param.11) | copy-start | bytes 3076
  166.0 25.3 %all-to-all-start.3 = ((bf16[16,24,1920]{2,1,0:T(8,128)(2,1)}), bf16[16,24,1920]{2,1,0:T(8,128)(2,1)S(1)}, u32[]{:S(2)}, u32[]{:S(2)}) async-start(bf16[16,24,1920]{2,1,0:T(8,128)(2,1)} %bitcast.15), calls=%async_computation.3 | async-start | bytes 2949120 | tf_op jit(solution)/shard_map/all_to_all | solution.py:60
  169.9 4.3 %collective-permute-start.4 = (s32[128,2]{1,0:T(8,128)S(1)}, s32[128,2]{1,0:T(8,128)S(1)}, u32[]{:S(2)}, u32[]{:S(2)}) collective-permute-start(s32[128,2]{1,0:T(8,128)S(1)} %copy.14.ids), channel_id=1, source_target_pairs={{0,16},{1,17},{2,18},{3,19},{4,20},{5,21},{6,22},{7,23},{8,24},{9,... | collective-permute-start | bytes 3080 | tf_op jit(solution)/shard_map/ppermute | solution.py:389
  178.0 1.0 copy-start.2
  179.0 26.3 %copy-start.3 = (f32[128,1920]{1,0:T(8,128)S(1)}, f32[128,1920]{1,0:T(8,128)}, u32[]{:S(2)}) copy-start(f32[128,1920]{1,0:T(8,128)} %copy-done.2) | copy-start | bytes 2949124
  179.0 19.1 %collective-permute-start.3 = (bf16[128,1920]{1,0:T(8,128)(2,1)}, bf16[128,1920]{1,0:T(8,128)(2,1)}, u32[]{:S(2)}, u32[]{:S(2)}) collective-permute-start(bf16[128,1920]{1,0:T(8,128)(2,1)} %get-tuple-element.26), channel_id=1, source_target_pairs={{0,64},{1,65},{2,66},{3,67},{4,68},{5,69},{6,70},{7,71},{8,72},{9,... | collective-permute-start | bytes 1474568 | tf_op jit(solution)/shard_map/ppermute | solution.py:50
  194.1 11.1 %collective-permute-start.7 = (bf16[128,1920]{1,0:T(8,128)(2,1)}, bf16[128,1920]{1,0:T(8,128)(2,1)S(1)}, u32[]{:S(2)}, u32[]{:S(2)}) collective-permute-start(bf16[128,1920]{1,0:T(8,128)(2,1)} %get-tuple-element.31), channel_id=1, source_target_pairs={{0,16},{1,17},{2,18},{3,19},{4,20},{5,21},{6,22},{7,23},{8,24},{9,... | collective-permute-start | bytes 1474568 | tf_op jit(solution)/shard_map/ppermute | solution.py:50
  195.6 9.6 %collective-permute-start.8 = (bf16[128,1920]{1,0:T(8,128)(2,1)S(1)}, bf16[128,1920]{1,0:T(8,128)(2,1)S(1)}, u32[]{:S(2)}, u32[]{:S(2)}) collective-permute-start(bf16[128,1920]{1,0:T(8,128)(2,1)S(1)} %get-tuple-element.32), channel_id=1, source_target_pairs={{0,80},{1,81},{2,82},{3,83},{4,84},{5,85},{6,86},{7,87},{8,88},{9,... | collective-permute-start | bytes 1474568 | tf_op jit(solution)/shard_map/ppermute | solution.py:50

commit v2 on v1

--- a/solution.py
+++ b/solution.py
@@ -10,17 +10,22 @@
 EPSILON = 1e-06
 BF16 = jnp.bfloat16
 F32 = jnp.float32
-VMEM_LIMIT = 48 * 1024 * 1024
-FILL = 512
+MIB = 1024 * 1024
+FILL = 1792
 DEPTH = 1792
+AHEAD = 1
 BACK = 896
 LANES = 128
 LAST = (((1,), (1,)), ((), ()))
 CORE_SWAP = [(0, 1), (1, 0), (2, 3), (3, 2)]
 
 
-def params():
-    return pltpu.CompilerParams(vmem_limit_bytes=VMEM_LIMIT)
+def params(mebibytes):
+    return pltpu.CompilerParams(vmem_limit_bytes=mebibytes * MIB)
+
+
+def in_hbm(array):
+    return pltpu.with_memory_space_constraint(array, pltpu.HBM)
 
 
 def whole(shape):
@@ -124,7 +129,7 @@
             (message_spec, whole((count, 1))) if first else message_spec,
             [pltpu.VMEM((height, 3 * count), BF16)],
         ),
-        compiler_params=params(),
+        compiler_params=params(24),
         name="message",
     )(place, tokens, cotangent, gain, ids, weights, tokens if first else inverse)
     return out
@@ -163,7 +168,7 @@
         functools.partial(gather_kernel, capacity),
         out_shape=jax.ShapeDtypeStruct((2 * count, rows), BF16),
         grid_spec=grid_of((1,), [whole(ids.shape)], whole((2 * count, rows))),
-        compiler_params=params(),
+        compiler_params=params(8),
         name="gather_matrix",
     )(place, ids)
 
@@ -176,12 +181,17 @@
     return lax.broadcasted_iota(jnp.int32, shape, 1) < 4
 
 
-def compact(x):
+def split_rows(x):
     rows, columns = x.shape
+    x = x.astype(F32)
     a, b = tiles(x, 6), tiles(pltpu.roll(x, 4, 0), 6)
-    shape = (rows // 48, 8, columns)
-    parts = [a[:, 0], jnp.where(upper(shape), a[:, 1], b[:, 3]), b[:, 4]]
-    return jnp.concatenate([p[:, None] for p in parts], axis=1).reshape(rows // 2, columns)
+    top = upper((rows // 48, 8, columns))
+    first = [a[:, 0], jnp.where(top, a[:, 1], b[:, 3]), b[:, 4]]
+    second = [b[:, 2], jnp.where(top, b[:, 3], a[:, 4]), a[:, 5]]
+    return [
+        jnp.concatenate([p[:, None] for p in parts], axis=1).reshape(rows // 2, columns).astype(BF16)
+        for parts in (first, second)
+    ]
 
 
 def interleave(x, y):
@@ -200,139 +210,174 @@
     return jnp.concatenate([p[:, None] for p in parts], axis=1).reshape(2 * rows, columns)
 
 
-def project_kernel(capacity, blocks, first, last, place, *refs):
-    own, other, gate, up, down = refs[:5]
-    rest = list(refs[5:])
-    previous = [] if first else [rest.pop(0) for _ in range(3)]
-    outs = [rest.pop(0) for _ in range(3)]
-    accs = rest if last else outs
-    step = pl.program_id(0)
-
-    @pl.when(step == 0)
-    def _():
-        for number, acc in enumerate(accs):
-            acc[...] = jnp.zeros_like(acc) if first else previous[number][...]
-
-    def add(rows):
-        x = rows[...]
-        accs[0][...] += jnp.dot(x, gate[...], preferred_element_type=F32)
-        accs[1][...] += jnp.dot(x, up[...], preferred_element_type=F32)
-        accs[2][...] += lax.dot_general(x, down[...], LAST, preferred_element_type=F32)
-
-    @pl.when(step < blocks)
-    def _():
-        add(own)
-
-    @pl.when(step >= blocks)
-    def _():
-        add(other)
-
-    if last:
-
-        @pl.when(step == 2 * blocks - 1)
-        def _():
-            rows = accs[2].shape[0]
-            pre_gate = compact(accs[0][...])
-            pre_up = compact(accs[1][...])
-            hidden = compact(pltpu.roll(accs[2][...], rows - capacity, 0))
-            sigma = jax.nn.sigmoid(pre_gate)
-            grad_gate = hidden * pre_up * sigma * (1.0 + pre_gate * (1.0 - sigma))
-            grad_up = hidden * pre_gate * sigma
-            outs[0][...] = grad_gate.astype(BF16)
-            outs[1][...] = grad_up.astype(BF16)
-            product = jnp.sum(grad_gate * pre_gate + grad_up * pre_up, axis=1, keepdims=True)
-            outs[2][...] = jnp.broadcast_to(product, outs[2].shape)
-
-
-def project(place, own, other, weights, at, previous, last, capacity):
+def start_all(copies):
+    for copy in copies:
+        copy.start()
+
+
+def wait_all(copies):
+    for copy in copies:
+        copy.wait()
+
+
+def chunk_copies(side, half, rows, gate, up, down, rows_in, gate_in, up_in, down_in, gate_at, sems):
+    copies = []
+    for i in range(half // DEPTH):
+        local = pl.ds(i * DEPTH, DEPTH)
+        at = pl.ds(pl.multiple_of(side * half + i * DEPTH, DEPTH), DEPTH)
+        to = pl.ds(pl.multiple_of(gate_at + i * DEPTH, DEPTH), DEPTH)
+        copies.append(
+            [
+                pltpu.make_async_copy(rows.at[:, local], rows_in.at[:, local], sems.at[i, 0]),
+                pltpu.make_async_copy(gate.at[at, :], gate_in.at[to, :], sems.at[i, 1]),
+                pltpu.make_async_copy(up.at[at, :], up_in.at[to, :], sems.at[i, 2]),
+                pltpu.make_async_copy(down.at[:, at], down_in.at[:, local], sems.at[i, 3]),
+            ]
+        )
+    return copies
+
+
+def project_half(copies, rows_in, gate_in, up_in, down_in, gate_at, accs, first, ahead):
+    for i, copy in enumerate(copies):
+        if i + AHEAD < len(copies):
+            start_all(copies[i + AHEAD])
+        elif ahead:
+            start_all(ahead.pop(0))
+        wait_all(copy)
+        local = pl.ds(i * DEPTH, DEPTH)
+        to = pl.ds(pl.multiple_of(gate_at + i * DEPTH, DEPTH), DEPTH)
+        normed, routed = split_rows(rows_in[:, local])
+        adds = (
+            jnp.dot(normed, gate_in[to, :], preferred_element_type=F32),
+            jnp.dot(normed, up_in[to, :], preferred_element_type=F32),
+            lax.dot_general(routed, down_in[:, local], LAST, preferred_element_type=F32),
+        )
+        for acc, add in zip(accs, adds):
+            acc[...] = add if first and i == 0 else acc[...] + add
+
+
+def project_kernel(place, rows, gate, up, down, acc_gate, acc_up, acc_hidden, rows_in, gate_in, up_in, down_in, sems):
+    half = rows.shape[1]
+    copies = chunk_copies(place[0], half, rows, gate, up, down, rows_in, gate_in, up_in, down_in, 0, sems)
+    for i in range(AHEAD):
+        start_all(copies[i])
+    project_half(copies, rows_in, gate_in, up_in, down_in, 0, (acc_gate, acc_up, acc_hidden), True, [])
+
+
+def project(place, rows, weights):
     gate, up, down = weights
-    rows, columns = own.shape
+    height, half = rows.shape
+    hidden = gate.shape[1]
+    any_space = pl.BlockSpec(memory_space=pl.ANY)
+    acc = jax.ShapeDtypeStruct((height // 2, hidden), F32)
+    return pl.pallas_call(
+        project_kernel,
+        out_shape=(acc,) * 3,
+        grid_spec=grid_of(
+            (1,),
+            [any_space] * 4,
+            (whole(acc.shape),) * 3,
+            [
+                pltpu.VMEM((height, half), BF16),
+                pltpu.VMEM((half, hidden), BF16),
+                pltpu.VMEM((half, hidden), BF16),
+                pltpu.VMEM((hidden, half), BF16),
+                pltpu.SemaphoreType.DMA((half // DEPTH, 4)),
+            ],
+        ),
+        compiler_params=params(20),
+        name="project",
+    )(place, rows, gate, up, down)
+
+
+def expert_kernel(place, rows, gate, up, down, in_gate, in_up, in_hidden, theirs, mine, rows_in, gate_in, up_in, down_in, acc_gate, acc_up, acc_hidden, out, sems, more_sems, out_sems):
+    half = rows.shape[1]
+    core = place[0]
+    side = 1 - core
+    copies = chunk_copies(
+        side, half, rows, gate, up, down, rows_in, gate_in, up_in, down_in, side * half, sems
+    )
+    rest = []
+    for i in range(half // DEPTH):
+        at = pl.ds(pl.multiple_of(core * half + i * DEPTH, DEPTH), DEPTH)
+        rest.append(
+            [
+                pltpu.make_async_copy(gate.at[at, :], gate_in.at[at, :], more_sems.at[i, 0]),
+                pltpu.make_async_copy(up.at[at, :], up_in.at[at, :], more_sems.at[i, 1]),
+            ]
+        )
+    for i in range(AHEAD):
+        start_all(copies[i])
+    accs = (acc_gate, acc_up, acc_hidden)
+    for acc, value in zip(accs, (in_gate, in_up, in_hidden)):
+        acc[...] = value[...]
+    ahead = list(rest)
+    project_half(copies, rows_in, gate_in, up_in, down_in, side * half, accs, False, ahead)
+    for copy in ahead:
+        start_all(copy)
+
+    pre_gate, pre_up, hidden = acc_gate[...], acc_up[...], acc_hidden[...]
+    sigma = jax.nn.sigmoid(pre_gate)
+    grad_gate = hidden * pre_up * sigma * (1.0 + pre_gate * (1.0 - sigma))
+    grad_up = hidden * pre_gate * sigma
+    product = jnp.sum(grad_gate * pre_gate + grad_up * pre_up, axis=1, keepdims=True)
+    product = jnp.broadcast_to(product, (product.shape[0], LANES))
+    product = interleave(product, product).astype(BF16)
+    grad_gate, grad_up = grad_gate.astype(BF16), grad_up.astype(BF16)
+    for copy in rest:
+        wait_all(copy)
+
+    columns = out.shape[2] - LANES
+
+    def one(start):
+        at = pl.ds(pl.multiple_of(start, LANES), BACK)
+        total = lax.dot_general(grad_gate, gate_in[at, :], LAST, preferred_element_type=F32)
+        return total + lax.dot_general(grad_up, up_in[at, :], LAST, preferred_element_type=F32)
+
+    sent = []
+    for slot, (to, whose) in enumerate(((theirs, side), (mine, core))):
+        for at in range(0, columns, BACK):
+            low, high = one(whose * columns + at), one((2 + whose) * columns + at)
+            out[slot, :, at : at + BACK] = interleave(low, high).astype(BF16)
+        out[slot, :, columns:] = product
+        copy = pltpu.make_async_copy(out.at[slot], to, out_sems.at[slot])
+        copy.start()
+        sent.append(copy)
+    wait_all(sent)
+
+
+def expert(place, rows, weights, accs):
+    gate, up, down = weights
+    height, half = rows.shape
     width, hidden = gate.shape
-    blocks = columns // DEPTH if columns % DEPTH == 0 else columns // 256
-    depth = columns // blocks
-    per_half = width // 2 // depth
-    start = at // depth
-
-    def at_block(i, place):
-        side = jnp.where(i < blocks, place[0], 1 - place[0])
-        return side * per_half + start + lax.rem(i, blocks)
-
-    acc = jax.ShapeDtypeStruct((rows, hidden), F32)
-    grad = jax.ShapeDtypeStruct((rows // 2, hidden), BF16)
-    product = jax.ShapeDtypeStruct((rows // 2, LANES), F32)
-    outs = (grad, grad, product) if last else (acc,) * 3
+    columns = width // 4
+    any_space = pl.BlockSpec(memory_space=pl.ANY)
+    message = jax.ShapeDtypeStruct((height, columns + LANES), BF16)
+    acc = accs[0].shape
     return pl.pallas_call(
-        functools.partial(project_kernel, capacity, blocks, not previous, last),
-        out_shape=outs,
+        expert_kernel,
+        out_shape=(message, message),
         grid_spec=grid_of(
-            (2 * blocks,),
+            (1,),
+            [any_space] * 4 + [whole(acc)] * 3,
+            (any_space, any_space),
             [
-                pl.BlockSpec((rows, depth), lambda i, place: (0, jnp.minimum(i, blocks - 1))),
-                pl.BlockSpec((rows, depth), lambda i, place: (0, jnp.maximum(i - blocks, 0))),
-                pl.BlockSpec((depth, hidden), lambda i, place: (at_block(i, place), 0)),
-                pl.BlockSpec((depth, hidden), lambda i, place: (at_block(i, place), 0)),
-                pl.BlockSpec((hidden, depth), lambda i, place: (0, at_block(i, place))),
-            ]
-            + [whole((rows, hidden))] * len(previous),
-            tuple(whole(o.shape) for o in outs),
-            [pltpu.VMEM((rows, hidden), F32)] * 3 if last else [],
+                pltpu.VMEM((height, half), BF16),
+                pltpu.VMEM((width, hidden), BF16),
+                pltpu.VMEM((width, hidden), BF16),
+                pltpu.VMEM((hidden, half), BF16),
+                pltpu.VMEM(acc, F32),
+                pltpu.VMEM(acc, F32),
+                pltpu.VMEM(acc, F32),
+                pltpu.VMEM((2,) + message.shape, BF16),
+                pltpu.SemaphoreType.DMA((half // DEPTH, 4)),
+                pltpu.SemaphoreType.DMA((half // DEPTH, 2)),
+                pltpu.SemaphoreType.DMA((2,)),
+            ],
         ),
-        compiler_params=params(),
-        name="project",
-    )(place, own, other, gate, up, down, *previous)
-
-
-def back_kernel(place, *refs):
-    grad_gate, grad_up, product, gate_0, gate_1, up_0, up_1 = refs[:7]
-    out = refs[-1]
-    other = refs[7] if len(refs) == 9 else None
-    columns = out.shape[1] - LANES
-
-    def one(gate, up):
-        total = lax.dot_general(grad_gate[...], gate[...], LAST, preferred_element_type=F32)
-        return total + lax.dot_general(grad_up[...], up[...], LAST, preferred_element_type=F32)
-
-    def put(rows, at):
-        if other is not None:
-            rows = rows + other[:, at].astype(F32)
-        out[:, at] = rows.astype(BF16)
-
-    step = pl.program_id(0)
-    put(interleave(one(gate_0, up_0), one(gate_1, up_1)), pl.ds(pl.multiple_of(step * BACK, LANES), BACK))
-
-    @pl.when(step == 0)
-    def _():
-        put(interleave(product[...], product[...]), pl.ds(columns, LANES))
-
-
-def back(place, grads, weights, other):
-    gate, up, _ = weights
-    rows, hidden = grads[0].shape
-    columns = gate.shape[0] // 4
-    steps = columns // BACK
-
-    def quarter(high):
-        def index(i, place):
-            side = 1 - place[0] if other is None else place[0]
-            return ((2 * high + side) * steps + i, 0)
-
-        return pl.BlockSpec((BACK, hidden), index)
-
-    shape = (2 * rows, columns + LANES)
-    extra = [] if other is None else [other]
-    return pl.pallas_call(
-        back_kernel,
-        out_shape=jax.ShapeDtypeStruct(shape, BF16),
-        grid_spec=grid_of(
-            (steps,),
-            [whole(g.shape) for g in grads]
-            + [quarter(0), quarter(1), quarter(0), quarter(1)]
-            + [whole(shape)] * len(extra),
-            whole(shape),
-        ),
-        compiler_params=params(),
-        name="back",
-    )(place, *grads, gate, gate, up, up, *extra)
+        compiler_params=params(32),
+        name="expert",
+    )(place, rows, gate, up, down, *accs)
 
 
 def combine_kernel(place, gather, rows, first, second):
@@ -360,7 +405,7 @@
             [whole(gather.shape), pl.BlockSpec((rows.shape[0], part), lambda i, place: (0, i))],
             (block, block),
         ),
-        compiler_params=params(),
+        compiler_params=params(12),
         name="combine",
     )(place, gather, rows)
 
@@ -378,11 +423,11 @@
     after = lax.rem(2 * high + low + 1, 4) // 2
     place = jnp.stack([core, low, high]).astype(jnp.int32)
     place_after = jnp.stack([core, low, after]).astype(jnp.int32)
-    weights = (w_gate[0], w_up[0], w_down[0])
+    weights = tuple(in_hbm(array[0]) for array in (w_gate, w_up, w_down))
 
     gain = norm_gain.reshape(1, width)
     make = functools.partial(
-        make_message, place, tokens, cotangent, gain, expert_ids.T, gate_weights, capacity=capacity, plane=plane
+        make_message, place, in_hbm(tokens), in_hbm(cotangent), gain, expert_ids.T, gate_weights, capacity=capacity, plane=plane
     )
     other, inverse = make(inverse=None, other=True)
     own = make(inverse=inverse, other=False)
@@ -391,18 +436,22 @@
 
     other = ring_permute(other, (1, 3))
     own = plane_exchange(own)
+    own, *gathers = lax.optimization_barrier((own, *gathers))
     other = plane_exchange(other)
 
-    grads = project(place, own, core_swap(own), weights, 0, (), True, capacity)
-    theirs = core_swap(back(place, grads, weights, None))
-    mine = back(place, grads, weights, theirs)
-
-    mine, other = lax.optimization_barrier((mine, other))
-    own_back = plane_exchange(mine)
-    grads = project(place, other, core_swap(other), weights, 0, (), True, capacity)
-    theirs = core_swap(back(place, grads, weights, None))
-    mine = back(place, grads, weights, theirs)
-    other_back = plane_exchange(mine)
+    def compute(rows, first):
+        accs = project(place, rows, weights)
+        swapped = core_swap(rows)
+        accs, swapped, *first = lax.optimization_barrier((accs, swapped, *first))
+        theirs, mine = expert(place, swapped, weights, accs)
+        summed = mine.astype(F32) + core_swap(theirs).astype(F32)
+        return summed.astype(BF16), first
+
+    own_back, _ = compute(own, ())
+    own_back, other = lax.optimization_barrier((own_back, other))
+    own_back = plane_exchange(own_back)
+    other_back, (own_back,) = compute(other, (own_back,))
+    other_back = plane_exchange(other_back)
 
     kept, sent = combine(place, gathers[0], own_back, F32)
     from_far = ring_permute(sent, (2, 2))

time: 209 us -> 211 us (level)
  Pallas kernels: 72.5 us -> 62 us
  waiting for transfers between devices: 89.1 us -> 96 us
  other arithmetic: 3.74 us -> 6.91 us
    ppermute x1, waiting for transfers between devices: 1.69 us -> 29.3 us  [body(): lax.ppermute(expert_ids, 'expert', [(k, (k + plane) % experts) for k in r...]
    all_to_all x4, waiting for transfers between devices: 71.7 us -> 48.3 us  [plane_exchange(): lax.all_to_all(shaped, 'expert', split_axis=0, concat_axis=0, tiled=True,...]
    pallas_call x6 -> x4, Pallas kernels: 52.8 us -> 41.8 us  [the longest x2 28.3 us: expert(): pl.pallas_call(expert_kernel, out_shape=(message, message), grid_spec=gri...]
    ppermute x4, waiting for transfers between devices: 7.12 us -> 12.1 us  [ring_permute(): return lax.ppermute(array, ('pipe', 'expert'), moves)]
    convert_element_type x0 -> x2, other arithmetic: none -> 3 us  [compute(): return (summed.astype(BF16), first)]
    ppermute x4, waiting for transfers between devices: 8.59 us -> 6.31 us  [core_swap(): return lax.ppermute(array, 'pipe', CORE_SWAP)]
    unnamed x18 -> x24, local copies, waits for them, and re-layouts: 6.3 us -> 8.15 us
  transfers between devices with their start and end apart: 13 -> 13, of which waited for: 9 -> 9; matrix products, arithmetic and copies ran while one was open for 0% -> 1% of each run, Pallas kernels for 19% -> 17%
where the time goes in v2:
time: 211 us; the launch traced here: 210 us
  waiting for transfers between devices  96 us (45%)
  Pallas kernels  62 us (29%)
  starting transfers between devices  35.8 us (17%)
  local copies, waits for them, and re-layouts  8.93 us (4%)
  other arithmetic  6.91 us (3%)
    all_to_all x4, waiting for transfers between devices, plane_exchange(): lax.all_to_all(shaped, 'expert', split_axis=0, concat_axis=0, tiled=True,...  48.3 us
    ppermute x1, waiting for transfers between devices, body(): lax.ppermute(expert_ids, 'expert', [(k, (k + plane) % experts) for k in r...  29.3 us
    pallas_call x2, Pallas kernels, expert(): pl.pallas_call(expert_kernel, out_shape=(message, message), grid_spec=gri...  28.3 us
    all_to_all x4, starting transfers between devices, plane_exchange(): lax.all_to_all(shaped, 'expert', split_axis=0, concat_axis=0, tiled=True,...  26.5 us
    pallas_call x2, Pallas kernels, project(): pl.pallas_call(project_kernel, out_shape=(acc,) * 3, grid_spec=grid_of((1...  13.5 us
    ppermute x4, waiting for transfers between devices, ring_permute(): return lax.ppermute(array, ('pipe', 'expert'), moves)  12.1 us
    pallas_call x2, Pallas kernels, make_message(): pl.pallas_call(functools.partial(message_kernel, capacity, other, first),...  11.3 us
    unnamed x24, local copies, waits for them, and re-layouts  8.15 us
  transfers between devices with their start and end apart: 13, of which 9 were waited for; matrix products, arithmetic and copies ran while one was open for 1% of the time, Pallas kernels for 17%

profile of v2, /device:TPU:0, one launch (start us, length us, event | category | flops | bytes accessed | tf_op | source)
XLA Modules:
  0.0 209.9 jit_solution(4667899288948932942)
XLA Ops:
  2.3 6.1 %message.2 = (bf16[384,3584]{1,0:T(8,128)(2,1)}, f32[128,1]{1,0:T(8,128)S(1)}) custom-call(s32[3]{0:T(128)S(1)} %pad_add_fusion.place, bf16[128,7168]{1,0:T(8,128)(2,1)} %refs_0_.3, bf16[128,7168]{1,0:T(8,128)(2,1)} %refs_1_.3, f32[1,7168]{1,0:T(1,128)S(1)} %bitcast.20, s32[2,128]{1,0:T(2,128)S(1)} %bitcast.22, f32[128,2]{1,0:T(8,128)S(1)} %copy.13.refs_4_, ...), custom_call_target="tpu_custom_call" | custom-call | tf_op jit(solution)/shard_map/message/pallas_call | solution.py:123
  8.5 5.2 %message.3 = bf16[384,3584]{1,0:T(8,128)(2,1)} custom-call(s32[3]{0:T(128)S(1)} %pad_add_fusion.place, bf16[128,7168]{1,0:T(8,128)(2,1)} %refs_0_.3, bf16[128,7168]{1,0:T(8,128)(2,1)} %refs_1_.3, f32[1,7168]{1,0:T(1,128)S(1)} %bitcast.21, s32[2,128]{1,0:T(2,128)S(1)} %bitcast.23, f32[128,2]{1,0:T(8,128)S(1)} %copy.13.refs_4_, ...), custom_call_target="tpu_custom_call" | custom-call | tf_op jit(solution)/shard_map/message/pallas_call | solution.py:123
  13.7 8.3 %all-to-all-start = ((bf16[16,24,3584]{2,1,0:T(8,128)(2,1)}), bf16[16,24,3584]{2,1,0:T(8,128)(2,1)}, u32[]{:S(2)}, u32[]{:S(2)}) async-start(bf16[16,24,3584]{2,1,0:T(8,128)(2,1)} %bitcast.5), calls=%async_computation | async-start | bytes 5505024 | tf_op jit(solution)/shard_map/all_to_all | solution.py:65
  26.2 29.3 %collective-permute-done.ids = s32[128,2]{1,0:T(8,128)S(1)} collective-permute-done((s32[128,2]{1,0:T(8,128)S(1)}, s32[128,2]{1,0:T(8,128)S(1)}, u32[]{:S(2)}, u32[]{:S(2)}) %collective-permute-start) | collective-permute-done | bytes 1056 | tf_op jit(solution)/shard_map/ppermute | solution.py:434
  56.6 4.0 %all-to-all-done = bf16[16,24,3584]{2,1,0:T(8,128)(2,1)} async-done(((bf16[16,24,3584]{2,1,0:T(8,128)(2,1)}), bf16[16,24,3584]{2,1,0:T(8,128)(2,1)}, u32[]{:S(2)}, u32[]{:S(2)}) %all-to-all-start) | async-done | bytes 2752544 | tf_op jit(solution)/shard_map/all_to_all | solution.py:65
  62.1 5.1 %all-to-all-start.1 = ((bf16[16,24,3584]{2,1,0:T(8,128)(2,1)}), bf16[16,24,3584]{2,1,0:T(8,128)(2,1)S(1)}, u32[]{:S(2)}, u32[]{:S(2)}) async-start(bf16[16,24,3584]{2,1,0:T(8,128)(2,1)} %bitcast.37), calls=%async_computation.1 | async-start | bytes 5505024 | tf_op jit(solution)/shard_map/all_to_all | solution.py:65
  67.2 7.1 %project.2 = (f32[192,512]{1,0:T(8,128)S(1)}, f32[192,512]{1,0:T(8,128)S(1)}, f32[192,512]{1,0:T(8,128)S(1)}) custom-call(s32[3]{0:T(128)S(1)} %pad_add_fusion.place, bf16[384,3584]{1,0:T(8,128)(2,1)} %bitcast.6.rows, bf16[7168,512]{1,0:T(8,128)(2,1)} %bitcast.24, bf16[7168,512]{1,0:T(8,128)(2,1)} %bitcast.28, bf16[512,7168]{1,0:T(8,128)(2,1)} %bitcast.32), custom_call_target="tpu_custom_call" | custom-call | tf_op jit(solution)/shard_map/project/pallas_call | solution.py:273
  74.3 14.2 %expert.2 = (bf16[384,1920]{1,0:T(8,128)(2,1)S(1)}, bf16[384,1920]{1,0:T(8,128)(2,1)S(1)}) custom-call(s32[3]{0:T(128)S(1)} %pad_add_fusion.place, bf16[384,3584]{1,0:T(8,128)(2,1)} %collective-permute-done.1.rows, bf16[7168,512]{1,0:T(8,128)(2,1)} %bitcast.25, bf16[7168,512]{1,0:T(8,128)(2,1)} %bitcast.29, bf16[512,7168]{1,0:T(8,128)(2,1)} %bitcast.33, ...), custom_call_target="tpu_custom_call" | custom-call | tf_op jit(solution)/shard_map/expert/pallas_call | solution.py:357
  88.8 3.0 %collective-permute-done.2 = bf16[384,1920]{1,0:T(8,128)(2,1)S(1)} collective-permute-done((bf16[384,1920]{1,0:T(8,128)(2,1)S(1)}, bf16[384,1920]{1,0:T(8,128)(2,1)S(1)}, u32[]{:S(2)}, u32[]{:S(2)}) %collective-permute-start.2) | collective-permute-done | bytes 1474592 | tf_op jit(solution)/shard_map/ppermute | solution.py:59
  93.3 12.1 %all-to-all-done.1 = bf16[16,24,3584]{2,1,0:T(8,128)(2,1)S(1)} async-done(((bf16[16,24,3584]{2,1,0:T(8,128)(2,1)}), bf16[16,24,3584]{2,1,0:T(8,128)(2,1)S(1)}, u32[]{:S(2)}, u32[]{:S(2)}) %all-to-all-start.1) | async-done | bytes 2752544 | tf_op jit(solution)/shard_map/all_to_all | solution.py:65
  105.4 9.4 %all-to-all-start.2 = ((bf16[16,24,1920]{2,1,0:T(8,128)(2,1)}), bf16[16,24,1920]{2,1,0:T(8,128)(2,1)}, u32[]{:S(2)}, u32[]{:S(2)}) async-start(bf16[16,24,1920]{2,1,0:T(8,128)(2,1)} %bitcast.36), calls=%async_computation.2 | async-start | bytes 2949120 | tf_op jit(solution)/shard_map/all_to_all | solution.py:65
  114.8 6.4 %project.3 = (f32[192,512]{1,0:T(8,128)S(1)}, f32[192,512]{1,0:T(8,128)S(1)}, f32[192,512]{1,0:T(8,128)S(1)}) custom-call(s32[3]{0:T(128)S(1)} %pad_add_fusion.place, bf16[384,3584]{1,0:T(8,128)(2,1)S(1)} %bitcast.18, bf16[7168,512]{1,0:T(8,128)(2,1)} %bitcast.26, bf16[7168,512]{1,0:T(8,128)(2,1)} %bitcast.30, bf16[512,7168]{1,0:T(8,128)(2,1)} %bitcast.34), custom_call_target="tpu_custom_call" | custom-call | tf_op jit(solution)/shard_map/project/pallas_call | solution.py:273
  122.7 16.0 %all-to-all-done.2 = bf16[16,24,1920]{2,1,0:T(8,128)(2,1)} async-done(((bf16[16,24,1920]{2,1,0:T(8,128)(2,1)}), bf16[16,24,1920]{2,1,0:T(8,128)(2,1)}, u32[]{:S(2)}, u32[]{:S(2)}) %all-to-all-start.2) | async-done | bytes 1474592 | tf_op jit(solution)/shard_map/all_to_all | solution.py:65
  140.7 14.1 %expert.3 = (bf16[384,1920]{1,0:T(8,128)(2,1)S(1)}, bf16[384,1920]{1,0:T(8,128)(2,1)S(1)}) custom-call(s32[3]{0:T(128)S(1)} %pad_add_fusion.place, bf16[384,3584]{1,0:T(8,128)(2,1)} %collective-permute-done.4.rows, bf16[7168,512]{1,0:T(8,128)(2,1)} %bitcast.27, bf16[7168,512]{1,0:T(8,128)(2,1)} %bitcast.31, bf16[512,7168]{1,0:T(8,128)(2,1)} %bitcast.35, ...), custom_call_target="tpu_custom_call" | custom-call | tf_op jit(solution)/shard_map/expert/pallas_call | solution.py:357
  155.0 3.3 %collective-permute-done.6 = bf16[384,1920]{1,0:T(8,128)(2,1)S(1)} collective-permute-done((bf16[384,1920]{1,0:T(8,128)(2,1)S(1)}, bf16[384,1920]{1,0:T(8,128)(2,1)S(1)}, u32[]{:S(2)}, u32[]{:S(2)}) %collective-permute-start.6) | collective-permute-done | bytes 1474592 | tf_op jit(solution)/shard_map/ppermute | solution.py:59
  159.7 3.7 %all-to-all-start.3 = ((bf16[16,24,1920]{2,1,0:T(8,128)(2,1)}), bf16[16,24,1920]{2,1,0:T(8,128)(2,1)S(1)}, u32[]{:S(2)}, u32[]{:S(2)}) async-start(bf16[16,24,1920]{2,1,0:T(8,128)(2,1)} %bitcast.15), calls=%async_computation.3 | async-start | bytes 2949120 | tf_op jit(solution)/shard_map/all_to_all | solution.py:65
  163.6 4.1 %combine.2 = (f32[128,1920]{1,0:T(8,128)S(1)}, bf16[128,1920]{1,0:T(8,128)(2,1)}) custom-call(s32[3]{0:T(128)S(1)} %pad_add_fusion.place, bf16[256,384]{1,0:T(8,128)(2,1)S(1)} %gather_matrix.2.gather, bf16[384,1920]{1,0:T(8,128)(2,1)} %bitcast.13.rows), custom_call_target="tpu_custom_call" | custom-call | tf_op jit(solution)/shard_map/combine/pallas_call | solution.py:397
  167.7 3.0 %collective-permute-start.5 = (bf16[128,1920]{1,0:T(8,128)(2,1)}, bf16[128,1920]{1,0:T(8,128)(2,1)}, u32[]{:S(2)}, u32[]{:S(2)}) collective-permute-start(bf16[128,1920]{1,0:T(8,128)(2,1)} %get-tuple-element.55), channel_id=1, source_target_pairs={{0,64},{1,65},{2,66},{3,67},{4,68},{5,69},{6,70},{7,71},{8,72},{9,... | collective-permute-start | bytes 1474568 | tf_op jit(solution)/shard_map/ppermute | solution.py:55
  170.7 16.2 %all-to-all-done.3 = bf16[16,24,1920]{2,1,0:T(8,128)(2,1)S(1)} async-done(((bf16[16,24,1920]{2,1,0:T(8,128)(2,1)}), bf16[16,24,1920]{2,1,0:T(8,128)(2,1)S(1)}, u32[]{:S(2)}, u32[]{:S(2)}) %all-to-all-start.3) | async-done | bytes 1474592 | tf_op jit(solution)/shard_map/all_to_all | solution.py:65
  186.9 2.7 %combine.3 = (bf16[128,1920]{1,0:T(8,128)(2,1)S(1)}, bf16[128,1920]{1,0:T(8,128)(2,1)}) custom-call(s32[3]{0:T(128)S(1)} %pad_add_fusion.2.place, bf16[256,384]{1,0:T(8,128)(2,1)S(1)} %gather_matrix.3.gather, bf16[384,1920]{1,0:T(8,128)(2,1)S(1)} %bitcast.19), custom_call_target="tpu_custom_call" | custom-call | tf_op jit(solution)/shard_map/combine/pallas_call | solution.py:397
  189.7 2.8 %collective-permute-start.8 = (bf16[128,1920]{1,0:T(8,128)(2,1)}, bf16[128,1920]{1,0:T(8,128)(2,1)S(1)}, u32[]{:S(2)}, u32[]{:S(2)}) collective-permute-start(bf16[128,1920]{1,0:T(8,128)(2,1)} %get-tuple-element.64), channel_id=1, source_target_pairs={{0,80},{1,81},{2,82},{3,83},{4,84},{5,85},{6,86},{7,87},{8,88},{9,... | collective-permute-start | bytes 1474568 | tf_op jit(solution)/shard_map/ppermute | solution.py:55
  193.2 9.0 %collective-permute-done.8 = bf16[128,1920]{1,0:T(8,128)(2,1)S(1)} collective-permute-done((bf16[128,1920]{1,0:T(8,128)(2,1)}, bf16[128,1920]{1,0:T(8,128)(2,1)S(1)}, u32[]{:S(2)}, u32[]{:S(2)}) %collective-permute-start.8) | collective-permute-done | bytes 491552 | tf_op jit(solution)/shard_map/ppermute | solution.py:55
  202.2 3.1 %collective-permute-done.7 = bf16[128,1920]{1,0:T(8,128)(2,1)S(1)} collective-permute-done((bf16[128,1920]{1,0:T(8,128)(2,1)S(1)}, bf16[128,1920]{1,0:T(8,128)(2,1)S(1)}, u32[]{:S(2)}, u32[]{:S(2)}) %collective-permute-start.7) | collective-permute-done | bytes 491552 | tf_op jit(solution)/shard_map/ppermute | solution.py:55
  207.6 2.2 %fusion.2 = bf16[128,1792]{1,0:T(8,128)(2,1)} fusion(f32[128,1920]{1,0:T(8,128)S(1)} %convert_add_fusion, f32[128]{0:T(128)S(1)} %get-tuple-element.66, bf16[128,7168]{1,0:T(8,128)(2,1)} %refs_0_.3, s32[]{:T(128)S(6)} %select_n.16, f32[1792]{0:T(1024)S(1)} %dynamic_slice.10, f32[128]{0:T(128)S(1)} %get-tuple-element.65, bf16[128,7168]{1,0:T(8,128)(2,1)} %refs_1_.3), kind=kLoop, calls=%fused_computation.6 | loop fusion | flops 1835008 | bytes 2301956 | tf_op jit(solution)/shard_map/convert_element_type | solution.py:473
  (44 shorter events, 19.1 us)
Async XLA Ops:
  0.9 0.8 copy-start.6
  1.6 0.7 copy-start.7
  8.5 5.2 %copy-start.4 = (f32[128,1]{1,0:T(8,128)}, f32[128,1]{1,0:T(8,128)S(1)}, u32[]{:S(2)}) copy-start(f32[128,1]{1,0:T(8,128)S(1)} %get-tuple-element.35.refs_5_) | copy-start | bytes 1540
  13.7 9.9 %copy-start.8 = (s32[128,2]{0,1:T(2,128)S(1)}, s32[128,2]{0,1:T(2,128)}, u32[]{:S(2)}) copy-start(s32[128,2]{0,1:T(2,128)} %param.11) | copy-start | bytes 3076
  13.7 46.9 %all-to-all-start = ((bf16[16,24,3584]{2,1,0:T(8,128)(2,1)}), bf16[16,24,3584]{2,1,0:T(8,128)(2,1)}, u32[]{:S(2)}, u32[]{:S(2)}) async-start(bf16[16,24,3584]{2,1,0:T(8,128)(2,1)} %bitcast.5), calls=%async_computation | async-start | bytes 5505024 | tf_op jit(solution)/shard_map/all_to_all | solution.py:65
  22.0 38.6 %collective-permute-start.3 = (bf16[384,3584]{1,0:T(8,128)(2,1)}, bf16[384,3584]{1,0:T(8,128)(2,1)S(1)}, u32[]{:S(2)}, u32[]{:S(2)}) collective-permute-start(bf16[384,3584]{1,0:T(8,128)(2,1)} %get-tuple-element.47), channel_id=1, source_target_pairs={{0,16},{1,17},{2,18},{3,19},{4,20},{5,21},{6,22},{7,23},{8,24},{9,... | collective-permute-start | bytes 8257544 | tf_op jit(solution)/shard_map/ppermute | solution.py:55
  23.7 31.9 %collective-permute-start = (s32[128,2]{1,0:T(8,128)S(1)}, s32[128,2]{1,0:T(8,128)S(1)}, u32[]{:S(2)}, u32[]{:S(2)}) collective-permute-start(s32[128,2]{1,0:T(8,128)S(1)} %copy.15.ids), channel_id=1, source_target_pairs={{0,16},{1,17},{2,18},{3,19},{4,20},{5,21},{6,22},{7,23},{8,24},{9,... | collective-permute-start | bytes 3080 | tf_op jit(solution)/shard_map/ppermute | solution.py:434
  60.6 13.7 %collective-permute-start.1 = (bf16[384,3584]{1,0:T(8,128)(2,1)}, bf16[384,3584]{1,0:T(8,128)(2,1)}, u32[]{:S(2)}, u32[]{:S(2)}) collective-permute-start(bf16[384,3584]{1,0:T(8,128)(2,1)} %bitcast.6.rows), channel_id=1, source_target_pairs={{0,32},{32,0},{64,96},{96,64},{1,33},{33,1},{65,97},{97,65},{2,34}... | collective-permute-start | bytes 8257544 | tf_op jit(solution)/shard_map/ppermute | solution.py:59
  60.6 1.5 copy-start.9
  62.1 43.3 %all-to-all-start.1 = ((bf16[16,24,3584]{2,1,0:T(8,128)(2,1)}), bf16[16,24,3584]{2,1,0:T(8,128)(2,1)S(1)}, u32[]{:S(2)}, u32[]{:S(2)}) async-start(bf16[16,24,3584]{2,1,0:T(8,128)(2,1)} %bitcast.37), calls=%async_computation.1 | async-start | bytes 5505024 | tf_op jit(solution)/shard_map/all_to_all | solution.py:65
  88.5 3.3 %collective-permute-start.2 = (bf16[384,1920]{1,0:T(8,128)(2,1)S(1)}, bf16[384,1920]{1,0:T(8,128)(2,1)S(1)}, u32[]{:S(2)}, u32[]{:S(2)}) collective-permute-start(bf16[384,1920]{1,0:T(8,128)(2,1)S(1)} %get-tuple-element.46), channel_id=1, source_target_pairs={{0,32},{32,0},{64,96},{96,64},{1,33},{33,1},{65,97},{97,65},{2,34}... | collective-permute-start | bytes 4423688 | tf_op jit(solution)/shard_map/ppermute | solution.py:59
  105.4 33.4 %collective-permute-start.4 = (bf16[384,3584]{1,0:T(8,128)(2,1)S(1)}, bf16[384,3584]{1,0:T(8,128)(2,1)}, u32[]{:S(2)}, u32[]{:S(2)}) collective-permute-start(bf16[384,3584]{1,0:T(8,128)(2,1)S(1)} %bitcast.17), channel_id=1, source_target_pairs={{0,32},{32,0},{64,96},{96,64},{1,33},{33,1},{65,97},{97,65},{2,34}... | collective-permute-start | bytes 8257544 | tf_op jit(solution)/shard_map/ppermute | solution.py:59
  105.4 33.4 %all-to-all-start.2 = ((bf16[16,24,1920]{2,1,0:T(8,128)(2,1)}), bf16[16,24,1920]{2,1,0:T(8,128)(2,1)}, u32[]{:S(2)}, u32[]{:S(2)}) async-start(bf16[16,24,1920]{2,1,0:T(8,128)(2,1)} %bitcast.36), calls=%async_computation.2 | async-start | bytes 2949120 | tf_op jit(solution)/shard_map/all_to_all | solution.py:65
  121.2 0.7 copy-start
  122.0 0.8 copy-start.2
  138.8 1.0 copy-start.1
  139.8 1.0 copy-start.3
  154.9 3.3 %collective-permute-start.6 = (bf16[384,1920]{1,0:T(8,128)(2,1)S(1)}, bf16[384,1920]{1,0:T(8,128)(2,1)S(1)}, u32[]{:S(2)}, u32[]{:S(2)}) collective-permute-start(bf16[384,1920]{1,0:T(8,128)(2,1)S(1)} %get-tuple-element.62), channel_id=1, source_target_pairs={{0,32},{32,0},{64,96},{96,64},{1,33},{33,1},{65,97},{97,65},{2,34}... | collective-permute-start | bytes 4423688 | tf_op jit(solution)/shard_map/ppermute | solution.py:59
  159.7 27.2 %all-to-all-start.3 = ((bf16[16,24,1920]{2,1,0:T(8,128)(2,1)}), bf16[16,24,1920]{2,1,0:T(8,128)(2,1)S(1)}, u32[]{:S(2)}, u32[]{:S(2)}) async-start(bf16[16,24,1920]{2,1,0:T(8,128)(2,1)} %bitcast.15), calls=%async_computation.3 | async-start | bytes 2949120 | tf_op jit(solution)/shard_map/all_to_all | solution.py:65
  167.7 25.5 %collective-permute-start.5 = (bf16[128,1920]{1,0:T(8,128)(2,1)}, bf16[128,1920]{1,0:T(8,128)(2,1)}, u32[]{:S(2)}, u32[]{:S(2)}) collective-permute-start(bf16[128,1920]{1,0:T(8,128)(2,1)} %get-tuple-element.55), channel_id=1, source_target_pairs={{0,64},{1,65},{2,66},{3,67},{4,68},{5,69},{6,70},{7,71},{8,72},{9,... | collective-permute-start | bytes 1474568 | tf_op jit(solution)/shard_map/ppermute | solution.py:55
  189.7 17.8 %copy-start.5 = (f32[128,1]{1,0:T(8,128)S(1)}, f32[128,1]{1,0:T(8,128)}, u32[]{:S(2)}) copy-start(f32[128,1]{1,0:T(8,128)} %copy-done.4) | copy-start | bytes 1540
  189.7 12.5 %collective-permute-start.8 = (bf16[128,1920]{1,0:T(8,128)(2,1)}, bf16[128,1920]{1,0:T(8,128)(2,1)S(1)}, u32[]{:S(2)}, u32[]{:S(2)}) collective-permute-start(bf16[128,1920]{1,0:T(8,128)(2,1)} %get-tuple-element.64), channel_id=1, source_target_pairs={{0,80},{1,81},{2,82},{3,83},{4,84},{5,85},{6,86},{7,87},{8,88},{9,... | collective-permute-start | bytes 1474568 | tf_op jit(solution)/shard_map/ppermute | solution.py:55
  192.4 12.9 %collective-permute-start.7 = (bf16[128,1920]{1,0:T(8,128)(2,1)S(1)}, bf16[128,1920]{1,0:T(8,128)(2,1)S(1)}, u32[]{:S(2)}, u32[]{:S(2)}) collective-permute-start(bf16[128,1920]{1,0:T(8,128)(2,1)S(1)} %get-tuple-element.63), channel_id=1, source_target_pairs={{0,16},{1,17},{2,18},{3,19},{4,20},{5,21},{6,22},{7,23},{8,24},{9,... | collective-permute-start | bytes 1474568 | tf_op jit(solution)/shard_map/ppermute | solution.py:55
  205.3 0.8 copy-start.10

commit v3 on v2

--- a/solution.py
+++ b/solution.py
@@ -18,6 +18,7 @@
 LANES = 128
 LAST = (((1,), (1,)), ((), ()))
 CORE_SWAP = [(0, 1), (1, 0), (2, 3), (3, 2)]
+HIGH_SWAP = [(0, 2), (2, 0), (1, 3), (3, 1)]
 
 
 def params(mebibytes):
@@ -38,139 +39,117 @@
     )
 
 
-def same_plane(group):
-    return [[x * group + k for k in range(group)] for x in range(lax.axis_size("expert") // group)]
-
-
-def ring_permute(array, steps):
-    plane = lax.axis_size("expert") // 2
-    moves = []
-    for x in range(4):
-        for core in range(2):
-            to = (x + steps[core]) % 4
-            for k in range(plane):
-                source = (2 * (x // 2) + core) * 2 * plane + (x % 2) * plane + k
-                target = (2 * (to // 2) + core) * 2 * plane + (to % 2) * plane + k
-                moves.append((source, target))
-    return lax.ppermute(array, ("pipe", "expert"), moves)
-
-
 def core_swap(array):
     return lax.ppermute(array, "pipe", CORE_SWAP)
 
 
-def plane_exchange(rows):
-    plane = lax.axis_size("expert") // 2
-    shaped = rows.reshape(plane, rows.shape[0] // plane, rows.shape[1])
-    out = lax.all_to_all(
-        shaped, "expert", split_axis=0, concat_axis=0, tiled=True, axis_index_groups=same_plane(plane)
-    )
-    return out.reshape(rows.shape)
-
-
-def message_kernel(capacity, other, first, place, *refs):
-    tokens, cotangent, gain, ids, weights = refs[:5]
-    if first:
-        all_tokens, rows, inverse, select = refs[5:]
-    else:
-        inverse, rows, select = refs[5:]
+def high_swap(array):
+    return lax.ppermute(array, "pipe", HIGH_SWAP)
+
+
+def exchange(rows):
+    experts = lax.axis_size("expert")
+    shaped = rows.reshape(experts, rows.shape[0] // experts, rows.shape[1])
+    return lax.all_to_all(shaped, "expert", split_axis=0, concat_axis=0, tiled=True).reshape(rows.shape)
+
+
+def message_kernel(capacity, place, all_tokens, tokens, cotangent, gain, ids, weights, rows, inverse, select, factors):
     top, count = ids.shape
 
     @pl.when(pl.program_id(0) == 0)
     def _():
         height = select.shape[0]
-        plane = height // (2 * capacity)
-        expert_of = lax.broadcasted_iota(jnp.int32, (2 * plane, count), 0)
+        experts = height // (2 * capacity)
+        expert_of = lax.broadcasted_iota(jnp.int32, (experts, count), 0)
         earlier_of = lax.broadcasted_iota(jnp.int32, (count, count), 0)
         later_of = lax.broadcasted_iota(jnp.int32, (count, count), 1)
         before = (earlier_of < later_of).astype(F32).astype(BF16)
         row = lax.broadcasted_iota(jnp.int32, (height, count), 0)
-        taken = jnp.zeros((2 * plane, 1), F32)
+        taken = jnp.zeros((experts, 1), F32)
         normed_part = jnp.zeros(row.shape, F32)
-        base = plane * (1 - place[1] if other else place[1])
         for k in range(top):
             expert = ids[k : k + 1, :]
             named = (expert_of == expert).astype(F32)
             earlier = jnp.dot(named.astype(BF16), before, preferred_element_type=F32) + taken
             rank = jnp.sum(earlier * named, axis=0, keepdims=True).astype(jnp.int32)
             taken = taken + jnp.sum(named, axis=1, keepdims=True)
-            local = expert - base
-            at = jnp.where((local >= 0) & (local < plane), local * (2 * capacity) + rank, -2 * capacity)
+            at = expert * (2 * capacity) + rank
             normed_part = normed_part + (row == at).astype(F32)
             select[:, (k + 1) * count : (k + 2) * count] = (row == at + capacity).astype(F32).astype(BF16)
+            column = jnp.sum(jnp.where(earlier_of == later_of, weights[k : k + 1, :], 0.0), axis=1, keepdims=True)
+            factors[:, k : k + 1] = column
         select[:, :count] = normed_part.astype(BF16)
-        if first:
-            values = all_tokens[...].astype(F32)
-            inverse[...] = lax.rsqrt(jnp.mean(values * values, axis=1, keepdims=True) + EPSILON)
+        values = all_tokens[...].astype(F32)
+        inverse[...] = lax.rsqrt(jnp.mean(values * values, axis=1, keepdims=True) + EPSILON)
 
     normed = (tokens[...].astype(F32) * inverse[...] * gain[...]).astype(BF16)
     values = cotangent[...].astype(F32)
-    parts = [normed] + [(weights[:, k : k + 1] * values).astype(BF16) for k in range(top)]
+    parts = [normed] + [(factors[:, k : k + 1] * values).astype(BF16) for k in range(top)]
     rows[...] = jnp.dot(select[...], jnp.concatenate(parts, axis=0), preferred_element_type=F32).astype(BF16)
 
 
-def make_message(place, tokens, cotangent, gain, ids, weights, inverse, capacity, plane, other):
+def make_message(place, tokens, cotangent, gain, ids, weights, capacity, experts):
     count, width = tokens.shape
+    top = ids.shape[0]
     half = width // 2
-    height = plane * 2 * capacity
+    height = experts * 2 * capacity
     steps = half // FILL
-    first = inverse is None
     column = lambda i, place: (0, place[0] * steps + i)
-    split = [pl.BlockSpec((count, FILL), column), pl.BlockSpec((count, FILL), column), pl.BlockSpec((1, FILL), column)]
-    last = (count, width) if first else (count, 1)
-    message = jax.ShapeDtypeStruct((height, half), BF16)
-    message_spec = pl.BlockSpec((height, FILL), lambda i, place: (0, i))
-    out = pl.pallas_call(
-        functools.partial(message_kernel, capacity, other, first),
-        out_shape=(message, jax.ShapeDtypeStruct((count, 1), F32)) if first else message,
+    return pl.pallas_call(
+        functools.partial(message_kernel, capacity),
+        out_shape=(jax.ShapeDtypeStruct((height, half), BF16), jax.ShapeDtypeStruct((count, 1), F32)),
         grid_spec=grid_of(
             (steps,),
-            split + [whole(ids.shape), whole(weights.shape), whole(last)],
-            (message_spec, whole((count, 1))) if first else message_spec,
-            [pltpu.VMEM((height, 3 * count), BF16)],
+            [
+                whole((count, width)),
+                pl.BlockSpec((count, FILL), column),
+                pl.BlockSpec((count, FILL), column),
+                pl.BlockSpec((1, FILL), column),
+                whole(ids.shape),
+                whole(weights.shape),
+            ],
+            (pl.BlockSpec((height, FILL), lambda i, place: (0, i)), whole((count, 1))),
+            [pltpu.VMEM((height, (top + 1) * count), BF16), pltpu.VMEM((count, top), F32)],
         ),
-        compiler_params=params(24),
+        compiler_params=params(32),
         name="message",
-    )(place, tokens, cotangent, gain, ids, weights, tokens if first else inverse)
-    return out
-
-
-def gather_kernel(capacity, place, ids, out):
-    count, top = ids.shape
+    )(place, tokens, tokens, cotangent, gain, ids, weights)
+
+
+def gather_kernel(capacity, ids, out):
+    top, count = ids.shape
     rows = out.shape[1]
-    plane = rows // (2 * capacity)
-    expert_of = lax.broadcasted_iota(jnp.int32, (count, 2 * plane), 1)
-    later_of = lax.broadcasted_iota(jnp.int32, (count, count), 0)
-    earlier_of = lax.broadcasted_iota(jnp.int32, (count, count), 1)
+    experts = rows // (2 * capacity)
+    expert_of = lax.broadcasted_iota(jnp.int32, (experts, count), 0)
+    earlier_of = lax.broadcasted_iota(jnp.int32, (count, count), 0)
+    later_of = lax.broadcasted_iota(jnp.int32, (count, count), 1)
     before = (earlier_of < later_of).astype(F32).astype(BF16)
-    row = lax.broadcasted_iota(jnp.int32, (count, rows), 1)
-    taken = jnp.zeros((1, 2 * plane), F32)
+    row = lax.broadcasted_iota(jnp.int32, (count, rows), 1).astype(F32)
+    taken = jnp.zeros((experts, 1), F32)
     first = jnp.zeros(row.shape, F32)
     second = jnp.zeros(row.shape, F32)
     for k in range(top):
-        expert = ids[:, k : k + 1]
+        expert = ids[k : k + 1, :]
         named = (expert_of == expert).astype(F32)
-        earlier = jnp.dot(before, named.astype(BF16), preferred_element_type=F32) + taken
-        rank = jnp.sum(earlier * named, axis=1, keepdims=True).astype(jnp.int32)
-        taken = taken + jnp.sum(named, axis=0, keepdims=True)
-        local = expert - place[1] * plane
-        at = jnp.where((local >= 0) & (local < plane), local * (2 * capacity) + rank, -2 * capacity)
+        earlier = jnp.dot(named.astype(BF16), before, preferred_element_type=F32) + taken
+        rank = jnp.sum(earlier * named, axis=0, keepdims=True)
+        taken = taken + jnp.sum(named, axis=1, keepdims=True)
+        at = expert.astype(F32) * (2 * capacity) + rank
+        at = jnp.sum(jnp.where(earlier_of == later_of, at, 0.0), axis=1, keepdims=True)
         first = first + (row == at).astype(F32)
         second = second + (row == at + capacity).astype(F32)
     out[:count, :] = first.astype(BF16)
     out[count:, :] = second.astype(BF16)
 
 
-def gather_matrix(place, ids, capacity, plane):
-    count = ids.shape[0]
-    rows = plane * 2 * capacity
+def gather_matrix(ids, capacity, experts):
+    count = ids.shape[1]
     return pl.pallas_call(
         functools.partial(gather_kernel, capacity),
-        out_shape=jax.ShapeDtypeStruct((2 * count, rows), BF16),
-        grid_spec=grid_of((1,), [whole(ids.shape)], whole((2 * count, rows))),
+        out_shape=jax.ShapeDtypeStruct((2 * count, experts * 2 * capacity), BF16),
         compiler_params=params(8),
         name="gather_matrix",
-    )(place, ids)
+    )(ids)
 
 
 def tiles(x, group):
@@ -285,7 +264,7 @@
                 pltpu.SemaphoreType.DMA((half // DEPTH, 4)),
             ],
         ),
-        compiler_params=params(20),
+        compiler_params=params(32),
         name="project",
     )(place, rows, gate, up, down)
 
@@ -375,7 +354,7 @@
                 pltpu.SemaphoreType.DMA((2,)),
             ],
         ),
-        compiler_params=params(32),
+        compiler_params=params(48),
         name="expert",
     )(place, rows, gate, up, down, *accs)
 
@@ -384,12 +363,12 @@
     count = first.shape[0]
     total = jnp.dot(gather[...], rows[...], preferred_element_type=F32)
     low, high = total[:count], total[count:]
-    flip = place[2] == 1
+    flip = place[1] == 1
     first[...] = jnp.where(flip, high, low).astype(first.dtype)
     second[...] = jnp.where(flip, low, high).astype(second.dtype)
 
 
-def combine(place, gather, rows, first_type):
+def combine(place, gather, rows):
     count = gather.shape[0] // 2
     columns = rows.shape[1]
     part = columns // 3
@@ -397,7 +376,7 @@
     return pl.pallas_call(
         combine_kernel,
         out_shape=(
-            jax.ShapeDtypeStruct((count, columns), first_type),
+            jax.ShapeDtypeStruct((count, columns), F32),
             jax.ShapeDtypeStruct((count, columns), BF16),
         ),
         grid_spec=grid_of(
@@ -412,57 +391,37 @@
 
 def body(tokens, cotangent, norm_gain, expert_ids, gate_weights, w_gate, w_up, w_down):
     experts = lax.axis_size("expert")
-    plane = experts // 2
     token_count, width = tokens.shape
     top_count = expert_ids.shape[1]
     capacity = token_count * top_count * 3 // (2 * experts)
     columns = width // lax.axis_size("pipe")
     pipe = lax.axis_index("pipe")
-    core, high = lax.rem(pipe, 2), pipe // 2
-    low = lax.axis_index("expert") // plane
-    after = lax.rem(2 * high + low + 1, 4) // 2
-    place = jnp.stack([core, low, high]).astype(jnp.int32)
-    place_after = jnp.stack([core, low, after]).astype(jnp.int32)
+    place = jnp.stack([lax.rem(pipe, 2), pipe // 2]).astype(jnp.int32)
     weights = tuple(in_hbm(array[0]) for array in (w_gate, w_up, w_down))
-
-    gain = norm_gain.reshape(1, width)
-    make = functools.partial(
-        make_message, place, in_hbm(tokens), in_hbm(cotangent), gain, expert_ids.T, gate_weights, capacity=capacity, plane=plane
+    ids = in_hbm(expert_ids.T)
+
+    rows, inverse = make_message(
+        place,
+        in_hbm(tokens),
+        in_hbm(cotangent),
+        in_hbm(norm_gain.reshape(1, width)),
+        ids,
+        in_hbm(gate_weights.T),
+        capacity,
+        experts,
     )
-    other, inverse = make(inverse=None, other=True)
-    own = make(inverse=inverse, other=False)
-    other_ids = lax.ppermute(expert_ids, "expert", [(k, (k + plane) % experts) for k in range(experts)])
-    gathers = [gather_matrix(place, ids, capacity, plane) for ids in (expert_ids, other_ids)]
-
-    other = ring_permute(other, (1, 3))
-    own = plane_exchange(own)
-    own, *gathers = lax.optimization_barrier((own, *gathers))
-    other = plane_exchange(other)
-
-    def compute(rows, first):
-        accs = project(place, rows, weights)
-        swapped = core_swap(rows)
-        accs, swapped, *first = lax.optimization_barrier((accs, swapped, *first))
-        theirs, mine = expert(place, swapped, weights, accs)
-        summed = mine.astype(F32) + core_swap(theirs).astype(F32)
-        return summed.astype(BF16), first
-
-    own_back, _ = compute(own, ())
-    own_back, other = lax.optimization_barrier((own_back, other))
-    own_back = plane_exchange(own_back)
-    other_back, (own_back,) = compute(other, (own_back,))
-    other_back = plane_exchange(other_back)
-
-    kept, sent = combine(place, gathers[0], own_back, F32)
-    from_far = ring_permute(sent, (2, 2))
-    forth, back_ = combine(place_after, gathers[1], other_back, BF16)
-    from_before = ring_permute(forth, (1, 1))
-    from_after = ring_permute(back_, (3, 3))
+    gather = gather_matrix(ids, capacity, experts)
+    rows, gather = lax.optimization_barrier((rows, gather))
+    rows = exchange(rows)
+    accs = project(place, rows, weights)
+    theirs, mine = expert(place, in_hbm(core_swap(rows)), weights, accs)
+    back = exchange((mine.astype(F32) + core_swap(theirs).astype(F32)).astype(BF16))
+    kept, sent = combine(place, gather, back)
+    total = kept + high_swap(sent).astype(F32)
 
     def own_columns(array):
         return lax.dynamic_slice_in_dim(array, pipe * columns, columns, array.ndim - 1)
 
-    total = kept + from_far.astype(F32) + from_before.astype(F32) + from_after.astype(F32)
     normed_grad, product = total[:, :columns], total[:, columns : columns + 1]
     value_part = own_columns(tokens).astype(F32)
     cotangent_part = own_columns(cotangent).astype(F32)

time: 211 us -> 181 us (0.86)
  blocking collectives: 0 us -> 116 us
  waiting for transfers between devices: 96 us -> 15.6 us
  starting transfers between devices: 35.8 us -> 3.06 us
  Pallas kernels: 62 us -> 37.5 us
  local copies, waits for them, and re-layouts: 8.93 us -> 3.16 us
    all_to_all x0 -> x2, blocking collectives: none -> 116 us  [exchange(): lax.all_to_all(shaped, 'expert', split_axis=0, concat_axis=0, tiled=True)]
    all_to_all x4 -> x0, waiting for transfers between devices: 48.3 us -> none  [plane_exchange(): lax.all_to_all(shaped, 'expert', split_axis=0, concat_axis=0, tiled=True,...]
    ppermute x5 -> x1, waiting for transfers between devices: 41.4 us -> 9.22 us  [high_swap(): return lax.ppermute(array, 'pipe', HIGH_SWAP)]
    all_to_all x4 -> x0, starting transfers between devices: 26.5 us -> none  [plane_exchange(): lax.all_to_all(shaped, 'expert', split_axis=0, concat_axis=0, tiled=True,...]
    pallas_call x2 -> x1, Pallas kernels: 28.3 us -> 18.9 us  [expert(): pl.pallas_call(expert_kernel, out_shape=(message, message), grid_spec=gri...]
    ppermute x5 -> x1, starting transfers between devices: 8.9 us -> 2.82 us  [high_swap(): return lax.ppermute(array, 'pipe', HIGH_SWAP)]
    unnamed x24 -> x2, local copies, waits for them, and re-layouts: 8.15 us -> 2.38 us
    pallas_call x2 -> x1, Pallas kernels: 13.5 us -> 7.9 us  [project(): pl.pallas_call(project_kernel, out_shape=(acc,) * 3, grid_spec=grid_of((1...]
  transfers between devices with their start and end apart: 13 -> 3, of which waited for: 9 -> 3; matrix products, arithmetic and copies ran while one was open for 1% -> 0% of each run, Pallas kernels for 17% -> 4%
where the time goes in v3:
time: 181 us; the launch traced here: 180 us
  blocking collectives  116 us (64%)
  Pallas kernels  37.5 us (21%)
  waiting for transfers between devices  15.6 us (9%)
  other arithmetic  5.1 us (3%)
  local copies, waits for them, and re-layouts  3.16 us (2%)
  starting transfers between devices  3.06 us (2%)
    all_to_all x2, blocking collectives, exchange(): lax.all_to_all(shaped, 'expert', split_axis=0, concat_axis=0, tiled=True)  116 us
    pallas_call x1, Pallas kernels, expert(): pl.pallas_call(expert_kernel, out_shape=(message, message), grid_spec=gri...  18.9 us
    ppermute x1, waiting for transfers between devices, high_swap(): return lax.ppermute(array, 'pipe', HIGH_SWAP)  9.22 us
    pallas_call x1, Pallas kernels, project(): pl.pallas_call(project_kernel, out_shape=(acc,) * 3, grid_spec=grid_of((1...  7.9 us
    pallas_call x1, Pallas kernels, make_message(): pl.pallas_call(functools.partial(message_kernel, capacity), out_shape=(ja...  7.19 us
    ppermute x2, waiting for transfers between devices, core_swap(): return lax.ppermute(array, 'pipe', CORE_SWAP)  6.35 us
  transfers between devices with their start and end apart: 3, of which 3 were waited for; matrix products, arithmetic and copies ran while one was open for 0% of the time, Pallas kernels for 4%

profile of v3, /device:TPU:0, one launch (start us, length us, event | category | flops | bytes accessed | tf_op | source)
XLA Modules:
  0.0 180.0 jit_solution(1043321551254439012)
XLA Ops:
  0.0 1.0 gather_matrix.1.gather
  1.1 0.1 pad_add_fusion.place
  1.1 7.2 %message.1 = (bf16[768,3584]{1,0:T(8,128)(2,1)S(1)}, f32[128,1]{1,0:T(8,128)S(1)}) custom-call(s32[2]{0:T(128)S(1)} %pad_add_fusion.place, bf16[128,7168]{1,0:T(8,128)(2,1)} %tokens.1, bf16[128,7168]{1,0:T(8,128)(2,1)} %tokens.1, bf16[128,7168]{1,0:T(8,128)(2,1)} %cotangent.1, f32[1,7168]{1,0:T(1,128)} %bitcast.23, s32[2,128]{1,0:T(2,128)} %bitcast.25, ...), custom_call_target="tpu_custom_call" | custom-call | tf_op jit(solution)/shard_map/message/pallas_call | solution.py:98
  8.3 74.7 %all_to_all.10 = bf16[32,24,3584]{2,1,0:T(8,128)(2,1)S(1)} all-to-all(bf16[32,24,3584]{2,1,0:T(8,128)(2,1)S(1)} %bitcast.15), channel_id=1, replica_groups=mesh['pipe'=4,'expert'=32] {'expert'}, dimensions={0} | all-to-all | bytes 11010048 | tf_op jit(solution)/shard_map/all_to_all | solution.py:53
  83.0 0.0 collective-permute-start
  83.0 7.9 %project.1 = (f32[384,512]{1,0:T(8,128)S(1)}, f32[384,512]{1,0:T(8,128)S(1)}, f32[384,512]{1,0:T(8,128)S(1)}) custom-call(s32[2]{0:T(128)S(1)} %pad_add_fusion.place, bf16[768,3584]{1,0:T(8,128)(2,1)S(1)} %bitcast.13, bf16[7168,512]{1,0:T(8,128)(2,1)} %bitcast.16, bf16[7168,512]{1,0:T(8,128)(2,1)} %bitcast.18, bf16[512,7168]{1,0:T(8,128)(2,1)} %bitcast.20), custom_call_target="tpu_custom_call" | custom-call | tf_op jit(solution)/shard_map/project/pallas_call | solution.py:252
  90.9 1.1 collective-permute-done.rows
  92.0 0.0 copy-start
  92.0 2.4 %copy-done = bf16[768,3584]{1,0:T(8,128)(2,1)} copy-done((bf16[768,3584]{1,0:T(8,128)(2,1)}, bf16[768,3584]{1,0:T(8,128)(2,1)S(1)}, u32[]{:S(2)}) %copy-start) | copy-done | bytes 5505048
  94.4 18.9 %expert.1 = (bf16[768,1920]{1,0:T(8,128)(2,1)S(1)}, bf16[768,1920]{1,0:T(8,128)(2,1)}) custom-call(s32[2]{0:T(128)S(1)} %pad_add_fusion.place, bf16[768,3584]{1,0:T(8,128)(2,1)} %copy-done, bf16[7168,512]{1,0:T(8,128)(2,1)} %bitcast.17, bf16[7168,512]{1,0:T(8,128)(2,1)} %bitcast.19, bf16[512,7168]{1,0:T(8,128)(2,1)} %bitcast.21, ...), custom_call_target="tpu_custom_call" | custom-call | tf_op jit(solution)/shard_map/expert/pallas_call | solution.py:336
  113.4 0.2 collective-permute-start.1
  113.6 5.2 %collective-permute-done.1 = bf16[768,1920]{1,0:T(8,128)(2,1)S(1)} collective-permute-done((bf16[768,1920]{1,0:T(8,128)(2,1)S(1)}, bf16[768,1920]{1,0:T(8,128)(2,1)S(1)}, u32[]{:S(2)}, u32[]{:S(2)}) %collective-permute-start.1) | collective-permute-done | bytes 2949152 | tf_op jit(solution)/shard_map/ppermute | solution.py:43
  118.8 2.6 %add_convert_fusion = bf16[768,1920]{1,0:T(8,128)(2,1)S(1)} fusion(bf16[768,1920]{1,0:T(8,128)(2,1)S(1)} %collective-permute-done.1, bf16[768,1920]{1,0:T(8,128)(2,1)} %get-tuple-element.23), kind=kLoop, calls=%fused_computation | loop fusion | flops 5898240 | bytes 8847360 | tf_op jit(solution)/shard_map/convert_element_type | solution.py:418
  121.4 40.9 %all_to_all.11 = bf16[32,24,1920]{2,1,0:T(8,128)(2,1)S(1)} all-to-all(bf16[32,24,1920]{2,1,0:T(8,128)(2,1)S(1)} %bitcast.22), channel_id=1, replica_groups=mesh['pipe'=4,'expert'=32] {'expert'}, dimensions={0} | all-to-all | bytes 5898240 | tf_op jit(solution)/shard_map/all_to_all | solution.py:53
  162.3 2.4 %combine.1 = (f32[128,1920]{1,0:T(8,128)S(1)}, bf16[128,1920]{1,0:T(8,128)(2,1)S(1)}) custom-call(s32[2]{0:T(128)S(1)} %pad_add_fusion.place, bf16[256,768]{1,0:T(8,128)(2,1)S(1)} %gather_matrix.1.gather, bf16[768,1920]{1,0:T(8,128)(2,1)S(1)} %bitcast.14), custom_call_target="tpu_custom_call" | custom-call | tf_op jit(solution)/shard_map/combine/pallas_call | solution.py:376
  164.8 2.8 %collective-permute-start.2 = (bf16[128,1920]{1,0:T(8,128)(2,1)S(1)}, bf16[128,1920]{1,0:T(8,128)(2,1)S(1)}, u32[]{:S(2)}, u32[]{:S(2)}) collective-permute-start(bf16[128,1920]{1,0:T(8,128)(2,1)S(1)} %get-tuple-element.26), channel_id=1, source_target_pairs={{0,64},{64,0},{32,96},{96,32},{1,65},{65,1},{33,97},{97,33},{2,66}... | collective-permute-start | bytes 1474568 | tf_op jit(solution)/shard_map/ppermute | solution.py:47
  167.6 0.8 dynamic_slice.10
  168.4 9.2 %collective-permute-done.2 = bf16[128,1920]{1,0:T(8,128)(2,1)S(1)} collective-permute-done((bf16[128,1920]{1,0:T(8,128)(2,1)S(1)}, bf16[128,1920]{1,0:T(8,128)(2,1)S(1)}, u32[]{:S(2)}, u32[]{:S(2)}) %collective-permute-start.2) | collective-permute-done | bytes 491552 | tf_op jit(solution)/shard_map/ppermute | solution.py:47
  177.6 0.1 convert_add_fusion
  177.7 0.1 fusion.5
  177.8 2.2 %fusion.2 = bf16[128,1792]{1,0:T(8,128)(2,1)} fusion(f32[128,1920]{1,0:T(8,128)S(1)} %convert_add_fusion, f32[128]{0:T(128)S(1)} %get-tuple-element.28, bf16[128,7168]{1,0:T(8,128)(2,1)} %tokens.1, s32[]{:T(128)S(6)} %select_n.10, f32[1792]{0:T(1024)S(1)} %dynamic_slice.10, f32[128]{0:T(128)S(1)} %get-tuple-element.27, bf16[128,7168]{1,0:T(8,128)(2,1)} %cotangent.1), kind=kLoop, calls=%fused_computation.5 | loop fusion | flops 1835008 | bytes 2301956 | tf_op jit(solution)/shard_map/convert_element_type | solution.py:432
Async XLA Ops:
  83.0 9.0 %collective-permute-start = (bf16[768,3584]{1,0:T(8,128)(2,1)S(1)}, bf16[768,3584]{1,0:T(8,128)(2,1)S(1)}, u32[]{:S(2)}, u32[]{:S(2)}) collective-permute-start(bf16[768,3584]{1,0:T(8,128)(2,1)S(1)} %bitcast.12), channel_id=1, source_target_pairs={{0,32},{32,0},{64,96},{96,64},{1,33},{33,1},{65,97},{97,65},{2,34}... | collective-permute-start | bytes 16515080 | tf_op jit(solution)/shard_map/ppermute | solution.py:43
  92.0 2.4 %copy-start = (bf16[768,3584]{1,0:T(8,128)(2,1)}, bf16[768,3584]{1,0:T(8,128)(2,1)S(1)}, u32[]{:S(2)}) copy-start(bf16[768,3584]{1,0:T(8,128)(2,1)S(1)} %collective-permute-done.rows) | copy-start | bytes 16515076
  113.4 5.5 %collective-permute-start.1 = (bf16[768,1920]{1,0:T(8,128)(2,1)S(1)}, bf16[768,1920]{1,0:T(8,128)(2,1)S(1)}, u32[]{:S(2)}, u32[]{:S(2)}) collective-permute-start(bf16[768,1920]{1,0:T(8,128)(2,1)S(1)} %get-tuple-element.24), channel_id=1, source_target_pairs={{0,32},{32,0},{64,96},{96,64},{1,33},{33,1},{65,97},{97,65},{2,34}... | collective-permute-start | bytes 8847368 | tf_op jit(solution)/shard_map/ppermute | solution.py:43
  164.8 12.8 %collective-permute-start.2 = (bf16[128,1920]{1,0:T(8,128)(2,1)S(1)}, bf16[128,1920]{1,0:T(8,128)(2,1)S(1)}, u32[]{:S(2)}, u32[]{:S(2)}) collective-permute-start(bf16[128,1920]{1,0:T(8,128)(2,1)S(1)} %get-tuple-element.26), channel_id=1, source_target_pairs={{0,64},{64,0},{32,96},{96,32},{1,65},{65,1},{33,97},{97,33},{2,66}... | collective-permute-start | bytes 1474568 | tf_op jit(solution)/shard_map/ppermute | solution.py:47

commit v4 on v3

--- a/solution.py
+++ b/solution.py
@@ -14,8 +14,10 @@
 FILL = 1792
 DEPTH = 1792
 AHEAD = 1
-BACK = 896
+BACK = 512
+DIRECT = 1024
 LANES = 128
+SMALL = pl.CostEstimate(flops=0, bytes_accessed=0, transcendentals=0)
 LAST = (((1,), (1,)), ((), ()))
 CORE_SWAP = [(0, 1), (1, 0), (2, 3), (3, 2)]
 HIGH_SWAP = [(0, 2), (2, 0), (1, 3), (3, 1)]
@@ -205,14 +207,14 @@
         local = pl.ds(i * DEPTH, DEPTH)
         at = pl.ds(pl.multiple_of(side * half + i * DEPTH, DEPTH), DEPTH)
         to = pl.ds(pl.multiple_of(gate_at + i * DEPTH, DEPTH), DEPTH)
-        copies.append(
-            [
-                pltpu.make_async_copy(rows.at[:, local], rows_in.at[:, local], sems.at[i, 0]),
-                pltpu.make_async_copy(gate.at[at, :], gate_in.at[to, :], sems.at[i, 1]),
-                pltpu.make_async_copy(up.at[at, :], up_in.at[to, :], sems.at[i, 2]),
-                pltpu.make_async_copy(down.at[:, at], down_in.at[:, local], sems.at[i, 3]),
-            ]
-        )
+        copy = [
+            pltpu.make_async_copy(gate.at[at, :], gate_in.at[to, :], sems.at[i, 1]),
+            pltpu.make_async_copy(up.at[at, :], up_in.at[to, :], sems.at[i, 2]),
+            pltpu.make_async_copy(down.at[:, at], down_in.at[:, local], sems.at[i, 3]),
+        ]
+        if rows is not None:
+            copy.append(pltpu.make_async_copy(rows.at[:, local], rows_in.at[:, local], sems.at[i, 0]))
+        copies.append(copy)
     return copies
 
 
@@ -269,13 +271,11 @@
     )(place, rows, gate, up, down)
 
 
-def expert_kernel(place, rows, gate, up, down, in_gate, in_up, in_hidden, theirs, mine, rows_in, gate_in, up_in, down_in, acc_gate, acc_up, acc_hidden, out, sems, more_sems, out_sems):
+def expert_kernel(place, rows, gate, up, down, in_gate, in_up, in_hidden, theirs, mine, grad_gate, grad_up, gate_in, up_in, down_in, acc_gate, acc_up, acc_hidden, out, sems, more_sems, out_sems):
     half = rows.shape[1]
     core = place[0]
     side = 1 - core
-    copies = chunk_copies(
-        side, half, rows, gate, up, down, rows_in, gate_in, up_in, down_in, side * half, sems
-    )
+    copies = chunk_copies(side, half, None, gate, up, down, None, gate_in, up_in, down_in, side * half, sems)
     rest = []
     for i in range(half // DEPTH):
         at = pl.ds(pl.multiple_of(core * half + i * DEPTH, DEPTH), DEPTH)
@@ -291,34 +291,35 @@
     for acc, value in zip(accs, (in_gate, in_up, in_hidden)):
         acc[...] = value[...]
     ahead = list(rest)
-    project_half(copies, rows_in, gate_in, up_in, down_in, side * half, accs, False, ahead)
+    project_half(copies, rows, gate_in, up_in, down_in, side * half, accs, False, ahead)
     for copy in ahead:
         start_all(copy)
 
     pre_gate, pre_up, hidden = acc_gate[...], acc_up[...], acc_hidden[...]
     sigma = jax.nn.sigmoid(pre_gate)
-    grad_gate = hidden * pre_up * sigma * (1.0 + pre_gate * (1.0 - sigma))
-    grad_up = hidden * pre_gate * sigma
-    product = jnp.sum(grad_gate * pre_gate + grad_up * pre_up, axis=1, keepdims=True)
+    to_gate = hidden * pre_up * sigma * (1.0 + pre_gate * (1.0 - sigma))
+    to_up = hidden * pre_gate * sigma
+    product = jnp.sum(to_gate * pre_gate + to_up * pre_up, axis=1, keepdims=True)
     product = jnp.broadcast_to(product, (product.shape[0], LANES))
     product = interleave(product, product).astype(BF16)
-    grad_gate, grad_up = grad_gate.astype(BF16), grad_up.astype(BF16)
+    grad_gate[...] = to_gate.astype(BF16)
+    grad_up[...] = to_up.astype(BF16)
     for copy in rest:
         wait_all(copy)
 
-    columns = out.shape[2] - LANES
+    columns = gate.shape[0] // 4
 
     def one(start):
         at = pl.ds(pl.multiple_of(start, LANES), BACK)
-        total = lax.dot_general(grad_gate, gate_in[at, :], LAST, preferred_element_type=F32)
-        return total + lax.dot_general(grad_up, up_in[at, :], LAST, preferred_element_type=F32)
+        total = lax.dot_general(grad_gate[...], gate_in[at, :], LAST, preferred_element_type=F32)
+        return total + lax.dot_general(grad_up[...], up_in[at, :], LAST, preferred_element_type=F32)
 
     sent = []
     for slot, (to, whose) in enumerate(((theirs, side), (mine, core))):
-        for at in range(0, columns, BACK):
+        for at in range(0, DIRECT, BACK):
             low, high = one(whose * columns + at), one((2 + whose) * columns + at)
             out[slot, :, at : at + BACK] = interleave(low, high).astype(BF16)
-        out[slot, :, columns:] = product
+        out[slot, :, DIRECT:] = product
         copy = pltpu.make_async_copy(out.at[slot], to, out_sems.at[slot])
         copy.start()
         sent.append(copy)
@@ -329,19 +330,18 @@
     gate, up, down = weights
     height, half = rows.shape
     width, hidden = gate.shape
-    columns = width // 4
     any_space = pl.BlockSpec(memory_space=pl.ANY)
-    message = jax.ShapeDtypeStruct((height, columns + LANES), BF16)
+    message = jax.ShapeDtypeStruct((height, DIRECT + LANES), BF16)
     acc = accs[0].shape
+    grad = jax.ShapeDtypeStruct(acc, BF16)
     return pl.pallas_call(
         expert_kernel,
-        out_shape=(message, message),
+        out_shape=(message, message, grad, grad),
         grid_spec=grid_of(
             (1,),
-            [any_space] * 4 + [whole(acc)] * 3,
-            (any_space, any_space),
+            [pl.BlockSpec(memory_space=pltpu.VMEM)] + [any_space] * 3 + [whole(acc)] * 3,
+            (any_space, any_space, whole(acc), whole(acc)),
             [
-                pltpu.VMEM((height, half), BF16),
                 pltpu.VMEM((width, hidden), BF16),
                 pltpu.VMEM((width, hidden), BF16),
                 pltpu.VMEM((hidden, half), BF16),
@@ -354,9 +354,68 @@
                 pltpu.SemaphoreType.DMA((2,)),
             ],
         ),
-        compiler_params=params(48),
+        compiler_params=params(40),
         name="expert",
     )(place, rows, gate, up, down, *accs)
+
+
+def rest_kernel(place, grad_gate, grad_up, gate, up, theirs, mine, gate_in, up_in, out, sems, out_sems):
+    columns = gate.shape[0] // 4
+    core, high = place[0], place[1]
+    width = columns - DIRECT
+    half = width // 2
+    copies = []
+    for slot, whose in enumerate((1 - core, core)):
+        for turn, part in enumerate((high, 1 - high)):
+            at = pl.ds(pl.multiple_of((2 * part + whose) * columns + DIRECT, 256), width)
+            to = 2 * slot + turn
+            copies.append(
+                [
+                    pltpu.make_async_copy(gate.at[at, :], gate_in.at[to], sems.at[to, 0]),
+                    pltpu.make_async_copy(up.at[at, :], up_in.at[to], sems.at[to, 1]),
+                ]
+            )
+    for copy in copies:
+        start_all(copy)
+    sent = []
+    for slot, to in enumerate((theirs, mine)):
+        for turn in range(2):
+            at = 2 * slot + turn
+            wait_all(copies[at])
+            rows = lax.dot_general(grad_gate[...], gate_in[at], LAST, preferred_element_type=F32)
+            rows = rows + lax.dot_general(grad_up[...], up_in[at], LAST, preferred_element_type=F32)
+            out[slot, :, turn * half : (turn + 1) * half] = interleave(rows[:, :half], rows[:, half:]).astype(BF16)
+        copy = pltpu.make_async_copy(out.at[slot], to, out_sems.at[slot])
+        copy.start()
+        sent.append(copy)
+    wait_all(sent)
+
+
+def rest(place, grads, weights):
+    gate, up, _ = weights
+    rows, hidden = grads[0].shape
+    width = gate.shape[0] // 4 - DIRECT
+    any_space = pl.BlockSpec(memory_space=pl.ANY)
+    message = jax.ShapeDtypeStruct((2 * rows, width), BF16)
+    return pl.pallas_call(
+        rest_kernel,
+        out_shape=(message, message),
+        grid_spec=grid_of(
+            (1,),
+            [whole((rows, hidden))] * 2 + [any_space] * 2,
+            (any_space, any_space),
+            [
+                pltpu.VMEM((4, width, hidden), BF16),
+                pltpu.VMEM((4, width, hidden), BF16),
+                pltpu.VMEM((2,) + message.shape, BF16),
+                pltpu.SemaphoreType.DMA((4, 2)),
+                pltpu.SemaphoreType.DMA((2,)),
+            ],
+        ),
+        compiler_params=params(24),
+        cost_estimate=SMALL,
+        name="rest",
+    )(place, *grads, gate, up)
 
 
 def combine_kernel(place, gather, rows, first, second):
@@ -389,47 +448,71 @@
     )(place, gather, rows)
 
 
+def final_kernel(width, place, gather, rows, kept, arrived, tokens, cotangent, gain, inverse, out):
+    count = tokens.shape[0]
+    total = jnp.dot(gather[...], rows[...], preferred_element_type=F32)
+    direct = kept[...] + arrived[...].astype(F32)
+    scale = inverse[...]
+    product = scale * scale * direct[:, DIRECT : DIRECT + 1] / width
+    half = rows.shape[1]
+    for at, size, grad in (
+        (0, DIRECT, direct[:, :DIRECT]),
+        (DIRECT, half, total[:count]),
+        (DIRECT + half, half, total[count:]),
+    ):
+        part = slice(at, at + size)
+        value = cotangent[:, part].astype(F32) + scale * gain[:, part] * grad
+        out[:, part] = (value - tokens[:, part].astype(F32) * product).astype(BF16)
+
+
+def final(place, gather, rows, kept, arrived, tokens, cotangent, gain, inverse):
+    count, width = tokens.shape
+    columns = width // 4
+    quarter = lambda height: pl.BlockSpec((height, columns), lambda i, place: (0, place[2]))
+    return pl.pallas_call(
+        functools.partial(final_kernel, width),
+        out_shape=jax.ShapeDtypeStruct((count, columns), BF16),
+        grid_spec=grid_of(
+            (1,),
+            [whole(array.shape) for array in (gather, rows, kept, arrived)]
+            + [quarter(count), quarter(count), quarter(1), whole(inverse.shape)],
+            whole((count, columns)),
+        ),
+        compiler_params=params(16),
+        name="final",
+    )(place, gather, rows, kept, arrived, tokens, cotangent, gain, inverse)
+
+
 def body(tokens, cotangent, norm_gain, expert_ids, gate_weights, w_gate, w_up, w_down):
     experts = lax.axis_size("expert")
     token_count, width = tokens.shape
     top_count = expert_ids.shape[1]
     capacity = token_count * top_count * 3 // (2 * experts)
-    columns = width // lax.axis_size("pipe")
     pipe = lax.axis_index("pipe")
-    place = jnp.stack([lax.rem(pipe, 2), pipe // 2]).astype(jnp.int32)
+    place = jnp.stack([lax.rem(pipe, 2), pipe // 2, pipe]).astype(jnp.int32)
     weights = tuple(in_hbm(array[0]) for array in (w_gate, w_up, w_down))
     ids = in_hbm(expert_ids.T)
+    tokens, cotangent, gain = in_hbm(tokens), in_hbm(cotangent), in_hbm(norm_gain.reshape(1, width))
 
     rows, inverse = make_message(
-        place,
-        in_hbm(tokens),
-        in_hbm(cotangent),
-        in_hbm(norm_gain.reshape(1, width)),
-        ids,
-        in_hbm(gate_weights.T),
-        capacity,
-        experts,
+        place, tokens, cotangent, gain, ids, in_hbm(gate_weights.T), capacity, experts
     )
     gather = gather_matrix(ids, capacity, experts)
     rows, gather = lax.optimization_barrier((rows, gather))
     rows = exchange(rows)
     accs = project(place, rows, weights)
-    theirs, mine = expert(place, in_hbm(core_swap(rows)), weights, accs)
-    back = exchange((mine.astype(F32) + core_swap(theirs).astype(F32)).astype(BF16))
-    kept, sent = combine(place, gather, back)
-    total = kept + high_swap(sent).astype(F32)
-
-    def own_columns(array):
-        return lax.dynamic_slice_in_dim(array, pipe * columns, columns, array.ndim - 1)
-
-    normed_grad, product = total[:, :columns], total[:, columns : columns + 1]
-    value_part = own_columns(tokens).astype(F32)
-    cotangent_part = own_columns(cotangent).astype(F32)
-    return (
-        cotangent_part
-        + inverse * own_columns(norm_gain) * normed_grad
-        - value_part * (inverse * inverse * product / width)
-    ).astype(BF16)
+    theirs, mine, *grads = expert(place, core_swap(rows), weights, accs)
+    direct = (mine.astype(F32) + core_swap(theirs).astype(F32)).astype(BF16)
+
+    theirs, mine = rest(place, grads, weights)
+    summed = mine.astype(F32) + core_swap(theirs).astype(F32)
+    half = summed.shape[1] // 2
+    summed = summed[:, :half] + high_swap(summed[:, half:].astype(BF16)).astype(F32)
+    direct = exchange(direct)
+    direct, summed = lax.optimization_barrier((direct, summed.astype(BF16)))
+    kept, sent = combine(place, gather, direct)
+    arrived = high_swap(sent)
+    return final(place, gather, exchange(summed), kept, arrived, tokens, cotangent, gain, inverse)
 
 
 def solution(mesh):

time: 181 us -> 181 us (level)
  blocking collectives: 116 us -> 74.7 us
  waiting for transfers between devices: 15.6 us -> 42.7 us
  starting transfers between devices: 3.06 us -> 17.3 us
  Pallas kernels: 37.5 us -> 41.5 us
  local copies, waits for them, and re-layouts: 3.16 us -> 0.07 us
    all_to_all x2 -> x1, blocking collectives: 116 us -> 74.7 us  [exchange(): lax.all_to_all(shaped, 'expert', split_axis=0, concat_axis=0, tiled=True)]
    ppermute x1 -> x2, waiting for transfers between devices: 9.22 us -> 41.4 us  [high_swap(): return lax.ppermute(array, 'pipe', HIGH_SWAP)]
    all_to_all x0 -> x2, starting transfers between devices: none -> 11.5 us  [exchange(): lax.all_to_all(shaped, 'expert', split_axis=0, concat_axis=0, tiled=True)]
    ppermute x2 -> x3, waiting for transfers between devices: 6.35 us -> 1.3 us  [core_swap(): return lax.ppermute(array, 'pipe', CORE_SWAP)]
    pallas_call x1 -> x3, Pallas kernels: 18.9 us -> 23.6 us  [the longest x1 14.2 us: expert(): pl.pallas_call(expert_kernel, out_shape=(message, message, grad, grad), g...]
    unnamed x2 -> x0, local copies, waits for them, and re-layouts: 2.38 us -> none
    convert_element_type x2, other arithmetic: 4.83 us -> 2.64 us  [the longest x1 1.68 us: body(): direct = (mine.astype(F32) + core_swap(theirs).astype(F32)).astype(BF16)]
    ppermute x1 -> x2, starting transfers between devices: 2.82 us -> 4.9 us  [high_swap(): return lax.ppermute(array, 'pipe', HIGH_SWAP)]
  transfers between devices with their start and end apart: 3 -> 7, of which waited for: 3 -> 3; matrix products, arithmetic and copies ran while one was open for 0% -> 2% of each run, Pallas kernels for 4% -> 9%
where the time goes in v4:
time: 181 us; the launch traced here: 180 us
  blocking collectives  74.7 us (41%)
  waiting for transfers between devices  42.7 us (24%)
  Pallas kernels  41.5 us (23%)
  starting transfers between devices  17.3 us (10%)
  other arithmetic  4.22 us (2%)
    all_to_all x1, blocking collectives, exchange(): lax.all_to_all(shaped, 'expert', split_axis=0, concat_axis=0, tiled=True)  74.7 us
    ppermute x2, waiting for transfers between devices, high_swap(): return lax.ppermute(array, 'pipe', HIGH_SWAP)  41.4 us
    pallas_call x1, Pallas kernels, expert(): pl.pallas_call(expert_kernel, out_shape=(message, message, grad, grad), g...  14.2 us
    all_to_all x2, starting transfers between devices, exchange(): lax.all_to_all(shaped, 'expert', split_axis=0, concat_axis=0, tiled=True)  11.5 us
    pallas_call x1, Pallas kernels, project(): pl.pallas_call(project_kernel, out_shape=(acc,) * 3, grid_spec=grid_of((1...  7.73 us
    pallas_call x1, Pallas kernels, make_message(): pl.pallas_call(functools.partial(message_kernel, capacity), out_shape=(ja...  7.2 us
    pallas_call x1, Pallas kernels, rest(): pl.pallas_call(rest_kernel, out_shape=(message, message), grid_spec=grid_...  6.36 us
    ppermute x2, starting transfers between devices, high_swap(): return lax.ppermute(array, 'pipe', HIGH_SWAP)  4.9 us
  transfers between devices with their start and end apart: 7, of which 3 were waited for; matrix products, arithmetic and copies ran while one was open for 2% of the time, Pallas kernels for 9%

profile of v4, /device:TPU:0, one launch (start us, length us, event | category | flops | bytes accessed | tf_op | source)
XLA Modules:
  0.0 180.5 jit_solution(11838949794993452716)
XLA Ops:
  0.0 1.0 gather_matrix.1.gather
  1.1 0.1 pad_add_fusion.place
  1.1 7.2 %message.1 = (bf16[768,3584]{1,0:T(8,128)(2,1)S(1)}, f32[128,1]{1,0:T(8,128)S(1)}) custom-call(s32[3]{0:T(128)S(1)} %pad_add_fusion.place, bf16[128,7168]{1,0:T(8,128)(2,1)} %tokens.3, bf16[128,7168]{1,0:T(8,128)(2,1)} %tokens.3, bf16[128,7168]{1,0:T(8,128)(2,1)} %cotangent.3, f32[1,7168]{1,0:T(1,128)} %bitcast.29, s32[2,128]{1,0:T(2,128)} %bitcast.32, ...), custom_call_target="tpu_custom_call" | custom-call | tf_op jit(solution)/shard_map/message/pallas_call | solution.py:100
  8.3 74.7 %all_to_all.15 = bf16[32,24,3584]{2,1,0:T(8,128)(2,1)S(1)} all-to-all(bf16[32,24,3584]{2,1,0:T(8,128)(2,1)S(1)} %bitcast.18), channel_id=1, replica_groups=mesh['pipe'=4,'expert'=32] {'expert'}, dimensions={0} | all-to-all | bytes 11010048 | tf_op jit(solution)/shard_map/all_to_all | solution.py:55
  83.0 0.0 collective-permute-start
  83.0 7.7 %project.1 = (f32[384,512]{1,0:T(8,128)S(1)}, f32[384,512]{1,0:T(8,128)S(1)}, f32[384,512]{1,0:T(8,128)S(1)}) custom-call(s32[3]{0:T(128)S(1)} %pad_add_fusion.place, bf16[768,3584]{1,0:T(8,128)(2,1)S(1)} %bitcast.16, bf16[7168,512]{1,0:T(8,128)(2,1)} %bitcast.20, bf16[7168,512]{1,0:T(8,128)(2,1)} %bitcast.23, bf16[512,7168]{1,0:T(8,128)(2,1)} %bitcast.26), custom_call_target="tpu_custom_call" | custom-call | tf_op jit(solution)/shard_map/project/pallas_call | solution.py:254
  90.8 1.3 collective-permute-done.rows
  92.0 14.2 %expert.1 = (bf16[768,1152]{1,0:T(8,128)(2,1)S(1)}, bf16[768,1152]{1,0:T(8,128)(2,1)S(1)}, bf16[384,512]{1,0:T(8,128)(2,1)S(1)}, bf16[384,512]{1,0:T(8,128)(2,1)S(1)}) custom-call(s32[3]{0:T(128)S(1)} %pad_add_fusion.place, bf16[768,3584]{1,0:T(8,128)(2,1)S(1)} %collective-permute-done.rows, bf16[7168,512]{1,0:T(8,128)(2,1)} %bitcast.21, ...), custom_call_target="tpu_custom_call" | custom-call | tf_op jit(solution)/shard_map/expert/pallas_call | solution.py:337
  106.3 0.4 collective-permute-start.1
  106.7 6.4 %rest.1 = (bf16[768,768]{1,0:T(8,128)(2,1)}, bf16[768,768]{1,0:T(8,128)(2,1)S(1)}) custom-call(s32[3]{0:T(128)S(1)} %pad_add_fusion.place, bf16[384,512]{1,0:T(8,128)(2,1)S(1)} %get-tuple-element.30.grad_gate, bf16[384,512]{1,0:T(8,128)(2,1)S(1)} %get-tuple-element.31.grad_up, bf16[7168,512]{1,0:T(8,128)(2,1)} %bitcast.22, bf16[7168,512]{1,0:T(8,128)(2,1)} %bitcast.25), custom_call_target="tpu_custom_call" | custom-call | tf_op jit(solution)/shard_map/rest/pallas_call | solution.py:400
  113.1 0.5 collective-permute-start.2
  113.6 1.7 add_convert_fusion
  115.2 4.0 %all-to-all-start.1 = ((bf16[32,24,1152]{2,1,0:T(8,128)(2,1)}), bf16[32,24,1152]{2,1,0:T(8,128)(2,1)S(1)}, u32[]{:S(2)}, u32[]{:S(2)}) async-start(bf16[32,24,1152]{2,1,0:T(8,128)(2,1)} %bitcast.28), calls=%async_computation.1 | async-start | bytes 3538944 | tf_op jit(solution)/shard_map/all_to_all | solution.py:55
  119.2 0.0 collective-permute-done.2
  119.2 1.5 convert_add_fusion
  120.7 0.1 slice.15
  120.8 2.8 %collective-permute-start.3 = (bf16[768,384]{1,0:T(8,128)(2,1)S(1)}, bf16[768,384]{1,0:T(8,128)(2,1)S(1)}, u32[]{:S(2)}, u32[]{:S(2)}) collective-permute-start(bf16[768,384]{1,0:T(8,128)(2,1)S(1)} %slice.15), channel_id=1, source_target_pairs={{0,64},{64,0},{32,96},{96,32},{1,65},{65,1},{33,97},{97,33},{2,66}... | collective-permute-start | bytes 1769480 | tf_op jit(solution)/shard_map/ppermute | solution.py:49
  123.6 31.0 %collective-permute-done.3 = bf16[768,384]{1,0:T(8,128)(2,1)S(1)} collective-permute-done((bf16[768,384]{1,0:T(8,128)(2,1)S(1)}, bf16[768,384]{1,0:T(8,128)(2,1)S(1)}, u32[]{:S(2)}, u32[]{:S(2)}) %collective-permute-start.3) | collective-permute-done | bytes 589856 | tf_op jit(solution)/shard_map/ppermute | solution.py:49
  154.6 1.0 fusion
  155.6 7.5 %all-to-all-start.2 = ((bf16[32,24,384]{2,1,0:T(8,128)(2,1)}), bf16[32,24,384]{2,1,0:T(8,128)(2,1)S(1)}, u32[]{:S(2)}, u32[]{:S(2)}) async-start(bf16[32,24,384]{2,1,0:T(8,128)(2,1)} %bitcast.13), calls=%async_computation.2 | async-start | bytes 1179648 | tf_op jit(solution)/shard_map/all_to_all | solution.py:55
  163.0 2.0 %combine.1 = (f32[128,1152]{1,0:T(8,128)S(1)}, bf16[128,1152]{1,0:T(8,128)(2,1)S(1)}) custom-call(s32[3]{0:T(128)S(1)} %pad_add_fusion.place, bf16[256,768]{1,0:T(8,128)(2,1)S(1)} %gather_matrix.1.gather, bf16[768,1152]{1,0:T(8,128)(2,1)S(1)} %bitcast.17), custom_call_target="tpu_custom_call" | custom-call | tf_op jit(solution)/shard_map/combine/pallas_call | solution.py:435
  165.0 2.1 %collective-permute-start.4 = (bf16[128,1152]{1,0:T(8,128)(2,1)S(1)}, bf16[128,1152]{1,0:T(8,128)(2,1)S(1)}, u32[]{:S(2)}, u32[]{:S(2)}) collective-permute-start(bf16[128,1152]{1,0:T(8,128)(2,1)S(1)} %get-tuple-element.37), channel_id=1, source_target_pairs={{0,64},{64,0},{32,96},{96,32},{1,65},{65,1},{33,97},{97,33},{2,66}... | collective-permute-start | bytes 884744 | tf_op jit(solution)/shard_map/ppermute | solution.py:49
  167.1 10.4 %collective-permute-done.4.arrived = bf16[128,1152]{1,0:T(8,128)(2,1)S(1)} collective-permute-done((bf16[128,1152]{1,0:T(8,128)(2,1)S(1)}, bf16[128,1152]{1,0:T(8,128)(2,1)S(1)}, u32[]{:S(2)}, u32[]{:S(2)}) %collective-permute-start.4) | collective-permute-done | bytes 294944 | tf_op jit(solution)/shard_map/ppermute | solution.py:49
  177.5 3.0 %final.1 = bf16[128,1792]{1,0:T(8,128)(2,1)} custom-call(s32[3]{0:T(128)S(1)} %pad_add_fusion.place, bf16[256,768]{1,0:T(8,128)(2,1)S(1)} %gather_matrix.1.gather, bf16[768,384]{1,0:T(8,128)(2,1)S(1)} %bitcast.19, f32[128,1152]{1,0:T(8,128)S(1)} %get-tuple-element.36.kept, bf16[128,1152]{1,0:T(8,128)(2,1)S(1)} %collective-permute-done.4.arrived, ...), custom_call_target="tpu_custom_call" | custom-call | tf_op jit(solution)/shard_map/final/pallas_call | solution.py:472
  (3 shorter events, 0.0 us)
Async XLA Ops:
  83.0 9.0 %collective-permute-start = (bf16[768,3584]{1,0:T(8,128)(2,1)S(1)}, bf16[768,3584]{1,0:T(8,128)(2,1)S(1)}, u32[]{:S(2)}, u32[]{:S(2)}) collective-permute-start(bf16[768,3584]{1,0:T(8,128)(2,1)S(1)} %bitcast.15), channel_id=1, source_target_pairs={{0,32},{32,0},{64,96},{96,64},{1,33},{33,1},{65,97},{97,65},{2,34}... | collective-permute-start | bytes 16515080 | tf_op jit(solution)/shard_map/ppermute | solution.py:45
  106.3 7.3 %collective-permute-start.1 = (bf16[768,1152]{1,0:T(8,128)(2,1)S(1)}, bf16[768,1152]{1,0:T(8,128)(2,1)S(1)}, u32[]{:S(2)}, u32[]{:S(2)}) collective-permute-start(bf16[768,1152]{1,0:T(8,128)(2,1)S(1)} %get-tuple-element.29), channel_id=1, source_target_pairs={{0,32},{32,0},{64,96},{96,64},{1,33},{33,1},{65,97},{97,65},{2,34}... | collective-permute-start | bytes 5308424 | tf_op jit(solution)/shard_map/ppermute | solution.py:45
  113.1 6.1 %collective-permute-start.2 = (bf16[768,768]{1,0:T(8,128)(2,1)}, bf16[768,768]{1,0:T(8,128)(2,1)}, u32[]{:S(2)}, u32[]{:S(2)}) collective-permute-start(bf16[768,768]{1,0:T(8,128)(2,1)} %get-tuple-element.33), channel_id=1, source_target_pairs={{0,32},{32,0},{64,96},{96,64},{1,33},{33,1},{65,97},{97,65},{2,34}... | collective-permute-start | bytes 3538952 | tf_op jit(solution)/shard_map/ppermute | solution.py:45
  115.2 40.3 %all-to-all-start.1 = ((bf16[32,24,1152]{2,1,0:T(8,128)(2,1)}), bf16[32,24,1152]{2,1,0:T(8,128)(2,1)S(1)}, u32[]{:S(2)}, u32[]{:S(2)}) async-start(bf16[32,24,1152]{2,1,0:T(8,128)(2,1)} %bitcast.28), calls=%async_computation.1 | async-start | bytes 3538944 | tf_op jit(solution)/shard_map/all_to_all | solution.py:55
  120.8 33.8 %collective-permute-start.3 = (bf16[768,384]{1,0:T(8,128)(2,1)S(1)}, bf16[768,384]{1,0:T(8,128)(2,1)S(1)}, u32[]{:S(2)}, u32[]{:S(2)}) collective-permute-start(bf16[768,384]{1,0:T(8,128)(2,1)S(1)} %slice.15), channel_id=1, source_target_pairs={{0,64},{64,0},{32,96},{96,32},{1,65},{65,1},{33,97},{97,33},{2,66}... | collective-permute-start | bytes 1769480 | tf_op jit(solution)/shard_map/ppermute | solution.py:49
  155.6 22.0 %all-to-all-start.2 = ((bf16[32,24,384]{2,1,0:T(8,128)(2,1)}), bf16[32,24,384]{2,1,0:T(8,128)(2,1)S(1)}, u32[]{:S(2)}, u32[]{:S(2)}) async-start(bf16[32,24,384]{2,1,0:T(8,128)(2,1)} %bitcast.13), calls=%async_computation.2 | async-start | bytes 1179648 | tf_op jit(solution)/shard_map/all_to_all | solution.py:55
  165.0 12.5 %collective-permute-start.4 = (bf16[128,1152]{1,0:T(8,128)(2,1)S(1)}, bf16[128,1152]{1,0:T(8,128)(2,1)S(1)}, u32[]{:S(2)}, u32[]{:S(2)}) collective-permute-start(bf16[128,1152]{1,0:T(8,128)(2,1)S(1)} %get-tuple-element.37), channel_id=1, source_target_pairs={{0,64},{64,0},{32,96},{96,32},{1,65},{65,1},{33,97},{97,33},{2,66}... | collective-permute-start | bytes 884744 | tf_op jit(solution)/shard_map/ppermute | solution.py:49

commit v5 on v4

--- a/solution.py
+++ b/solution.py
@@ -17,7 +17,6 @@
 BACK = 512
 DIRECT = 1024
 LANES = 128
-SMALL = pl.CostEstimate(flops=0, bytes_accessed=0, transcendentals=0)
 LAST = (((1,), (1,)), ((), ()))
 CORE_SWAP = [(0, 1), (1, 0), (2, 3), (3, 2)]
 HIGH_SWAP = [(0, 2), (2, 0), (1, 3), (3, 1)]
@@ -271,7 +270,7 @@
     )(place, rows, gate, up, down)
 
 
-def expert_kernel(place, rows, gate, up, down, in_gate, in_up, in_hidden, theirs, mine, grad_gate, grad_up, gate_in, up_in, down_in, acc_gate, acc_up, acc_hidden, out, sems, more_sems, out_sems):
+def expert_kernel(place, rows, gate, up, down, in_gate, in_up, in_hidden, theirs, mine, grad_gate, grad_up, product, gate_in, up_in, down_in, acc_gate, acc_up, acc_hidden, out, sems, more_sems, out_sems):
     half = rows.shape[1]
     core = place[0]
     side = 1 - core
@@ -299,27 +298,24 @@
     sigma = jax.nn.sigmoid(pre_gate)
     to_gate = hidden * pre_up * sigma * (1.0 + pre_gate * (1.0 - sigma))
     to_up = hidden * pre_gate * sigma
-    product = jnp.sum(to_gate * pre_gate + to_up * pre_up, axis=1, keepdims=True)
-    product = jnp.broadcast_to(product, (product.shape[0], LANES))
-    product = interleave(product, product).astype(BF16)
+    total = jnp.sum(to_gate * pre_gate + to_up * pre_up, axis=1, keepdims=True)
+    product[...] = jnp.broadcast_to(total, product.shape)
     grad_gate[...] = to_gate.astype(BF16)
     grad_up[...] = to_up.astype(BF16)
     for copy in rest:
         wait_all(copy)
 
     columns = gate.shape[0] // 4
-
-    def one(start):
-        at = pl.ds(pl.multiple_of(start, LANES), BACK)
-        total = lax.dot_general(grad_gate[...], gate_in[at, :], LAST, preferred_element_type=F32)
-        return total + lax.dot_general(grad_up[...], up_in[at, :], LAST, preferred_element_type=F32)
-
+    width = columns - DIRECT
+    part = width // 2
     sent = []
     for slot, (to, whose) in enumerate(((theirs, side), (mine, core))):
-        for at in range(0, DIRECT, BACK):
-            low, high = one(whose * columns + at), one((2 + whose) * columns + at)
-            out[slot, :, at : at + BACK] = interleave(low, high).astype(BF16)
-        out[slot, :, DIRECT:] = product
+        for turn, high in enumerate((place[1], 1 - place[1])):
+            at = pl.ds(pl.multiple_of((2 * high + whose) * columns + DIRECT, LANES), width)
+            rows_out = lax.dot_general(grad_gate[...], gate_in[at, :], LAST, preferred_element_type=F32)
+            rows_out = rows_out + lax.dot_general(grad_up[...], up_in[at, :], LAST, preferred_element_type=F32)
+            rows_out = interleave(rows_out[:, :part], rows_out[:, part:]).astype(BF16)
+            out[slot, :, turn * part : (turn + 1) * part] = rows_out
         copy = pltpu.make_async_copy(out.at[slot], to, out_sems.at[slot])
         copy.start()
         sent.append(copy)
@@ -331,16 +327,17 @@
     height, half = rows.shape
     width, hidden = gate.shape
     any_space = pl.BlockSpec(memory_space=pl.ANY)
-    message = jax.ShapeDtypeStruct((height, DIRECT + LANES), BF16)
+    message = jax.ShapeDtypeStruct((height, width // 4 - DIRECT), BF16)
     acc = accs[0].shape
     grad = jax.ShapeDtypeStruct(acc, BF16)
+    product = jax.ShapeDtypeStruct((acc[0], LANES), F32)
     return pl.pallas_call(
         expert_kernel,
-        out_shape=(message, message, grad, grad),
+        out_shape=(message, message, grad, grad, product),
         grid_spec=grid_of(
             (1,),
             [pl.BlockSpec(memory_space=pltpu.VMEM)] + [any_space] * 3 + [whole(acc)] * 3,
-            (any_space, any_space, whole(acc), whole(acc)),
+            (any_space, any_space, whole(acc), whole(acc), whole(product.shape)),
             [
                 pltpu.VMEM((width, hidden), BF16),
                 pltpu.VMEM((width, hidden), BF16),
@@ -359,16 +356,14 @@
     )(place, rows, gate, up, down, *accs)
 
 
-def rest_kernel(place, grad_gate, grad_up, gate, up, theirs, mine, gate_in, up_in, out, sems, out_sems):
+def direct_kernel(place, grad_gate, grad_up, product, gate, up, theirs, mine, gate_in, up_in, out, sems, out_sems):
     columns = gate.shape[0] // 4
-    core, high = place[0], place[1]
-    width = columns - DIRECT
-    half = width // 2
+    core = place[0]
     copies = []
     for slot, whose in enumerate((1 - core, core)):
-        for turn, part in enumerate((high, 1 - high)):
-            at = pl.ds(pl.multiple_of((2 * part + whose) * columns + DIRECT, 256), width)
-            to = 2 * slot + turn
+        for high in range(2):
+            at = pl.ds(pl.multiple_of((2 * high + whose) * columns, 256), DIRECT)
+            to = 2 * slot + high
             copies.append(
                 [
                     pltpu.make_async_copy(gate.at[at, :], gate_in.at[to], sems.at[to, 0]),
@@ -377,45 +372,72 @@
             )
     for copy in copies:
         start_all(copy)
+    products = interleave(product[...], product[...]).astype(BF16)
+
+    def one(index, at):
+        part = slice(at, at + BACK)
+        total = lax.dot_general(grad_gate[...], gate_in[index, part, :], LAST, preferred_element_type=F32)
+        return total + lax.dot_general(grad_up[...], up_in[index, part, :], LAST, preferred_element_type=F32)
+
     sent = []
     for slot, to in enumerate((theirs, mine)):
-        for turn in range(2):
-            at = 2 * slot + turn
-            wait_all(copies[at])
-            rows = lax.dot_general(grad_gate[...], gate_in[at], LAST, preferred_element_type=F32)
-            rows = rows + lax.dot_general(grad_up[...], up_in[at], LAST, preferred_element_type=F32)
-            out[slot, :, turn * half : (turn + 1) * half] = interleave(rows[:, :half], rows[:, half:]).astype(BF16)
+        wait_all(copies[2 * slot])
+        wait_all(copies[2 * slot + 1])
+        for at in range(0, DIRECT, BACK):
+            rows = interleave(one(2 * slot, at), one(2 * slot + 1, at))
+            out[slot, :, at : at + BACK] = rows.astype(BF16)
+        out[slot, :, DIRECT:] = products
         copy = pltpu.make_async_copy(out.at[slot], to, out_sems.at[slot])
         copy.start()
         sent.append(copy)
     wait_all(sent)
 
 
-def rest(place, grads, weights):
+def direct_rows(place, grads, product, weights):
     gate, up, _ = weights
     rows, hidden = grads[0].shape
-    width = gate.shape[0] // 4 - DIRECT
     any_space = pl.BlockSpec(memory_space=pl.ANY)
-    message = jax.ShapeDtypeStruct((2 * rows, width), BF16)
-    return pl.pallas_call(
-        rest_kernel,
+    message = jax.ShapeDtypeStruct((2 * rows, DIRECT + LANES), BF16)
+    return pl.pallas_call(
+        direct_kernel,
         out_shape=(message, message),
         grid_spec=grid_of(
             (1,),
-            [whole((rows, hidden))] * 2 + [any_space] * 2,
+            [whole((rows, hidden))] * 2 + [whole(product.shape)] + [any_space] * 2,
             (any_space, any_space),
             [
-                pltpu.VMEM((4, width, hidden), BF16),
-                pltpu.VMEM((4, width, hidden), BF16),
+                pltpu.VMEM((4, DIRECT, hidden), BF16),
+                pltpu.VMEM((4, DIRECT, hidden), BF16),
                 pltpu.VMEM((2,) + message.shape, BF16),
                 pltpu.SemaphoreType.DMA((4, 2)),
                 pltpu.SemaphoreType.DMA((2,)),
             ],
         ),
-        compiler_params=params(24),
-        cost_estimate=SMALL,
-        name="rest",
-    )(place, *grads, gate, up)
+        compiler_params=params(32),
+        name="direct_rows",
+    )(place, *grads, product, gate, up)
+
+
+def merge_kernel(mine, other, kept, arrived, out):
+    columns = mine.shape[1]
+    out[:, :columns] = (mine[...].astype(F32) + other[...].astype(F32)).astype(BF16)
+    out[:, columns:] = (kept[...] + arrived[...].astype(F32)).astype(BF16)
+
+
+def merge(mine, other, kept, arrived):
+    rows = mine.shape[0]
+    block = rows // 4
+    columns = mine.shape[1] + kept.shape[1]
+    spec = lambda array: pl.BlockSpec((block, array.shape[1]), lambda i: (i, 0))
+    return pl.pallas_call(
+        merge_kernel,
+        out_shape=jax.ShapeDtypeStruct((rows, columns), BF16),
+        grid=(4,),
+        in_specs=[spec(array) for array in (mine, other, kept, arrived)],
+        out_specs=pl.BlockSpec((block, columns), lambda i: (i, 0)),
+        compiler_params=params(12),
+        name="merge",
+    )(mine, other, kept, arrived)
 
 
 def combine_kernel(place, gather, rows, first, second):
@@ -429,7 +451,7 @@
 
 def combine(place, gather, rows):
     count = gather.shape[0] // 2
-    columns = rows.shape[1]
+    columns = DIRECT + LANES
     part = columns // 3
     block = pl.BlockSpec((count, part), lambda i, place: (0, i))
     return pl.pallas_call(
@@ -468,13 +490,19 @@
 def final(place, gather, rows, kept, arrived, tokens, cotangent, gain, inverse):
     count, width = tokens.shape
     columns = width // 4
+    half = (columns - DIRECT) // 2
     quarter = lambda height: pl.BlockSpec((height, columns), lambda i, place: (0, place[2]))
     return pl.pallas_call(
         functools.partial(final_kernel, width),
         out_shape=jax.ShapeDtypeStruct((count, columns), BF16),
         grid_spec=grid_of(
             (1,),
-            [whole(array.shape) for array in (gather, rows, kept, arrived)]
+            [
+                whole(gather.shape),
+                pl.BlockSpec((rows.shape[0], half), lambda i, place: (0, (DIRECT + LANES) // half)),
+                whole(kept.shape),
+                whole(arrived.shape),
+            ]
             + [quarter(count), quarter(count), quarter(1), whole(inverse.shape)],
             whole((count, columns)),
         ),
@@ -501,18 +529,17 @@
     rows, gather = lax.optimization_barrier((rows, gather))
     rows = exchange(rows)
     accs = project(place, rows, weights)
-    theirs, mine, *grads = expert(place, core_swap(rows), weights, accs)
-    direct = (mine.astype(F32) + core_swap(theirs).astype(F32)).astype(BF16)
-
-    theirs, mine = rest(place, grads, weights)
+    theirs, mine, *grads, product = expert(place, core_swap(rows), weights, accs)
     summed = mine.astype(F32) + core_swap(theirs).astype(F32)
     half = summed.shape[1] // 2
-    summed = summed[:, :half] + high_swap(summed[:, half:].astype(BF16)).astype(F32)
-    direct = exchange(direct)
-    direct, summed = lax.optimization_barrier((direct, summed.astype(BF16)))
-    kept, sent = combine(place, gather, direct)
+    kept, sent = summed[:, :half], summed[:, half:].astype(BF16)
+    kept, sent, product, *grads = lax.optimization_barrier((kept, sent, product, *grads))
     arrived = high_swap(sent)
-    return final(place, gather, exchange(summed), kept, arrived, tokens, cotangent, gain, inverse)
+    theirs, mine = direct_rows(place, grads, product, weights)
+    theirs, arrived = lax.optimization_barrier((theirs, arrived))
+    back = exchange(merge(mine, core_swap(theirs), kept, arrived))
+    kept, sent = combine(place, gather, back)
+    return final(place, gather, back, kept, high_swap(sent), tokens, cotangent, gain, inverse)
 
 
 def solution(mesh):

time: 181 us -> 179 us (0.989)
  blocking collectives: 74.7 us -> 110 us
  waiting for transfers between devices: 42.7 us -> 20.4 us
  starting transfers between devices: 17.3 us -> 6.07 us
  other arithmetic: 4.22 us -> 0.32 us
    all_to_all x1 -> x2, blocking collectives: 74.7 us -> 110 us  [exchange(): lax.all_to_all(shaped, 'expert', split_axis=0, concat_axis=0, tiled=True)]
    ppermute x2, waiting for transfers between devices: 41.4 us -> 12.7 us  [high_swap(): return lax.ppermute(array, 'pipe', HIGH_SWAP)]
    all_to_all x2 -> x0, starting transfers between devices: 11.5 us -> none  [exchange(): lax.all_to_all(shaped, 'expert', split_axis=0, concat_axis=0, tiled=True)]
    ppermute x3, waiting for transfers between devices: 1.3 us -> 7.71 us  [core_swap(): return lax.ppermute(array, 'pipe', CORE_SWAP)]
    convert_element_type x2 -> x0, other arithmetic: 2.64 us -> none  [the longest x1 1.68 us: body(): direct = (mine.astype(F32) + core_swap(theirs).astype(F32)).astype(BF16)]
    pallas_call x2 -> x3, Pallas kernels: 20.6 us -> 20.7 us  [the longest x1 12.8 us: expert(): pl.pallas_call(expert_kernel, out_shape=(message, message, grad, grad, pr...]
  transfers between devices with their start and end apart: 7 -> 5, of which waited for: 3 -> 5; matrix products, arithmetic and copies ran while one was open for 2% -> 0% of each run, Pallas kernels for 9% -> 8%
where the time goes in v5:
time: 179 us
  blocking collectives  110 us (61%)
  Pallas kernels  41.6 us (23%)
  waiting for transfers between devices  20.4 us (11%)
  starting transfers between devices  6.07 us (3%)
    all_to_all x2, blocking collectives, exchange(): lax.all_to_all(shaped, 'expert', split_axis=0, concat_axis=0, tiled=True)  110 us
    pallas_call x1, Pallas kernels, expert(): pl.pallas_call(expert_kernel, out_shape=(message, message, grad, grad, pr...  12.8 us
    ppermute x2, waiting for transfers between devices, high_swap(): return lax.ppermute(array, 'pipe', HIGH_SWAP)  12.7 us
    pallas_call x1, Pallas kernels, project(): pl.pallas_call(project_kernel, out_shape=(acc,) * 3, grid_spec=grid_of((1...  7.72 us
    ppermute x3, waiting for transfers between devices, core_swap(): return lax.ppermute(array, 'pipe', CORE_SWAP)  7.71 us
    pallas_call x1, Pallas kernels, direct_rows(): pl.pallas_call(direct_kernel, out_shape=(message, message), grid_spec=gri...  7.34 us
    pallas_call x1, Pallas kernels, make_message(): pl.pallas_call(functools.partial(message_kernel, capacity), out_shape=(ja...  7.19 us
    ppermute x2, starting transfers between devices, high_swap(): return lax.ppermute(array, 'pipe', HIGH_SWAP)  5.86 us
  transfers between devices with their start and end apart: 5, of which 5 were waited for; matrix products, arithmetic and copies ran while one was open for 0% of the time, Pallas kernels for 8%

profile of v5, /device:TPU:0, one launch (start us, length us, event | category | flops | bytes accessed | tf_op | source)
XLA Modules:
  0.0 178.8 jit_solution(14888125035414298166)
XLA Ops:
  0.0 1.0 gather_matrix.1.gather
  1.1 0.1 pad_add_fusion.place
  1.1 7.2 %message.1 = (bf16[768,3584]{1,0:T(8,128)(2,1)S(1)}, f32[128,1]{1,0:T(8,128)S(1)}) custom-call(s32[3]{0:T(128)S(1)} %pad_add_fusion.place, bf16[128,7168]{1,0:T(8,128)(2,1)} %tokens.3, bf16[128,7168]{1,0:T(8,128)(2,1)} %tokens.3, bf16[128,7168]{1,0:T(8,128)(2,1)} %cotangent.3, f32[1,7168]{1,0:T(1,128)} %bitcast.27, s32[2,128]{1,0:T(2,128)} %bitcast.30, ...), custom_call_target="tpu_custom_call" | custom-call | tf_op jit(solution)/shard_map/message/pallas_call | solution.py:99
  8.3 74.7 %all_to_all.10 = bf16[32,24,3584]{2,1,0:T(8,128)(2,1)S(1)} all-to-all(bf16[32,24,3584]{2,1,0:T(8,128)(2,1)S(1)} %bitcast.18), channel_id=1, replica_groups=mesh['pipe'=4,'expert'=32] {'expert'}, dimensions={0} | all-to-all | bytes 11010048 | tf_op jit(solution)/shard_map/all_to_all | solution.py:54
  83.0 0.0 collective-permute-start
  83.0 7.7 %project.1 = (f32[384,512]{1,0:T(8,128)S(1)}, f32[384,512]{1,0:T(8,128)S(1)}, f32[384,512]{1,0:T(8,128)S(1)}) custom-call(s32[3]{0:T(128)S(1)} %pad_add_fusion.place, bf16[768,3584]{1,0:T(8,128)(2,1)S(1)} %bitcast.14, bf16[7168,512]{1,0:T(8,128)(2,1)} %bitcast.19, bf16[7168,512]{1,0:T(8,128)(2,1)} %bitcast.22, bf16[512,7168]{1,0:T(8,128)(2,1)} %bitcast.25), custom_call_target="tpu_custom_call" | custom-call | tf_op jit(solution)/shard_map/project/pallas_call | solution.py:253
  90.7 1.3 collective-permute-done.rows
  92.0 12.8 %expert.1 = (bf16[768,768]{1,0:T(8,128)(2,1)S(1)}, bf16[768,768]{1,0:T(8,128)(2,1)S(1)}, bf16[384,512]{1,0:T(8,128)(2,1)S(1)}, bf16[384,512]{1,0:T(8,128)(2,1)S(1)}, f32[384,128]{1,0:T(8,128)S(1)}) custom-call(s32[3]{0:T(128)S(1)} %pad_add_fusion.place, bf16[768,3584]{1,0:T(8,128)(2,1)S(1)} %collective-permute-done.rows, bf16[7168,512]{1,0:T(8,128)(2,1)} %bitcast.20, ...), custom_call_target="tpu_custom_call" | custom-call | tf_op jit(solution)/shard_map/expert/pallas_call | solution.py:334
  104.8 0.2 collective-permute-start.1
  105.0 2.7 %collective-permute-done.1 = bf16[768,768]{1,0:T(8,128)(2,1)S(1)} collective-permute-done((bf16[768,768]{1,0:T(8,128)(2,1)S(1)}, bf16[768,768]{1,0:T(8,128)(2,1)S(1)}, u32[]{:S(2)}, u32[]{:S(2)}) %collective-permute-start.1) | collective-permute-done | bytes 1179680 | tf_op jit(solution)/shard_map/ppermute | solution.py:44
  107.8 0.2 convert_add_fusion
  108.0 0.1 slice.9.kept
  108.1 0.1 slice.12
  108.2 3.0 %collective-permute-start.2 = (bf16[768,384]{1,0:T(8,128)(2,1)S(1)}, bf16[768,384]{1,0:T(8,128)(2,1)S(1)}, u32[]{:S(2)}, u32[]{:S(2)}) collective-permute-start(bf16[768,384]{1,0:T(8,128)(2,1)S(1)} %slice.12), channel_id=1, source_target_pairs={{0,64},{64,0},{32,96},{96,32},{1,65},{65,1},{33,97},{97,33},{2,66}... | collective-permute-start | bytes 1769480 | tf_op jit(solution)/shard_map/ppermute | solution.py:48
  111.2 7.3 %direct_rows.1 = (bf16[768,1152]{1,0:T(8,128)(2,1)S(1)}, bf16[768,1152]{1,0:T(8,128)(2,1)S(1)}) custom-call(s32[3]{0:T(128)S(1)} %pad_add_fusion.place, bf16[384,512]{1,0:T(8,128)(2,1)S(1)} %get-tuple-element.39.grad_gate, bf16[384,512]{1,0:T(8,128)(2,1)S(1)} %get-tuple-element.40.grad_up, f32[384,128]{1,0:T(8,128)S(1)} %get-tuple-element.41.product, ...), custom_call_target="tpu_custom_call" | custom-call | tf_op jit(solution)/shard_map/direct_rows/pallas_call | solution.py:401
  118.6 6.8 %collective-permute-done.2.arrived = bf16[768,384]{1,0:T(8,128)(2,1)S(1)} collective-permute-done((bf16[768,384]{1,0:T(8,128)(2,1)S(1)}, bf16[768,384]{1,0:T(8,128)(2,1)S(1)}, u32[]{:S(2)}, u32[]{:S(2)}) %collective-permute-start.2) | collective-permute-done | bytes 589856 | tf_op jit(solution)/shard_map/ppermute | solution.py:48
  125.3 0.0 collective-permute-start.3
  125.3 3.7 %collective-permute-done.3.other = bf16[768,1152]{1,0:T(8,128)(2,1)S(1)} collective-permute-done((bf16[768,1152]{1,0:T(8,128)(2,1)S(1)}, bf16[768,1152]{1,0:T(8,128)(2,1)S(1)}, u32[]{:S(2)}, u32[]{:S(2)}) %collective-permute-start.3) | collective-permute-done | bytes 1769504 | tf_op jit(solution)/shard_map/ppermute | solution.py:44
  129.0 0.6 merge.1
  129.6 35.4 %all_to_all.11 = bf16[32,24,1536]{2,1,0:T(8,128)(2,1)S(1)} all-to-all(bf16[32,24,1536]{2,1,0:T(8,128)(2,1)S(1)} %bitcast.17), channel_id=1, replica_groups=mesh['pipe'=4,'expert'=32] {'expert'}, dimensions={0} | all-to-all | bytes 4718592 | tf_op jit(solution)/shard_map/all_to_all | solution.py:54
  165.0 2.0 %combine.1 = (f32[128,1152]{1,0:T(8,128)S(1)}, bf16[128,1152]{1,0:T(8,128)(2,1)S(1)}) custom-call(s32[3]{0:T(128)S(1)} %pad_add_fusion.place, bf16[256,768]{1,0:T(8,128)(2,1)S(1)} %gather_matrix.1.gather, bf16[768,1536]{1,0:T(8,128)(2,1)S(1)} %bitcast.15), custom_call_target="tpu_custom_call" | custom-call | tf_op jit(solution)/shard_map/combine/pallas_call | solution.py:457
  167.0 2.8 %collective-permute-start.4 = (bf16[128,1152]{1,0:T(8,128)(2,1)S(1)}, bf16[128,1152]{1,0:T(8,128)(2,1)S(1)}, u32[]{:S(2)}, u32[]{:S(2)}) collective-permute-start(bf16[128,1152]{1,0:T(8,128)(2,1)S(1)} %get-tuple-element.49), channel_id=1, source_target_pairs={{0,64},{64,0},{32,96},{96,32},{1,65},{65,1},{33,97},{97,33},{2,66}... | collective-permute-start | bytes 884744 | tf_op jit(solution)/shard_map/ppermute | solution.py:48
  169.8 5.9 %collective-permute-done.4.arrived = bf16[128,1152]{1,0:T(8,128)(2,1)S(1)} collective-permute-done((bf16[128,1152]{1,0:T(8,128)(2,1)S(1)}, bf16[128,1152]{1,0:T(8,128)(2,1)S(1)}, u32[]{:S(2)}, u32[]{:S(2)}) %collective-permute-start.4) | collective-permute-done | bytes 294944 | tf_op jit(solution)/shard_map/ppermute | solution.py:48
  175.8 3.0 %final.1 = bf16[128,1792]{1,0:T(8,128)(2,1)} custom-call(s32[3]{0:T(128)S(1)} %pad_add_fusion.place, bf16[256,768]{1,0:T(8,128)(2,1)S(1)} %gather_matrix.1.gather, bf16[768,1536]{1,0:T(8,128)(2,1)S(1)} %bitcast.16, f32[128,1152]{1,0:T(8,128)S(1)} %get-tuple-element.48.kept, bf16[128,1152]{1,0:T(8,128)(2,1)S(1)} %collective-permute-done.4.arrived, ...), custom_call_target="tpu_custom_call" | custom-call | tf_op jit(solution)/shard_map/final/pallas_call | solution.py:495
Async XLA Ops:
  83.0 9.0 %collective-permute-start = (bf16[768,3584]{1,0:T(8,128)(2,1)S(1)}, bf16[768,3584]{1,0:T(8,128)(2,1)S(1)}, u32[]{:S(2)}, u32[]{:S(2)}) collective-permute-start(bf16[768,3584]{1,0:T(8,128)(2,1)S(1)} %bitcast.13), channel_id=1, source_target_pairs={{0,32},{32,0},{64,96},{96,64},{1,33},{33,1},{65,97},{97,65},{2,34}... | collective-permute-start | bytes 16515080 | tf_op jit(solution)/shard_map/ppermute | solution.py:44
  104.8 2.9 %collective-permute-start.1 = (bf16[768,768]{1,0:T(8,128)(2,1)S(1)}, bf16[768,768]{1,0:T(8,128)(2,1)S(1)}, u32[]{:S(2)}, u32[]{:S(2)}) collective-permute-start(bf16[768,768]{1,0:T(8,128)(2,1)S(1)} %get-tuple-element.35), channel_id=1, source_target_pairs={{0,32},{32,0},{64,96},{96,64},{1,33},{33,1},{65,97},{97,65},{2,34}... | collective-permute-start | bytes 3538952 | tf_op jit(solution)/shard_map/ppermute | solution.py:44
  108.2 17.2 %collective-permute-start.2 = (bf16[768,384]{1,0:T(8,128)(2,1)S(1)}, bf16[768,384]{1,0:T(8,128)(2,1)S(1)}, u32[]{:S(2)}, u32[]{:S(2)}) collective-permute-start(bf16[768,384]{1,0:T(8,128)(2,1)S(1)} %slice.12), channel_id=1, source_target_pairs={{0,64},{64,0},{32,96},{96,32},{1,65},{65,1},{33,97},{97,33},{2,66}... | collective-permute-start | bytes 1769480 | tf_op jit(solution)/shard_map/ppermute | solution.py:48
  125.3 3.7 %collective-permute-start.3 = (bf16[768,1152]{1,0:T(8,128)(2,1)S(1)}, bf16[768,1152]{1,0:T(8,128)(2,1)S(1)}, u32[]{:S(2)}, u32[]{:S(2)}) collective-permute-start(bf16[768,1152]{1,0:T(8,128)(2,1)S(1)} %get-tuple-element.45), channel_id=1, source_target_pairs={{0,32},{32,0},{64,96},{96,64},{1,33},{33,1},{65,97},{97,65},{2,34}... | collective-permute-start | bytes 5308424 | tf_op jit(solution)/shard_map/ppermute | solution.py:44
  167.0 8.8 %collective-permute-start.4 = (bf16[128,1152]{1,0:T(8,128)(2,1)S(1)}, bf16[128,1152]{1,0:T(8,128)(2,1)S(1)}, u32[]{:S(2)}, u32[]{:S(2)}) collective-permute-start(bf16[128,1152]{1,0:T(8,128)(2,1)S(1)} %get-tuple-element.49), channel_id=1, source_target_pairs={{0,64},{64,0},{32,96},{96,32},{1,65},{65,1},{33,97},{97,33},{2,66}... | collective-permute-start | bytes 884744 | tf_op jit(solution)/shard_map/ppermute | solution.py:48

commit v6 on v3

v6 whole, which is shorter than its diff:
```python
import functools

import jax
import jax.numpy as jnp
from jax import lax
from jax.experimental import pallas as pl
from jax.experimental.pallas import tpu as pltpu
from jax.sharding import PartitionSpec as P

EPSILON = 1e-06
BF16 = jnp.bfloat16
F32 = jnp.float32
MIB = 1024 * 1024
FILL = 1792
DEPTH = 1792
BACK = 896
LANES = 128
LAST = (((1,), (1,)), ((), ()))
CORE_SWAP = [(0, 1), (1, 0), (2, 3), (3, 2)]
HIGH_SWAP = [(0, 2), (2, 0), (1, 3), (3, 1)]


def params(mebibytes):
    return pltpu.CompilerParams(vmem_limit_bytes=mebibytes * MIB)


def in_hbm(array):
    return pltpu.with_memory_space_constraint(array, pltpu.HBM)


def whole(shape):
    return pl.BlockSpec(shape, lambda *_: (0,) * len(shape))


def grid_of(grid, in_specs, out_specs, scratch=()):
    return pltpu.PrefetchScalarGridSpec(
        num_scalar_prefetch=1, grid=grid, in_specs=in_specs, out_specs=out_specs, scratch_shapes=scratch
    )


def core_swap(array):
    return lax.ppermute(array, "pipe", CORE_SWAP)


def high_swap(array):
    return lax.ppermute(array, "pipe", HIGH_SWAP)


def exchange(rows):
    experts = lax.axis_size("expert")
    shaped = rows.reshape(experts, rows.shape[0] // experts, rows.shape[1])
    return lax.all_to_all(shaped, "expert", split_axis=0, concat_axis=0, tiled=True).reshape(rows.shape)


def message_kernel(capacity, place, all_tokens, tokens, cotangent, gain, ids, weights, rows, inverse, select, factors):
    top, count = ids.shape

    @pl.when(pl.program_id(0) == 0)
    def _():
        height = select.shape[0]
        experts = height // (2 * capacity)
        expert_of = lax.broadcasted_iota(jnp.int32, (experts, count), 0)
        earlier_of = lax.broadcasted_iota(jnp.int32, (count, count), 0)
        later_of = lax.broadcasted_iota(jnp.int32, (count, count), 1)
        before = (earlier_of < later_of).astype(F32).astype(BF16)
        row = lax.broadcasted_iota(jnp.int32, (height, count), 0)
        taken = jnp.zeros((experts, 1), F32)
        normed_part = jnp.zeros(row.shape, F32)
        for k in range(top):
            expert = ids[k : k + 1, :]
            named = (expert_of == expert).astype(F32)
            earlier = jnp.dot(named.astype(BF16), before, preferred_element_type=F32) + taken
            rank = jnp.sum(earlier * named, axis=0, keepdims=True).astype(jnp.int32)
            taken = taken + jnp.sum(named, axis=1, keepdims=True)
            at = expert * (2 * capacity) + rank
            normed_part = normed_part + (row == at).astype(F32)
            select[:, (k + 1) * count : (k + 2) * count] = (row == at + capacity).astype(F32).astype(BF16)
            column = jnp.sum(jnp.where(earlier_of == later_of, weights[k : k + 1, :], 0.0), axis=1, keepdims=True)
            factors[:, k : k + 1] = column
        select[:, :count] = normed_part.astype(BF16)
        values = all_tokens[...].astype(F32)
        inverse[...] = lax.rsqrt(jnp.mean(values * values, axis=1, keepdims=True) + EPSILON)

    normed = (tokens[...].astype(F32) * inverse[...] * gain[...]).astype(BF16)
    values = cotangent[...].astype(F32)
    parts = [normed] + [(factors[:, k : k + 1] * values).astype(BF16) for k in range(top)]
    rows[...] = jnp.dot(select[...], jnp.concatenate(parts, axis=0), preferred_element_type=F32).astype(BF16)


def make_message(place, tokens, cotangent, gain, ids, weights, capacity, experts):
    count, width = tokens.shape
    top = ids.shape[0]
    half = width // 2
    height = experts * 2 * capacity
    steps = half // FILL
    column = lambda i, place: (0, place[0] * steps + i)
    return pl.pallas_call(
        functools.partial(message_kernel, capacity),
        out_shape=(jax.ShapeDtypeStruct((height, half), BF16), jax.ShapeDtypeStruct((count, 1), F32)),
        grid_spec=grid_of(
            (steps,),
            [
                whole((count, width)),
                pl.BlockSpec((count, FILL), column),
                pl.BlockSpec((count, FILL), column),
                pl.BlockSpec((1, FILL), column),
                whole(ids.shape),
                whole(weights.shape),
            ],
            (pl.BlockSpec((height, FILL), lambda i, place: (0, i)), whole((count, 1))),
            [pltpu.VMEM((height, (top + 1) * count), BF16), pltpu.VMEM((count, top), F32)],
        ),
        compiler_params=params(32),
        name="message",
    )(place, tokens, tokens, cotangent, gain, ids, weights)


def gather_kernel(capacity, ids, out):
    top, count = ids.shape
    rows = out.shape[1]
    experts = rows // (2 * capacity)
    expert_of = lax.broadcasted_iota(jnp.int32, (experts, count), 0)
    earlier_of = lax.broadcasted_iota(jnp.int32, (count, count), 0)
    later_of = lax.broadcasted_iota(jnp.int32, (count, count), 1)
    before = (earlier_of < later_of).astype(F32).astype(BF16)
    row = lax.broadcasted_iota(jnp.int32, (count, rows), 1).astype(F32)
    taken = jnp.zeros((experts, 1), F32)
    first = jnp.zeros(row.shape, F32)
    second = jnp.zeros(row.shape, F32)
    for k in range(top):
        expert = ids[k : k + 1, :]
        named = (expert_of == expert).astype(F32)
        earlier = jnp.dot(named.astype(BF16), before, preferred_element_type=F32) + taken
        rank = jnp.sum(earlier * named, axis=0, keepdims=True)
        taken = taken + jnp.sum(named, axis=1, keepdims=True)
        at = expert.astype(F32) * (2 * capacity) + rank
        at = jnp.sum(jnp.where(earlier_of == later_of, at, 0.0), axis=1, keepdims=True)
        first = first + (row == at).astype(F32)
        second = second + (row == at + capacity).astype(F32)
    out[:count, :] = first.astype(BF16)
    out[count:, :] = second.astype(BF16)


def gather_matrix(ids, capacity, experts):
    count = ids.shape[1]
    return pl.pallas_call(
        functools.partial(gather_kernel, capacity),
        out_shape=jax.ShapeDtypeStruct((2 * count, experts * 2 * capacity), BF16),
        compiler_params=params(8),
        name="gather_matrix",
    )(ids)


def tiles(x, group):
    return x.reshape(x.shape[0] // (8 * group), group, 8, x.shape[1])


def upper(shape):
    return lax.broadcasted_iota(jnp.int32, shape, 1) < 4


def split_rows(x):
    rows, columns = x.shape
    x = x.astype(F32)
    a, b = tiles(x, 6), tiles(pltpu.roll(x, 4, 0), 6)
    top = upper((rows // 48, 8, columns))
    first = [a[:, 0], jnp.where(top, a[:, 1], b[:, 3]), b[:, 4]]
    second = [b[:, 2], jnp.where(top, b[:, 3], a[:, 4]), a[:, 5]]
    return [
        jnp.concatenate([p[:, None] for p in parts], axis=1).reshape(rows // 2, columns).astype(BF16)
        for parts in (first, second)
    ]


def interleave(x, y):
    rows, columns = x.shape
    x0, x1, x2 = tiles(x, 3), tiles(pltpu.roll(x, 4, 0), 3), tiles(pltpu.roll(x, rows - 4, 0), 3)
    y0, y1 = tiles(y, 3), tiles(pltpu.roll(y, 4, 0), 3)
    shape = (rows // 24, 8, columns)
    parts = [
        x0[:, 0],
        jnp.where(upper(shape), x0[:, 1], y1[:, 0]),
        y1[:, 1],
        x1[:, 2],
        jnp.where(upper(shape), x2[:, 2], y0[:, 1]),
        y0[:, 2],
    ]
    return jnp.concatenate([p[:, None] for p in parts], axis=1).reshape(2 * rows, columns)


def project_half(rows, gate, up, down, down_in, sems, side, accs, first):
    half = rows.shape[1]
    copies = []
    for i in range(half // DEPTH):
        at = pl.ds(pl.multiple_of(side * half + i * DEPTH, DEPTH), DEPTH)
        to = pl.ds(i * DEPTH, DEPTH)
        copies.append(pltpu.make_async_copy(down.at[:, at], down_in.at[:, to], sems.at[i]))
        copies[i].start()
    for i in range(half // DEPTH):
        at = pl.ds(pl.multiple_of(side * half + i * DEPTH, DEPTH), DEPTH)
        to = slice(i * DEPTH, (i + 1) * DEPTH)
        normed, routed = split_rows(rows[:, to])
        to_gate = jnp.dot(normed, gate[at, :], preferred_element_type=F32)
        to_up = jnp.dot(normed, up[at, :], preferred_element_type=F32)
        copies[i].wait()
        to_hidden = lax.dot_general(routed, down_in[:, to], LAST, preferred_element_type=F32)
        for acc, add in zip(accs, (to_gate, to_up, to_hidden)):
            acc[...] = add if first and i == 0 else acc[...] + add


def back_rows(place, side, grad_gate, grad_up, gate, up, out):
    columns = out.shape[1]

    def one(start):
        at = pl.ds(pl.multiple_of(start, LANES), BACK)
        total = lax.dot_general(grad_gate[...], gate[at, :], LAST, preferred_element_type=F32)
        return total + lax.dot_general(grad_up[...], up[at, :], LAST, preferred_element_type=F32)

    for at in range(0, columns, BACK):
        rows = interleave(one(side * columns + at), one((2 + side) * columns + at))
        out[:, at : at + BACK] = rows.astype(BF16)


def down_scratch(half, hidden):
    return [pltpu.VMEM((hidden, half), BF16), pltpu.SemaphoreType.DMA((half // DEPTH,))]


def project_kernel(place, rows, gate, up, down, acc_gate, acc_up, acc_hidden, down_in, sems):
    project_half(rows, gate, up, down, down_in, sems, place[0], (acc_gate, acc_up, acc_hidden), True)


def project(place, rows, weights):
    acc = jax.ShapeDtypeStruct((rows.shape[0] // 2, weights[0].shape[1]), F32)
    resident = pl.BlockSpec(memory_space=pltpu.VMEM)
    return pl.pallas_call(
        project_kernel,
        out_shape=(acc,) * 3,
        grid_spec=grid_of(
            (1,),
            [resident] * 3 + [pl.BlockSpec(memory_space=pl.ANY)],
            (resident,) * 3,
            down_scratch(rows.shape[1], acc.shape[1]),
        ),
        compiler_params=params(20),
        name="project",
    )(place, rows, *weights)


def expert_kernel(place, rows, gate, up, down, in_gate, in_up, in_hidden, theirs, grad_gate, grad_up, acc_gate, acc_up, acc_hidden, down_in, sems):
    side = 1 - place[0]
    accs = (acc_gate, acc_up, acc_hidden)
    for acc, value in zip(accs, (in_gate, in_up, in_hidden)):
        acc[...] = value[...]
    project_half(rows, gate, up, down, down_in, sems, side, accs, False)
    pre_gate, pre_up, hidden = acc_gate[...], acc_up[...], acc_hidden[...]
    sigma = jax.nn.sigmoid(pre_gate)
    grad_gate[...] = (hidden * pre_up * sigma * (1.0 + pre_gate * (1.0 - sigma))).astype(BF16)
    grad_up[...] = (hidden * pre_gate * sigma).astype(BF16)
    back_rows(place, side, grad_gate, grad_up, gate, up, theirs)


def expert(place, rows, weights, accs):
    height = rows.shape[0]
    acc = accs[0].shape
    grad = jax.ShapeDtypeStruct(acc, BF16)
    resident = pl.BlockSpec(memory_space=pltpu.VMEM)
    return pl.pallas_call(
        expert_kernel,
        out_shape=(jax.ShapeDtypeStruct((height, weights[0].shape[0] // 4), BF16), grad, grad),
        grid_spec=grid_of(
            (1,),
            [resident] * 3 + [pl.BlockSpec(memory_space=pl.ANY)] + [resident] * 3,
            (resident,) * 3,
            [pltpu.VMEM(acc, F32)] * 3 + down_scratch(rows.shape[1], acc[1]),
        ),
        compiler_params=params(24),
        name="expert",
    )(place, rows, *weights, *accs)


def mine_kernel(place, grad_gate, grad_up, gate, up, mine):
    back_rows(place, place[0], grad_gate, grad_up, gate, up, mine)


def mine_rows(place, grads, weights):
    gate, up, _ = weights
    resident = pl.BlockSpec(memory_space=pltpu.VMEM)
    return pl.pallas_call(
        mine_kernel,
        out_shape=jax.ShapeDtypeStruct((2 * grads[0].shape[0], gate.shape[0] // 4), BF16),
        grid_spec=grid_of((1,), [resident] * 4, resident),
        compiler_params=params(16),
        name="mine_rows",
    )(place, *grads, gate, up)


def merge_kernel(mine, other, out):
    out[...] = (mine[...].astype(F32) + other[...].astype(F32)).astype(BF16)


def merge(mine, other):
    rows, columns = mine.shape
    spec = pl.BlockSpec((rows // 4, columns), lambda i: (i, 0))
    return pl.pallas_call(
        merge_kernel,
        out_shape=jax.ShapeDtypeStruct((rows, columns), BF16),
        grid=(4,),
        in_specs=[spec, spec],
        out_specs=spec,
        compiler_params=params(12),
        name="merge",
    )(mine, other)


def combine_kernel(place, gather, rows, tokens_0, tokens_1, gain_0, gain_1, kept, sent, product):
    count = kept.shape[0]
    total = jnp.dot(gather[...], rows[...], preferred_element_type=F32)
    low, high = total[:count], total[count:]
    flip = place[1] == 1
    kept[...] = jnp.where(flip, high, low)
    sent[...] = jnp.where(flip, low, high).astype(BF16)
    part = low * (tokens_0[...].astype(F32) * gain_0[...]) + high * (tokens_1[...].astype(F32) * gain_1[...])
    part = jnp.broadcast_to(jnp.sum(part, axis=1, keepdims=True), product.shape)

    @pl.when(pl.program_id(0) == 0)
    def _():
        product[...] = part

    @pl.when(pl.program_id(0) > 0)
    def _():
        product[...] += part


def combine(place, gather, rows, tokens, gain):
    count = gather.shape[0] // 2
    height, columns = rows.shape
    steps = 2
    part = columns // steps
    block = pl.BlockSpec((count, part), lambda i, place: (0, i))

    def quarter(size, high):
        return pl.BlockSpec((size, part), lambda i, place: (0, (2 * high + place[0]) * steps + i))

    return pl.pallas_call(
        combine_kernel,
        out_shape=(
            jax.ShapeDtypeStruct((count, columns), F32),
            jax.ShapeDtypeStruct((count, columns), BF16),
            jax.ShapeDtypeStruct((count, LANES), F32),
        ),
        grid_spec=grid_of(
            (steps,),
            [
                whole(gather.shape),
                pl.BlockSpec((height, part), lambda i, place: (0, i)),
                quarter(count, 0),
                quarter(count, 1),
                quarter(1, 0),
                quarter(1, 1),
            ],
            (block, block, whole((count, LANES))),
        ),
        compiler_params=params(16),
        name="combine",
    )(place, gather, rows, tokens, tokens, gain, gain)


def final_kernel(width, place, kept, arrived, own_product, other_product, tokens, cotangent, gain, inverse, out):
    scale = inverse[...]
    row_product = own_product[:, :1] + other_product[:, :1]
    grad = kept[...] + arrived[...].astype(F32)
    value = cotangent[...].astype(F32) + scale * gain[...] * grad
    out[...] = (value - tokens[...].astype(F32) * (scale * scale * scale * row_product / width)).astype(BF16)


def final(place, kept, arrived, own_product, other_product, tokens, cotangent, gain, inverse):
    count, width = tokens.shape
    columns = width // 4
    quarter = lambda height: pl.BlockSpec((height, columns), lambda i, place: (0, place[2]))
    return pl.pallas_call(
        functools.partial(final_kernel, width),
        out_shape=jax.ShapeDtypeStruct((count, columns), BF16),
        grid_spec=grid_of(
            (1,),
            [whole(array.shape) for array in (kept, arrived, own_product, other_product)]
            + [quarter(count), quarter(count), quarter(1), whole(inverse.shape)],
            whole((count, columns)),
        ),
        compiler_params=params(16),
        name="final",
    )(place, kept, arrived, own_product, other_product, tokens, cotangent, gain, inverse)


def body(tokens, cotangent, norm_gain, expert_ids, gate_weights, w_gate, w_up, w_down):
    experts = lax.axis_size("expert")
    token_count, width = tokens.shape
    top_count = expert_ids.shape[1]
    capacity = token_count * top_count * 3 // (2 * experts)
    pipe = lax.axis_index("pipe")
    place = jnp.stack([lax.rem(pipe, 2), pipe // 2, pipe]).astype(jnp.int32)
    weights = (w_gate[0], w_up[0], in_hbm(w_down[0]))
    ids = in_hbm(expert_ids.T)
    tokens, cotangent, gain = in_hbm(tokens), in_hbm(cotangent), in_hbm(norm_gain.reshape(1, width))

    rows, inverse = make_message(
        place, tokens, cotangent, gain, ids, in_hbm(gate_weights.T), capacity, experts
    )
    rows, ids = lax.optimization_barrier((exchange(rows), ids))
    accs = project(place, rows, weights)
    theirs, *grads = expert(place, core_swap(rows), weights, accs)
    back = merge(mine_rows(place, grads, weights), core_swap(theirs))
    back, gather = lax.optimization_barrier((back, gather_matrix(ids, capacity, experts)))
    kept, sent, product = combine(place, gather, exchange(back), tokens, gain)
    product = product + core_swap(product)
    return final(
        place, kept, high_swap(sent), product, high_swap(product), tokens, cotangent, gain, inverse
    )


def solution(mesh):
    in_specs = (
        P("expert", None),
        P("expert", None),
        P(),
        P("expert", None),
        P("expert", None),
        P("expert", None, "pipe"),
        P("expert", None, "pipe"),
        P("expert", "pipe", None),
    )
    out_specs = P("expert", "pipe")
    return jax.shard_map(body, mesh=mesh, in_specs=in_specs, out_specs=out_specs, check_vma=False)
```

time: 181 us -> 168 us (0.928)
  other arithmetic: 5.1 us -> 0.09 us
  waiting for transfers between devices: 15.6 us -> 12.2 us
  local copies, waits for them, and re-layouts: 3.16 us -> 0.02 us
  blocking collectives: 116 us -> 114 us
    convert_element_type x2 -> x0, other arithmetic: 4.83 us -> none  [the longest x1 2.58 us: body(): (mine.astype(F32) + core_swap(theirs).astype(F32)).astype(BF16)]
    ppermute x2 -> x3, waiting for transfers between devices: 6.35 us -> 3.44 us  [core_swap(): return lax.ppermute(array, 'pipe', CORE_SWAP)]
    unnamed x2 -> x6, local copies, waits for them, and re-layouts: 2.38 us -> 0.02 us
    ppermute x1 -> x2, starting transfers between devices: 2.82 us -> 3.69 us  [high_swap(): return lax.ppermute(array, 'pipe', HIGH_SWAP)]
    pallas_call x1 -> x4, Pallas kernels: 18.9 us -> 18.1 us  [the longest x1 10.6 us: expert(): pl.pallas_call(expert_kernel, out_shape=(jax.ShapeDtypeStruct((height, we...]
    ppermute x1 -> x2, waiting for transfers between devices: 9.22 us -> 8.78 us  [high_swap(): return lax.ppermute(array, 'pipe', HIGH_SWAP)]
  transfers between devices with their start and end apart: 3 -> 5, of which waited for: 3 -> 3; matrix products, arithmetic and copies ran while one was open for 0% -> 0% of each run, Pallas kernels for 4% -> 7%
where the time goes in v6:
time: 168 us
  blocking collectives  114 us (68%)
  Pallas kernels  36.8 us (22%)
  waiting for transfers between devices  12.2 us (7%)
  starting transfers between devices  4.14 us (2%)
    all_to_all x2, blocking collectives, exchange(): lax.all_to_all(shaped, 'expert', split_axis=0, concat_axis=0, tiled=True)  114 us
    pallas_call x1, Pallas kernels, expert(): pl.pallas_call(expert_kernel, out_shape=(jax.ShapeDtypeStruct((height, we...  10.6 us
    ppermute x2, waiting for transfers between devices, high_swap(): return lax.ppermute(array, 'pipe', HIGH_SWAP)  8.78 us
    pallas_call x1, Pallas kernels, make_message(): pl.pallas_call(functools.partial(message_kernel, capacity), out_shape=(ja...  7.45 us
    pallas_call x1, Pallas kernels, project(): pl.pallas_call(project_kernel, out_shape=(acc,) * 3, grid_spec=grid_of((1...  6.81 us
    pallas_call x1, Pallas kernels, mine_rows(): pl.pallas_call(mine_kernel, out_shape=jax.ShapeDtypeStruct((2 * grads[0]....  4.02 us
    ppermute x2, starting transfers between devices, high_swap(): return lax.ppermute(array, 'pipe', HIGH_SWAP)  3.69 us
    ppermute x3, waiting for transfers between devices, core_swap(): return lax.ppermute(array, 'pipe', CORE_SWAP)  3.44 us
  transfers between devices with their start and end apart: 5, of which 3 were waited for; matrix products, arithmetic and copies ran while one was open for 0% of the time, Pallas kernels for 7%

profile of v6, /device:TPU:0, one launch (start us, length us, event | category | flops | bytes accessed | tf_op | source)
XLA Modules:
  0.0 167.6 jit_solution(9414972462952615493)
XLA Ops:
  0.0 0.1 pad_add_fusion.place
  0.1 7.4 %message.1 = (bf16[768,3584]{1,0:T(8,128)(2,1)S(1)}, f32[128,1]{1,0:T(8,128)S(1)}) custom-call(s32[3]{0:T(128)S(1)} %pad_add_fusion.place, bf16[128,7168]{1,0:T(8,128)(2,1)} %tokens.3, bf16[128,7168]{1,0:T(8,128)(2,1)} %tokens.3, bf16[128,7168]{1,0:T(8,128)(2,1)} %cotangent.3, f32[1,7168]{1,0:T(1,128)} %bitcast.28, s32[2,128]{1,0:T(2,128)} %bitcast.32, ...), custom_call_target="tpu_custom_call" | custom-call | tf_op jit(solution)/shard_map/message/pallas_call | solution.py:97
  7.5 0.0 slice-start.1
  7.5 0.0 copy-start
  7.6 74.9 %all_to_all.10 = bf16[32,24,3584]{2,1,0:T(8,128)(2,1)S(1)} all-to-all(bf16[32,24,3584]{2,1,0:T(8,128)(2,1)S(1)} %bitcast.25), channel_id=1, replica_groups=mesh['pipe'=4,'expert'=32] {'expert'}, dimensions={0} | all-to-all | bytes 11010048 | tf_op jit(solution)/shard_map/all_to_all | solution.py:52
  82.5 0.0 collective-permute-start
  82.5 0.0 slice-done
  82.5 6.8 %project.1 = (f32[384,512]{1,0:T(8,128)S(1)}, f32[384,512]{1,0:T(8,128)S(1)}, f32[384,512]{1,0:T(8,128)S(1)}) custom-call(s32[3]{0:T(128)S(1)} %pad_add_fusion.place, bf16[768,3584]{1,0:T(8,128)(2,1)S(1)} %bitcast.22, bf16[7168,512]{1,0:T(8,128)(2,1)S(1)} %bitcast.15, bf16[7168,512]{1,0:T(8,128)(2,1)S(1)} %bitcast.18, bf16[512,7168]{1,0:T(8,128)(2,1)} %bitcast.26), custom_call_target="tpu_custom_call" | custom-call | tf_op jit(solution)/shard_map/project/pallas_call | solution.py:235
  89.3 2.2 %collective-permute-done.rows = bf16[768,3584]{1,0:T(8,128)(2,1)S(1)} collective-permute-done((bf16[768,3584]{1,0:T(8,128)(2,1)S(1)}, bf16[768,3584]{1,0:T(8,128)(2,1)S(1)}, u32[]{:S(2)}, u32[]{:S(2)}) %collective-permute-start) | collective-permute-done | bytes 5505056 | tf_op jit(solution)/shard_map/ppermute | solution.py:42
  91.5 10.6 %expert.1 = (bf16[768,1792]{1,0:T(8,128)(2,1)S(1)}, bf16[384,512]{1,0:T(8,128)(2,1)S(1)}, bf16[384,512]{1,0:T(8,128)(2,1)S(1)}) custom-call(s32[3]{0:T(128)S(1)} %pad_add_fusion.place, bf16[768,3584]{1,0:T(8,128)(2,1)S(1)} %collective-permute-done.rows, bf16[7168,512]{1,0:T(8,128)(2,1)S(1)} %bitcast.16, bf16[7168,512]{1,0:T(8,128)(2,1)S(1)} %bitcast.19, ...), custom_call_target="tpu_custom_call" | custom-call | tf_op jit(solution)/shard_map/expert/pallas_call | solution.py:267
  102.2 0.5 collective-permute-start.1
  102.6 1.0 gather_matrix.1.gather
  103.7 4.0 %mine_rows.1.mine = bf16[768,1792]{1,0:T(8,128)(2,1)S(1)} custom-call(s32[3]{0:T(128)S(1)} %pad_add_fusion.place, bf16[384,512]{1,0:T(8,128)(2,1)S(1)} %get-tuple-element.25.grad_gate, bf16[384,512]{1,0:T(8,128)(2,1)S(1)} %get-tuple-element.26.grad_up, bf16[7168,512]{1,0:T(8,128)(2,1)S(1)} %bitcast.17, bf16[7168,512]{1,0:T(8,128)(2,1)S(1)} %bitcast.20), custom_call_target="tpu_custom_call" | custom-call | tf_op jit(solution)/shard_map/mine_rows/pallas_call | solution.py:288
  107.7 0.0 collective-permute-done.1.other
  107.7 0.7 merge.1
  108.4 39.3 %all_to_all.11 = bf16[32,24,1792]{2,1,0:T(8,128)(2,1)S(1)} all-to-all(bf16[32,24,1792]{2,1,0:T(8,128)(2,1)S(1)} %bitcast.24), channel_id=1, replica_groups=mesh['pipe'=4,'expert'=32] {'expert'}, dimensions={0} | all-to-all | bytes 5505024 | tf_op jit(solution)/shard_map/all_to_all | solution.py:52
  147.7 3.4 %combine.1 = (f32[128,1792]{1,0:T(8,128)S(1)}, bf16[128,1792]{1,0:T(8,128)(2,1)S(1)}, f32[128,128]{1,0:T(8,128)S(1)}) custom-call(s32[3]{0:T(128)S(1)} %pad_add_fusion.place, bf16[256,768]{1,0:T(8,128)(2,1)S(1)} %gather_matrix.1.gather, bf16[768,1792]{1,0:T(8,128)(2,1)S(1)} %bitcast.23, bf16[128,7168]{1,0:T(8,128)(2,1)} %tokens.3, bf16[128,7168]{1,0:T(8,128)(2,1)} %tokens.3, ...), custom_call_target="tpu_custom_call" | custom-call | tf_op jit(solution)/shard_map/combine/pallas_call | solution.py:344
  151.1 2.8 %collective-permute-start.2 = (bf16[128,1792]{1,0:T(8,128)(2,1)S(1)}, bf16[128,1792]{1,0:T(8,128)(2,1)S(1)}, u32[]{:S(2)}, u32[]{:S(2)}) collective-permute-start(bf16[128,1792]{1,0:T(8,128)(2,1)S(1)} %get-tuple-element.32), channel_id=1, source_target_pairs={{0,64},{64,0},{32,96},{96,32},{1,65},{65,1},{33,97},{97,33},{2,66}... | collective-permute-start | bytes 1376264 | tf_op jit(solution)/shard_map/ppermute | solution.py:46
  153.9 0.0 collective-permute-start.3
  153.9 1.3 collective-permute-done.3
  155.1 0.9 collective-permute-start.4
  156.0 8.8 %collective-permute-done.4.other_product = f32[128,128]{1,0:T(8,128)S(1)} collective-permute-done((f32[128,128]{1,0:T(8,128)S(1)}, f32[128,128]{1,0:T(8,128)S(1)}, u32[]{:S(2)}, u32[]{:S(2)}) %collective-permute-start.4) | collective-permute-done | bytes 65568 | tf_op jit(solution)/shard_map/ppermute | solution.py:46
  164.8 0.0 collective-permute-done.2.arrived
  164.8 2.8 %final.1 = bf16[128,1792]{1,0:T(8,128)(2,1)} custom-call(s32[3]{0:T(128)S(1)} %pad_add_fusion.place, f32[128,1792]{1,0:T(8,128)S(1)} %get-tuple-element.31.kept, bf16[128,1792]{1,0:T(8,128)(2,1)S(1)} %collective-permute-done.2.arrived, f32[128,128]{1,0:T(8,128)S(1)} %add.4.own_product, f32[128,128]{1,0:T(8,128)S(1)} %collective-permute-done.4.other_product, ...), custom_call_target="tpu_custom_call" | custom-call | tf_op jit(solution)/shard_map/final/pallas_call | solution.py:380
  (5 shorter events, 0.0 us)
Async XLA Ops:
  0.1 82.4 %slice-start = ((s8[7340032]{0:T(1024)(128)(4,1)}), s8[4194304]{0:T(1024)(128)(4,1)S(1)}, s32[]{:S(2)}) async-start(s8[7340032]{0:T(1024)(128)(4,1)} %bitcast.13), calls=%async_computation.2 | async-start | bytes 8388608
  7.5 75.0 %slice-start.1 = ((s8[7340032]{0:T(1024)(128)(4,1)}), s8[3145728]{0:T(1024)(128)(4,1)S(1)}, s32[]{:S(2)}) async-start(s8[7340032]{0:T(1024)(128)(4,1)} %bitcast.13), calls=%async_computation.3 | async-start | bytes 6291456
  7.5 75.0 %copy-start = (bf16[1,7168,512]{2,1,0:T(8,128)(2,1)S(1)}, bf16[1,7168,512]{2,1,0:T(8,128)(2,1)}, u32[]{:S(2)}) copy-start(bf16[1,7168,512]{2,1,0:T(8,128)(2,1)} %param.14) | copy-start | bytes 22020100
  82.5 9.0 %collective-permute-start = (bf16[768,3584]{1,0:T(8,128)(2,1)S(1)}, bf16[768,3584]{1,0:T(8,128)(2,1)S(1)}, u32[]{:S(2)}, u32[]{:S(2)}) collective-permute-start(bf16[768,3584]{1,0:T(8,128)(2,1)S(1)} %bitcast.21), channel_id=1, source_target_pairs={{0,32},{32,0},{64,96},{96,64},{1,33},{33,1},{65,97},{97,65},{2,34}... | collective-permute-start | bytes 16515080 | tf_op jit(solution)/shard_map/ppermute | solution.py:42
  102.2 5.5 %collective-permute-start.1 = (bf16[768,1792]{1,0:T(8,128)(2,1)S(1)}, bf16[768,1792]{1,0:T(8,128)(2,1)S(1)}, u32[]{:S(2)}, u32[]{:S(2)}) collective-permute-start(bf16[768,1792]{1,0:T(8,128)(2,1)S(1)} %get-tuple-element.27), channel_id=1, source_target_pairs={{0,32},{32,0},{64,96},{96,64},{1,33},{33,1},{65,97},{97,65},{2,34}... | collective-permute-start | bytes 8257544 | tf_op jit(solution)/shard_map/ppermute | solution.py:42
  151.1 13.7 %collective-permute-start.2 = (bf16[128,1792]{1,0:T(8,128)(2,1)S(1)}, bf16[128,1792]{1,0:T(8,128)(2,1)S(1)}, u32[]{:S(2)}, u32[]{:S(2)}) collective-permute-start(bf16[128,1792]{1,0:T(8,128)(2,1)S(1)} %get-tuple-element.32), channel_id=1, source_target_pairs={{0,64},{64,0},{32,96},{96,32},{1,65},{65,1},{33,97},{97,33},{2,66}... | collective-permute-start | bytes 1376264 | tf_op jit(solution)/shard_map/ppermute | solution.py:46
  153.9 1.3 collective-permute-start.3
  155.1 9.7 %collective-permute-start.4 = (f32[128,128]{1,0:T(8,128)S(1)}, f32[128,128]{1,0:T(8,128)S(1)}, u32[]{:S(2)}, u32[]{:S(2)}) collective-permute-start(f32[128,128]{1,0:T(8,128)S(1)} %add.4.own_product), channel_id=1, source_target_pairs={{0,64},{64,0},{32,96},{96,32},{1,65},{65,1},{33,97},{97,33},{2,66}... | collective-permute-start | bytes 196616 | tf_op jit(solution)/shard_map/ppermute | solution.py:46

commit v7 on v6

--- a/solution.py
+++ b/solution.py
@@ -66,6 +66,8 @@
         row = lax.broadcasted_iota(jnp.int32, (height, count), 0)
         taken = jnp.zeros((experts, 1), F32)
         normed_part = jnp.zeros(row.shape, F32)
+        routed_part = jnp.zeros(row.shape, F32)
+        factor = jnp.zeros(row.shape, F32)
         for k in range(top):
             expert = ids[k : k + 1, :]
             named = (expert_of == expert).astype(F32)
@@ -73,23 +75,25 @@
             rank = jnp.sum(earlier * named, axis=0, keepdims=True).astype(jnp.int32)
             taken = taken + jnp.sum(named, axis=1, keepdims=True)
             at = expert * (2 * capacity) + rank
-            normed_part = normed_part + (row == at).astype(F32)
-            select[:, (k + 1) * count : (k + 2) * count] = (row == at + capacity).astype(F32).astype(BF16)
-            column = jnp.sum(jnp.where(earlier_of == later_of, weights[k : k + 1, :], 0.0), axis=1, keepdims=True)
-            factors[:, k : k + 1] = column
+            hit = row == at
+            hit_routed = row == at + capacity
+            normed_part = jnp.where(hit, 1.0, normed_part)
+            routed_part = jnp.where(hit_routed, 1.0, routed_part)
+            factor = jnp.where(hit, 1.0, jnp.where(hit_routed, weights[k : k + 1, :], factor))
         select[:, :count] = normed_part.astype(BF16)
+        select[:, count:] = routed_part.astype(BF16)
+        factors[...] = jnp.broadcast_to(jnp.sum(factor, axis=1, keepdims=True), factors.shape)
         values = all_tokens[...].astype(F32)
         inverse[...] = lax.rsqrt(jnp.mean(values * values, axis=1, keepdims=True) + EPSILON)
 
     normed = (tokens[...].astype(F32) * inverse[...] * gain[...]).astype(BF16)
-    values = cotangent[...].astype(F32)
-    parts = [normed] + [(factors[:, k : k + 1] * values).astype(BF16) for k in range(top)]
-    rows[...] = jnp.dot(select[...], jnp.concatenate(parts, axis=0), preferred_element_type=F32).astype(BF16)
+    both = jnp.concatenate([normed, cotangent[...]], axis=0)
+    picked = jnp.dot(select[...], both, preferred_element_type=F32)
+    rows[...] = (picked * factors[:, :1]).astype(BF16)
 
 
 def make_message(place, tokens, cotangent, gain, ids, weights, capacity, experts):
     count, width = tokens.shape
-    top = ids.shape[0]
     half = width // 2
     height = experts * 2 * capacity
     steps = half // FILL
@@ -108,7 +112,7 @@
                 whole(weights.shape),
             ],
             (pl.BlockSpec((height, FILL), lambda i, place: (0, i)), whole((count, 1))),
-            [pltpu.VMEM((height, (top + 1) * count), BF16), pltpu.VMEM((count, top), F32)],
+            [pltpu.VMEM((height, 2 * count), BF16), pltpu.VMEM((height, LANES), F32)],
         ),
         compiler_params=params(32),
         name="message",
@@ -312,57 +316,62 @@
     )(mine, other)
 
 
-def combine_kernel(place, gather, rows, tokens_0, tokens_1, gain_0, gain_1, kept, sent, product):
+def combine_kernel(place, gather, rows, kept, sent):
     count = kept.shape[0]
     total = jnp.dot(gather[...], rows[...], preferred_element_type=F32)
     low, high = total[:count], total[count:]
     flip = place[1] == 1
     kept[...] = jnp.where(flip, high, low)
     sent[...] = jnp.where(flip, low, high).astype(BF16)
-    part = low * (tokens_0[...].astype(F32) * gain_0[...]) + high * (tokens_1[...].astype(F32) * gain_1[...])
-    part = jnp.broadcast_to(jnp.sum(part, axis=1, keepdims=True), product.shape)
-
-    @pl.when(pl.program_id(0) == 0)
-    def _():
-        product[...] = part
-
-    @pl.when(pl.program_id(0) > 0)
-    def _():
-        product[...] += part
-
-
-def combine(place, gather, rows, tokens, gain):
+
+
+def combine(place, gather, rows):
     count = gather.shape[0] // 2
     height, columns = rows.shape
     steps = 2
     part = columns // steps
     block = pl.BlockSpec((count, part), lambda i, place: (0, i))
-
-    def quarter(size, high):
-        return pl.BlockSpec((size, part), lambda i, place: (0, (2 * high + place[0]) * steps + i))
-
     return pl.pallas_call(
         combine_kernel,
-        out_shape=(
-            jax.ShapeDtypeStruct((count, columns), F32),
-            jax.ShapeDtypeStruct((count, columns), BF16),
-            jax.ShapeDtypeStruct((count, LANES), F32),
-        ),
+        out_shape=(jax.ShapeDtypeStruct((count, columns), F32), jax.ShapeDtypeStruct((count, columns), BF16)),
         grid_spec=grid_of(
             (steps,),
-            [
-                whole(gather.shape),
-                pl.BlockSpec((height, part), lambda i, place: (0, i)),
-                quarter(count, 0),
-                quarter(count, 1),
-                quarter(1, 0),
-                quarter(1, 1),
-            ],
-            (block, block, whole((count, LANES))),
+            [whole(gather.shape), pl.BlockSpec((height, part), lambda i, place: (0, i))],
+            (block, block),
         ),
         compiler_params=params(16),
         name="combine",
-    )(place, gather, rows, tokens, tokens, gain, gain)
+    )(place, gather, rows)
+
+
+def product_kernel(place, kept, sent, own_tokens, other_tokens, own_gain, other_gain, product):
+    part = kept[...] * (own_tokens[...].astype(F32) * own_gain[...])
+    part = part + sent[...].astype(F32) * (other_tokens[...].astype(F32) * other_gain[...])
+    product[...] = jnp.broadcast_to(jnp.sum(part, axis=1, keepdims=True), product.shape)
+
+
+def row_products(place, kept, sent, tokens, gain):
+    count, columns = kept.shape
+
+    def quarter(size, other):
+        def index(i, place):
+            high = 1 - place[1] if other else place[1]
+            return (0, 2 * high + place[0])
+
+        return pl.BlockSpec((size, columns), index)
+
+    return pl.pallas_call(
+        product_kernel,
+        out_shape=jax.ShapeDtypeStruct((count, LANES), F32),
+        grid_spec=grid_of(
+            (1,),
+            [whole(kept.shape), whole(sent.shape)]
+            + [quarter(count, False), quarter(count, True), quarter(1, False), quarter(1, True)],
+            whole((count, LANES)),
+        ),
+        compiler_params=params(16),
+        name="row_products",
+    )(place, kept, sent, tokens, tokens, gain, gain)
 
 
 def final_kernel(width, place, kept, arrived, own_product, other_product, tokens, cotangent, gain, inverse, out):
@@ -400,17 +409,25 @@
     place = jnp.stack([lax.rem(pipe, 2), pipe // 2, pipe]).astype(jnp.int32)
     weights = (w_gate[0], w_up[0], in_hbm(w_down[0]))
     ids = in_hbm(expert_ids.T)
-    tokens, cotangent, gain = in_hbm(tokens), in_hbm(cotangent), in_hbm(norm_gain.reshape(1, width))
+    gain = norm_gain.reshape(1, width)
 
     rows, inverse = make_message(
-        place, tokens, cotangent, gain, ids, in_hbm(gate_weights.T), capacity, experts
+        place,
+        in_hbm(tokens),
+        in_hbm(cotangent),
+        in_hbm(gain),
+        ids,
+        in_hbm(gate_weights.T),
+        capacity,
+        experts,
     )
     rows, ids = lax.optimization_barrier((exchange(rows), ids))
     accs = project(place, rows, weights)
     theirs, *grads = expert(place, core_swap(rows), weights, accs)
     back = merge(mine_rows(place, grads, weights), core_swap(theirs))
     back, gather = lax.optimization_barrier((back, gather_matrix(ids, capacity, experts)))
-    kept, sent, product = combine(place, gather, exchange(back), tokens, gain)
+    kept, sent = combine(place, gather, exchange(back))
+    product = row_products(place, kept, sent, tokens, gain)
     product = product + core_swap(product)
     return final(
         place, kept, high_swap(sent), product, high_swap(product), tokens, cotangent, gain, inverse

time: 168 us -> 164 us (0.976)
  Pallas kernels: 36.8 us -> 33.8 us
  transfers between devices with their start and end apart: 5 -> 5, of which waited for: 3 -> 3; matrix products, arithmetic and copies ran while one was open for 0% -> 0% of each run, Pallas kernels for 7% -> 8%
where the time goes in v7:
time: 164 us
  blocking collectives  114 us (70%)
  Pallas kernels  33.8 us (21%)
  waiting for transfers between devices  11.3 us (7%)
  starting transfers between devices  4.14 us (3%)
    all_to_all x2, blocking collectives, exchange(): lax.all_to_all(shaped, 'expert', split_axis=0, concat_axis=0, tiled=True)  114 us
    pallas_call x1, Pallas kernels, expert(): pl.pallas_call(expert_kernel, out_shape=(jax.ShapeDtypeStruct((height, we...  10.6 us
    ppermute x2, waiting for transfers between devices, high_swap(): return lax.ppermute(array, 'pipe', HIGH_SWAP)  7.88 us
    pallas_call x1, Pallas kernels, project(): pl.pallas_call(project_kernel, out_shape=(acc,) * 3, grid_spec=grid_of((1...  6.84 us
    pallas_call x1, Pallas kernels, make_message(): pl.pallas_call(functools.partial(message_kernel, capacity), out_shape=(ja...  5.92 us
    pallas_call x1, Pallas kernels, mine_rows(): pl.pallas_call(mine_kernel, out_shape=jax.ShapeDtypeStruct((2 * grads[0]....  4.02 us
    ppermute x2, starting transfers between devices, high_swap(): return lax.ppermute(array, 'pipe', HIGH_SWAP)  3.69 us
    ppermute x3, waiting for transfers between devices, core_swap(): return lax.ppermute(array, 'pipe', CORE_SWAP)  3.4 us
  transfers between devices with their start and end apart: 5, of which 3 were waited for; matrix products, arithmetic and copies ran while one was open for 0% of the time, Pallas kernels for 8%

profile of v7, /device:TPU:0, one launch (start us, length us, event | category | flops | bytes accessed | tf_op | source)
XLA Modules:
  0.0 163.7 jit_solution(2706444258644888579)
XLA Ops:
  0.0 0.1 pad_add_fusion.place
  0.1 5.9 %message.1 = (bf16[768,3584]{1,0:T(8,128)(2,1)S(1)}, f32[128,1]{1,0:T(8,128)S(1)}) custom-call(s32[3]{0:T(128)S(1)} %pad_add_fusion.place, bf16[128,7168]{1,0:T(8,128)(2,1)} %tokens.3, bf16[128,7168]{1,0:T(8,128)(2,1)} %tokens.3, bf16[128,7168]{1,0:T(8,128)(2,1)} %cotangent.3, f32[1,7168]{1,0:T(1,128)} %bitcast.26, s32[2,128]{1,0:T(2,128)} %bitcast.32, ...), custom_call_target="tpu_custom_call" | custom-call | tf_op jit(solution)/shard_map/message/pallas_call | solution.py:101
  6.0 0.0 slice-start.1
  6.0 0.0 copy-start
  6.0 74.9 %all_to_all.10 = bf16[32,24,3584]{2,1,0:T(8,128)(2,1)S(1)} all-to-all(bf16[32,24,3584]{2,1,0:T(8,128)(2,1)S(1)} %bitcast.25), channel_id=1, replica_groups=mesh['pipe'=4,'expert'=32] {'expert'}, dimensions={0} | all-to-all | bytes 11010048 | tf_op jit(solution)/shard_map/all_to_all | solution.py:52
  81.0 0.0 collective-permute-start
  81.0 6.8 %project.1 = (f32[384,512]{1,0:T(8,128)S(1)}, f32[384,512]{1,0:T(8,128)S(1)}, f32[384,512]{1,0:T(8,128)S(1)}) custom-call(s32[3]{0:T(128)S(1)} %pad_add_fusion.place, bf16[768,3584]{1,0:T(8,128)(2,1)S(1)} %bitcast.22, bf16[7168,512]{1,0:T(8,128)(2,1)S(1)} %bitcast.15, bf16[7168,512]{1,0:T(8,128)(2,1)S(1)} %bitcast.18, bf16[512,7168]{1,0:T(8,128)(2,1)} %bitcast.30), custom_call_target="tpu_custom_call" | custom-call | tf_op jit(solution)/shard_map/project/pallas_call | solution.py:239
  87.8 2.2 %collective-permute-done.rows = bf16[768,3584]{1,0:T(8,128)(2,1)S(1)} collective-permute-done((bf16[768,3584]{1,0:T(8,128)(2,1)S(1)}, bf16[768,3584]{1,0:T(8,128)(2,1)S(1)}, u32[]{:S(2)}, u32[]{:S(2)}) %collective-permute-start) | collective-permute-done | bytes 5505056 | tf_op jit(solution)/shard_map/ppermute | solution.py:42
  90.0 10.6 %expert.1 = (bf16[768,1792]{1,0:T(8,128)(2,1)S(1)}, bf16[384,512]{1,0:T(8,128)(2,1)S(1)}, bf16[384,512]{1,0:T(8,128)(2,1)S(1)}) custom-call(s32[3]{0:T(128)S(1)} %pad_add_fusion.place, bf16[768,3584]{1,0:T(8,128)(2,1)S(1)} %collective-permute-done.rows, bf16[7168,512]{1,0:T(8,128)(2,1)S(1)} %bitcast.16, bf16[7168,512]{1,0:T(8,128)(2,1)S(1)} %bitcast.19, ...), custom_call_target="tpu_custom_call" | custom-call | tf_op jit(solution)/shard_map/expert/pallas_call | solution.py:271
  100.6 0.4 collective-permute-start.1
  101.1 1.0 gather_matrix.1.gather
  102.1 4.0 %mine_rows.1.mine = bf16[768,1792]{1,0:T(8,128)(2,1)S(1)} custom-call(s32[3]{0:T(128)S(1)} %pad_add_fusion.place, bf16[384,512]{1,0:T(8,128)(2,1)S(1)} %get-tuple-element.24.grad_gate, bf16[384,512]{1,0:T(8,128)(2,1)S(1)} %get-tuple-element.25.grad_up, bf16[7168,512]{1,0:T(8,128)(2,1)S(1)} %bitcast.17, bf16[7168,512]{1,0:T(8,128)(2,1)S(1)} %bitcast.20), custom_call_target="tpu_custom_call" | custom-call | tf_op jit(solution)/shard_map/mine_rows/pallas_call | solution.py:292
  106.1 0.0 collective-permute-done.1.other
  106.2 0.7 merge.1
  106.9 39.3 %all_to_all.11 = bf16[32,24,1792]{2,1,0:T(8,128)(2,1)S(1)} all-to-all(bf16[32,24,1792]{2,1,0:T(8,128)(2,1)S(1)} %bitcast.24), channel_id=1, replica_groups=mesh['pipe'=4,'expert'=32] {'expert'}, dimensions={0} | all-to-all | bytes 5505024 | tf_op jit(solution)/shard_map/all_to_all | solution.py:52
  146.1 2.1 %combine.1 = (f32[128,1792]{1,0:T(8,128)S(1)}, bf16[128,1792]{1,0:T(8,128)(2,1)S(1)}) custom-call(s32[3]{0:T(128)S(1)} %pad_add_fusion.place, bf16[256,768]{1,0:T(8,128)(2,1)S(1)} %gather_matrix.1.gather, bf16[768,1792]{1,0:T(8,128)(2,1)S(1)} %bitcast.23), custom_call_target="tpu_custom_call" | custom-call | tf_op jit(solution)/shard_map/combine/pallas_call | solution.py:334
  148.2 0.0 copy-start.2
  148.2 2.8 %collective-permute-start.2 = (bf16[128,1792]{1,0:T(8,128)(2,1)S(1)}, bf16[128,1792]{1,0:T(8,128)(2,1)S(1)}, u32[]{:S(2)}, u32[]{:S(2)}) collective-permute-start(bf16[128,1792]{1,0:T(8,128)(2,1)S(1)} %get-tuple-element.31.sent), channel_id=1, source_target_pairs={{0,64},{64,0},{32,96},{96,32},{1,65},{65,1},{33,97},{97,33},{2,66}... | collective-permute-start | bytes 1376264 | tf_op jit(solution)/shard_map/ppermute | solution.py:46
  151.1 0.9 row_products.1
  152.0 0.0 collective-permute-start.3
  152.0 1.2 collective-permute-done.3
  153.3 0.9 collective-permute-start.4
  154.1 7.9 %collective-permute-done.4.other_product = f32[128,128]{1,0:T(8,128)S(1)} collective-permute-done((f32[128,128]{1,0:T(8,128)S(1)}, f32[128,128]{1,0:T(8,128)S(1)}, u32[]{:S(2)}, u32[]{:S(2)}) %collective-permute-start.4) | collective-permute-done | bytes 65568 | tf_op jit(solution)/shard_map/ppermute | solution.py:46
  162.0 1.6 final.1
  (12 shorter events, 0.0 us)
Async XLA Ops:
  0.1 80.9 %slice-start = ((s8[7340032]{0:T(1024)(128)(4,1)}), s8[4194304]{0:T(1024)(128)(4,1)S(1)}, s32[]{:S(2)}) async-start(s8[7340032]{0:T(1024)(128)(4,1)} %bitcast.13), calls=%async_computation.2 | async-start | bytes 8388608
  6.0 75.0 %slice-start.1 = ((s8[7340032]{0:T(1024)(128)(4,1)}), s8[3145728]{0:T(1024)(128)(4,1)S(1)}, s32[]{:S(2)}) async-start(s8[7340032]{0:T(1024)(128)(4,1)} %bitcast.13), calls=%async_computation.3 | async-start | bytes 6291456
  6.0 75.0 %copy-start = (bf16[1,7168,512]{2,1,0:T(8,128)(2,1)S(1)}, bf16[1,7168,512]{2,1,0:T(8,128)(2,1)}, u32[]{:S(2)}) copy-start(bf16[1,7168,512]{2,1,0:T(8,128)(2,1)} %param.14) | copy-start | bytes 22020100
  81.0 9.0 %collective-permute-start = (bf16[768,3584]{1,0:T(8,128)(2,1)S(1)}, bf16[768,3584]{1,0:T(8,128)(2,1)S(1)}, u32[]{:S(2)}, u32[]{:S(2)}) collective-permute-start(bf16[768,3584]{1,0:T(8,128)(2,1)S(1)} %bitcast.21), channel_id=1, source_target_pairs={{0,32},{32,0},{64,96},{96,64},{1,33},{33,1},{65,97},{97,65},{2,34}... | collective-permute-start | bytes 16515080 | tf_op jit(solution)/shard_map/ppermute | solution.py:42
  100.6 5.5 %collective-permute-start.1 = (bf16[768,1792]{1,0:T(8,128)(2,1)S(1)}, bf16[768,1792]{1,0:T(8,128)(2,1)S(1)}, u32[]{:S(2)}, u32[]{:S(2)}) collective-permute-start(bf16[768,1792]{1,0:T(8,128)(2,1)S(1)} %get-tuple-element.26), channel_id=1, source_target_pairs={{0,32},{32,0},{64,96},{96,64},{1,33},{33,1},{65,97},{97,65},{2,34}... | collective-permute-start | bytes 8257544 | tf_op jit(solution)/shard_map/ppermute | solution.py:42
  146.1 4.9 %copy-start.1 = (bf16[128,7168]{1,0:T(8,128)(2,1)S(1)}, bf16[128,7168]{1,0:T(8,128)(2,1)}, u32[]{:S(2)}) copy-start(bf16[128,7168]{1,0:T(8,128)(2,1)} %tokens.3) | copy-start | bytes 5505028
  146.1 4.9 %copy-start.3 = (f32[7168]{0:T(1024)S(1)}, f32[7168]{0:T(1024)}, u32[]{:S(2)}) copy-start(f32[7168]{0:T(1024)} %param.10) | copy-start | bytes 86020
  148.2 13.8 %copy-start.2 = (bf16[128,7168]{1,0:T(8,128)(2,1)S(1)}, bf16[128,7168]{1,0:T(8,128)(2,1)}, u32[]{:S(2)}) copy-start(bf16[128,7168]{1,0:T(8,128)(2,1)} %cotangent.3) | copy-start | bytes 5505028
  148.2 13.8 %collective-permute-start.2 = (bf16[128,1792]{1,0:T(8,128)(2,1)S(1)}, bf16[128,1792]{1,0:T(8,128)(2,1)S(1)}, u32[]{:S(2)}, u32[]{:S(2)}) collective-permute-start(bf16[128,1792]{1,0:T(8,128)(2,1)S(1)} %get-tuple-element.31.sent), channel_id=1, source_target_pairs={{0,64},{64,0},{32,96},{96,32},{1,65},{65,1},{33,97},{97,33},{2,66}... | collective-permute-start | bytes 1376264 | tf_op jit(solution)/shard_map/ppermute | solution.py:46
  152.0 1.3 collective-permute-start.3
  153.3 8.8 %collective-permute-start.4 = (f32[128,128]{1,0:T(8,128)S(1)}, f32[128,128]{1,0:T(8,128)S(1)}, u32[]{:S(2)}, u32[]{:S(2)}) collective-permute-start(f32[128,128]{1,0:T(8,128)S(1)} %add.4.own_product), channel_id=1, source_target_pairs={{0,64},{64,0},{32,96},{96,32},{1,65},{65,1},{33,97},{97,33},{2,66}... | collective-permute-start | bytes 196616 | tf_op jit(solution)/shard_map/ppermute | solution.py:46

commit v8 on v7

--- a/solution.py
+++ b/solution.py
@@ -11,7 +11,7 @@
 BF16 = jnp.bfloat16
 F32 = jnp.float32
 MIB = 1024 * 1024
-FILL = 1792
+FILL = 896
 DEPTH = 1792
 BACK = 896
 LANES = 128
@@ -52,71 +52,80 @@
     return lax.all_to_all(shaped, "expert", split_axis=0, concat_axis=0, tiled=True).reshape(rows.shape)
 
 
-def message_kernel(capacity, place, all_tokens, tokens, cotangent, gain, ids, weights, rows, inverse, select, factors):
+def message_kernel(capacity, place, tokens, cotangent, gain, ids, weights, rows, inverse, tokens_in, cotangent_in, select, factors, sems):
     top, count = ids.shape
-
-    @pl.when(pl.program_id(0) == 0)
-    def _():
-        height = select.shape[0]
-        experts = height // (2 * capacity)
-        expert_of = lax.broadcasted_iota(jnp.int32, (experts, count), 0)
-        earlier_of = lax.broadcasted_iota(jnp.int32, (count, count), 0)
-        later_of = lax.broadcasted_iota(jnp.int32, (count, count), 1)
-        before = (earlier_of < later_of).astype(F32).astype(BF16)
-        row = lax.broadcasted_iota(jnp.int32, (height, count), 0)
-        taken = jnp.zeros((experts, 1), F32)
-        normed_part = jnp.zeros(row.shape, F32)
-        routed_part = jnp.zeros(row.shape, F32)
-        factor = jnp.zeros(row.shape, F32)
-        for k in range(top):
-            expert = ids[k : k + 1, :]
-            named = (expert_of == expert).astype(F32)
-            earlier = jnp.dot(named.astype(BF16), before, preferred_element_type=F32) + taken
-            rank = jnp.sum(earlier * named, axis=0, keepdims=True).astype(jnp.int32)
-            taken = taken + jnp.sum(named, axis=1, keepdims=True)
-            at = expert * (2 * capacity) + rank
-            hit = row == at
-            hit_routed = row == at + capacity
-            normed_part = jnp.where(hit, 1.0, normed_part)
-            routed_part = jnp.where(hit_routed, 1.0, routed_part)
-            factor = jnp.where(hit, 1.0, jnp.where(hit_routed, weights[k : k + 1, :], factor))
-        select[:, :count] = normed_part.astype(BF16)
-        select[:, count:] = routed_part.astype(BF16)
-        factors[...] = jnp.broadcast_to(jnp.sum(factor, axis=1, keepdims=True), factors.shape)
-        values = all_tokens[...].astype(F32)
-        inverse[...] = lax.rsqrt(jnp.mean(values * values, axis=1, keepdims=True) + EPSILON)
-
-    normed = (tokens[...].astype(F32) * inverse[...] * gain[...]).astype(BF16)
-    both = jnp.concatenate([normed, cotangent[...]], axis=0)
-    picked = jnp.dot(select[...], both, preferred_element_type=F32)
-    rows[...] = (picked * factors[:, :1]).astype(BF16)
+    half = rows.shape[1]
+    start = place[0] * half
+    own_half = pl.ds(pl.multiple_of(start, half), half)
+    copies = (
+        pltpu.make_async_copy(tokens, tokens_in, sems.at[0]),
+        pltpu.make_async_copy(cotangent.at[:, own_half], cotangent_in, sems.at[1]),
+    )
+    for copy in copies:
+        copy.start()
+    height = select.shape[0]
+    experts = height // (2 * capacity)
+    expert_of = lax.broadcasted_iota(jnp.int32, (experts, count), 0)
+    earlier_of = lax.broadcasted_iota(jnp.int32, (count, count), 0)
+    later_of = lax.broadcasted_iota(jnp.int32, (count, count), 1)
+    before = (earlier_of < later_of).astype(F32).astype(BF16)
+    row = lax.broadcasted_iota(jnp.int32, (height, count), 0)
+    taken = jnp.zeros((experts, 1), F32)
+    normed_part = jnp.zeros(row.shape, F32)
+    routed_part = jnp.zeros(row.shape, F32)
+    factor = jnp.zeros(row.shape, F32)
+    for k in range(top):
+        expert = ids[k : k + 1, :]
+        named = (expert_of == expert).astype(F32)
+        earlier = jnp.dot(named.astype(BF16), before, preferred_element_type=F32) + taken
+        rank = jnp.sum(earlier * named, axis=0, keepdims=True).astype(jnp.int32)
+        taken = taken + jnp.sum(named, axis=1, keepdims=True)
+        at = expert * (2 * capacity) + rank
+        hit = row == at
+        hit_routed = row == at + capacity
+        normed_part = jnp.where(hit, 1.0, normed_part)
+        routed_part = jnp.where(hit_routed, 1.0, routed_part)
+        factor = jnp.where(hit, 1.0, jnp.where(hit_routed, weights[k : k + 1, :], factor))
+    select[:, :count] = normed_part.astype(BF16)
+    select[:, count:] = routed_part.astype(BF16)
+    factors[...] = jnp.broadcast_to(jnp.sum(factor, axis=1, keepdims=True), factors.shape)
+    copies[0].wait()
+    values = tokens_in[...].astype(F32)
+    scale = lax.rsqrt(jnp.mean(values * values, axis=1, keepdims=True) + EPSILON)
+    inverse[...] = scale
+    copies[1].wait()
+    for at in range(0, half, FILL):
+        own = pl.ds(pl.multiple_of(start + at, LANES), FILL)
+        normed = (tokens_in[:, own].astype(F32) * scale * gain[:, own]).astype(BF16)
+        both = jnp.concatenate([normed, cotangent_in[:, at : at + FILL]], axis=0)
+        picked = jnp.dot(select[...], both, preferred_element_type=F32)
+        rows[:, at : at + FILL] = (picked * factors[:, :1]).astype(BF16)
 
 
 def make_message(place, tokens, cotangent, gain, ids, weights, capacity, experts):
     count, width = tokens.shape
     half = width // 2
     height = experts * 2 * capacity
-    steps = half // FILL
-    column = lambda i, place: (0, place[0] * steps + i)
+    any_space = pl.BlockSpec(memory_space=pl.ANY)
+    resident = pl.BlockSpec(memory_space=pltpu.VMEM)
     return pl.pallas_call(
         functools.partial(message_kernel, capacity),
         out_shape=(jax.ShapeDtypeStruct((height, half), BF16), jax.ShapeDtypeStruct((count, 1), F32)),
         grid_spec=grid_of(
-            (steps,),
+            (1,),
+            [any_space, any_space, whole(gain.shape), whole(ids.shape), whole(weights.shape)],
+            (resident, whole((count, 1))),
             [
-                whole((count, width)),
-                pl.BlockSpec((count, FILL), column),
-                pl.BlockSpec((count, FILL), column),
-                pl.BlockSpec((1, FILL), column),
-                whole(ids.shape),
-                whole(weights.shape),
+                pltpu.VMEM((count, width), BF16),
+                pltpu.VMEM((count, half), BF16),
+                pltpu.VMEM((height, 2 * count), BF16),
+                pltpu.VMEM((height, LANES), F32),
+                pltpu.SemaphoreType.DMA((2,)),
             ],
-            (pl.BlockSpec((height, FILL), lambda i, place: (0, i)), whole((count, 1))),
-            [pltpu.VMEM((height, 2 * count), BF16), pltpu.VMEM((height, LANES), F32)],
         ),
-        compiler_params=params(32),
+        compiler_params=params(24),
         name="message",
-    )(place, tokens, tokens, cotangent, gain, ids, weights)
+    )(place, tokens, cotangent, gain, ids, weights)
 
 
 def gather_kernel(capacity, ids, out):
@@ -192,7 +201,7 @@
     return jnp.concatenate([p[:, None] for p in parts], axis=1).reshape(2 * rows, columns)
 
 
-def project_half(rows, gate, up, down, down_in, sems, side, accs, first):
+def project_half(rows, gate, up, down, down_in, sems, side, accs, bases):
     half = rows.shape[1]
     copies = []
     for i in range(half // DEPTH):
@@ -208,8 +217,9 @@
         to_up = jnp.dot(normed, up[at, :], preferred_element_type=F32)
         copies[i].wait()
         to_hidden = lax.dot_general(routed, down_in[:, to], LAST, preferred_element_type=F32)
-        for acc, add in zip(accs, (to_gate, to_up, to_hidden)):
-            acc[...] = add if first and i == 0 else acc[...] + add
+        for number, add in enumerate((to_gate, to_up, to_hidden)):
+            base = (bases if i == 0 else accs)[number]
+            accs[number][...] = add if base is None else base[...] + add
 
 
 def back_rows(place, side, grad_gate, grad_up, gate, up, out):
@@ -230,7 +240,7 @@
 
 
 def project_kernel(place, rows, gate, up, down, acc_gate, acc_up, acc_hidden, down_in, sems):
-    project_half(rows, gate, up, down, down_in, sems, place[0], (acc_gate, acc_up, acc_hidden), True)
+    project_half(rows, gate, up, down, down_in, sems, place[0], (acc_gate, acc_up, acc_hidden), (None,) * 3)
 
 
 def project(place, rows, weights):
@@ -253,9 +263,7 @@
 def expert_kernel(place, rows, gate, up, down, in_gate, in_up, in_hidden, theirs, grad_gate, grad_up, acc_gate, acc_up, acc_hidden, down_in, sems):
     side = 1 - place[0]
     accs = (acc_gate, acc_up, acc_hidden)
-    for acc, value in zip(accs, (in_gate, in_up, in_hidden)):
-        acc[...] = value[...]
-    project_half(rows, gate, up, down, down_in, sems, side, accs, False)
+    project_half(rows, gate, up, down, down_in, sems, side, accs, (in_gate, in_up, in_hidden))
     pre_gate, pre_up, hidden = acc_gate[...], acc_up[...], acc_hidden[...]
     sigma = jax.nn.sigmoid(pre_gate)
     grad_gate[...] = (hidden * pre_up * sigma * (1.0 + pre_gate * (1.0 - sigma))).astype(BF16)
@@ -316,31 +324,21 @@
     )(mine, other)
 
 
-def combine_kernel(place, gather, rows, kept, sent):
-    count = kept.shape[0]
-    total = jnp.dot(gather[...], rows[...], preferred_element_type=F32)
-    low, high = total[:count], total[count:]
-    flip = place[1] == 1
-    kept[...] = jnp.where(flip, high, low)
-    sent[...] = jnp.where(flip, low, high).astype(BF16)
-
-
-def combine(place, gather, rows):
+def sums_kernel(place, gather, rows, out):
+    out[...] = jnp.dot(gather[...], rows[...], preferred_element_type=F32).astype(out.dtype)
+
+
+def token_sums(place, gather, rows, other, kind):
     count = gather.shape[0] // 2
     height, columns = rows.shape
-    steps = 2
-    part = columns // steps
-    block = pl.BlockSpec((count, part), lambda i, place: (0, i))
-    return pl.pallas_call(
-        combine_kernel,
-        out_shape=(jax.ShapeDtypeStruct((count, columns), F32), jax.ShapeDtypeStruct((count, columns), BF16)),
-        grid_spec=grid_of(
-            (steps,),
-            [whole(gather.shape), pl.BlockSpec((height, part), lambda i, place: (0, i))],
-            (block, block),
-        ),
+    resident = pl.BlockSpec(memory_space=pltpu.VMEM)
+    mine = pl.BlockSpec((count, height), lambda i, place: (1 - place[1] if other else place[1], 0))
+    return pl.pallas_call(
+        sums_kernel,
+        out_shape=jax.ShapeDtypeStruct((count, columns), kind),
+        grid_spec=grid_of((1,), [mine, resident], resident),
         compiler_params=params(16),
-        name="combine",
+        name="token_sums",
     )(place, gather, rows)
 
 
@@ -426,7 +424,9 @@
     theirs, *grads = expert(place, core_swap(rows), weights, accs)
     back = merge(mine_rows(place, grads, weights), core_swap(theirs))
     back, gather = lax.optimization_barrier((back, gather_matrix(ids, capacity, experts)))
-    kept, sent = combine(place, gather, exchange(back))
+    back = exchange(back)
+    sent = token_sums(place, gather, back, True, BF16)
+    kept = token_sums(place, gather, back, False, F32)
     product = row_products(place, kept, sent, tokens, gain)
     product = product + core_swap(product)
     return final(

time: 164 us -> 162 us (0.988)
  transfers between devices with their start and end apart: 5 -> 5, of which waited for: 3 -> 3; matrix products, arithmetic and copies ran while one was open for 0% -> 0% of each run, Pallas kernels for 8% -> 9%
where the time goes in v8:
time: 162 us
  blocking collectives  114 us (70%)
  Pallas kernels  33.1 us (20%)
  waiting for transfers between devices  10.2 us (6%)
  starting transfers between devices  4.15 us (3%)
    all_to_all x2, blocking collectives, exchange(): lax.all_to_all(shaped, 'expert', split_axis=0, concat_axis=0, tiled=True)  114 us
    pallas_call x1, Pallas kernels, expert(): pl.pallas_call(expert_kernel, out_shape=(jax.ShapeDtypeStruct((height, we...  10.4 us
    pallas_call x1, Pallas kernels, project(): pl.pallas_call(project_kernel, out_shape=(acc,) * 3, grid_spec=grid_of((1...  6.81 us
    ppermute x2, waiting for transfers between devices, high_swap(): return lax.ppermute(array, 'pipe', HIGH_SWAP)  6.74 us
    pallas_call x1, Pallas kernels, make_message(): pl.pallas_call(functools.partial(message_kernel, capacity), out_shape=(ja...  5.39 us
    pallas_call x1, Pallas kernels, mine_rows(): pl.pallas_call(mine_kernel, out_shape=jax.ShapeDtypeStruct((2 * grads[0]....  4.02 us
    ppermute x2, starting transfers between devices, high_swap(): return lax.ppermute(array, 'pipe', HIGH_SWAP)  3.7 us
    ppermute x3, waiting for transfers between devices, core_swap(): return lax.ppermute(array, 'pipe', CORE_SWAP)  3.43 us
  transfers between devices with their start and end apart: 5, of which 3 were waited for; matrix products, arithmetic and copies ran while one was open for 0% of the time, Pallas kernels for 9%

profile of v8, /device:TPU:0, one launch (start us, length us, event | category | flops | bytes accessed | tf_op | source)
XLA Modules:
  0.0 161.9 jit_solution(11066724894611025116)
XLA Ops:
  0.0 0.1 pad_add_fusion.place
  0.1 5.4 %message.1 = (bf16[768,3584]{1,0:T(8,128)(2,1)S(1)}, f32[128,1]{1,0:T(8,128)S(1)}) custom-call(s32[3]{0:T(128)S(1)} %pad_add_fusion.place, bf16[128,7168]{1,0:T(8,128)(2,1)} %tokens.3, bf16[128,7168]{1,0:T(8,128)(2,1)} %cotangent.3, f32[1,7168]{1,0:T(1,128)} %bitcast.27, s32[2,128]{1,0:T(2,128)} %bitcast.33, f32[2,128]{1,0:T(2,128)} %bitcast.35), custom_call_target="tpu_custom_call" | custom-call | tf_op jit(solution)/shard_map/message/pallas_call | solution.py:111
  5.5 0.0 slice-start.1
  5.5 0.0 copy-start
  5.5 74.9 %all_to_all.10 = bf16[32,24,3584]{2,1,0:T(8,128)(2,1)S(1)} all-to-all(bf16[32,24,3584]{2,1,0:T(8,128)(2,1)S(1)} %bitcast.26), channel_id=1, replica_groups=mesh['pipe'=4,'expert'=32] {'expert'}, dimensions={0} | all-to-all | bytes 11010048 | tf_op jit(solution)/shard_map/all_to_all | solution.py:52
  80.5 6.8 %project.1 = (f32[384,512]{1,0:T(8,128)S(1)}, f32[384,512]{1,0:T(8,128)S(1)}, f32[384,512]{1,0:T(8,128)S(1)}) custom-call(s32[3]{0:T(128)S(1)} %pad_add_fusion.place, bf16[768,3584]{1,0:T(8,128)(2,1)S(1)} %bitcast.24, bf16[7168,512]{1,0:T(8,128)(2,1)S(1)} %bitcast.15, bf16[7168,512]{1,0:T(8,128)(2,1)S(1)} %bitcast.18, bf16[512,7168]{1,0:T(8,128)(2,1)} %bitcast.31), custom_call_target="tpu_custom_call" | custom-call | tf_op jit(solution)/shard_map/project/pallas_call | solution.py:249
  87.3 2.2 %collective-permute-done.rows = bf16[768,3584]{1,0:T(8,128)(2,1)S(1)} collective-permute-done((bf16[768,3584]{1,0:T(8,128)(2,1)S(1)}, bf16[768,3584]{1,0:T(8,128)(2,1)S(1)}, u32[]{:S(2)}, u32[]{:S(2)}) %collective-permute-start) | collective-permute-done | bytes 5505056 | tf_op jit(solution)/shard_map/ppermute | solution.py:42
  89.5 10.4 %expert.1 = (bf16[768,1792]{1,0:T(8,128)(2,1)S(1)}, bf16[384,512]{1,0:T(8,128)(2,1)S(1)}, bf16[384,512]{1,0:T(8,128)(2,1)S(1)}) custom-call(s32[3]{0:T(128)S(1)} %pad_add_fusion.place, bf16[768,3584]{1,0:T(8,128)(2,1)S(1)} %collective-permute-done.rows, bf16[7168,512]{1,0:T(8,128)(2,1)S(1)} %bitcast.16, bf16[7168,512]{1,0:T(8,128)(2,1)S(1)} %bitcast.19, ...), custom_call_target="tpu_custom_call" | custom-call | tf_op jit(solution)/shard_map/expert/pallas_call | solution.py:279
  99.9 0.4 collective-permute-start.1
  100.3 1.0 gather_matrix.1.gather
  101.4 4.0 %mine_rows.1.mine = bf16[768,1792]{1,0:T(8,128)(2,1)S(1)} custom-call(s32[3]{0:T(128)S(1)} %pad_add_fusion.place, bf16[384,512]{1,0:T(8,128)(2,1)S(1)} %get-tuple-element.22.grad_gate, bf16[384,512]{1,0:T(8,128)(2,1)S(1)} %get-tuple-element.23.grad_up, bf16[7168,512]{1,0:T(8,128)(2,1)S(1)} %bitcast.17, bf16[7168,512]{1,0:T(8,128)(2,1)S(1)} %bitcast.20), custom_call_target="tpu_custom_call" | custom-call | tf_op jit(solution)/shard_map/mine_rows/pallas_call | solution.py:300
  105.4 0.7 merge.1
  106.1 39.3 %all_to_all.11 = bf16[32,24,1792]{2,1,0:T(8,128)(2,1)S(1)} all-to-all(bf16[32,24,1792]{2,1,0:T(8,128)(2,1)S(1)} %bitcast.25), channel_id=1, replica_groups=mesh['pipe'=4,'expert'=32] {'expert'}, dimensions={0} | all-to-all | bytes 5505024 | tf_op jit(solution)/shard_map/all_to_all | solution.py:52
  145.4 1.1 token_sums.3.sent
  146.5 0.0 copy-start.1
  146.5 0.0 copy-start.3
  146.5 2.8 %collective-permute-start.2 = (bf16[128,1792]{1,0:T(8,128)(2,1)S(1)}, bf16[128,1792]{1,0:T(8,128)(2,1)S(1)}, u32[]{:S(2)}, u32[]{:S(2)}) collective-permute-start(bf16[128,1792]{1,0:T(8,128)(2,1)S(1)} %token_sums.3.sent), channel_id=1, source_target_pairs={{0,64},{64,0},{32,96},{96,32},{1,65},{65,1},{33,97},{97,33},{2,66}... | collective-permute-start | bytes 1376264 | tf_op jit(solution)/shard_map/ppermute | solution.py:46
  149.3 1.1 token_sums.2.kept
  150.4 0.9 row_products.1
  151.4 0.0 collective-permute-start.3
  151.4 1.2 collective-permute-done.3
  152.7 0.9 collective-permute-start.4
  153.5 6.7 %collective-permute-done.4.other_product = f32[128,128]{1,0:T(8,128)S(1)} collective-permute-done((f32[128,128]{1,0:T(8,128)S(1)}, f32[128,128]{1,0:T(8,128)S(1)}, u32[]{:S(2)}, u32[]{:S(2)}) %collective-permute-start.4) | collective-permute-done | bytes 65568 | tf_op jit(solution)/shard_map/ppermute | solution.py:46
  160.3 1.6 %final.1 = bf16[128,1792]{1,0:T(8,128)(2,1)} custom-call(s32[3]{0:T(128)S(1)} %pad_add_fusion.place, f32[128,1792]{1,0:T(8,128)S(1)} %token_sums.2.kept, bf16[128,1792]{1,0:T(8,128)(2,1)S(1)} %collective-permute-done.2.arrived, f32[128,128]{1,0:T(8,128)S(1)} %add.4.own_product, f32[128,128]{1,0:T(8,128)S(1)} %collective-permute-done.4.other_product, ...), custom_call_target="tpu_custom_call" | custom-call | tf_op jit(solution)/shard_map/final/pallas_call | solution.py:387
  (13 shorter events, 0.0 us)
Async XLA Ops:
  0.1 80.4 %slice-start = ((s8[7340032]{0:T(1024)(128)(4,1)}), s8[4194304]{0:T(1024)(128)(4,1)S(1)}, s32[]{:S(2)}) async-start(s8[7340032]{0:T(1024)(128)(4,1)} %bitcast.13), calls=%async_computation.2 | async-start | bytes 8388608
  5.5 75.0 %slice-start.1 = ((s8[7340032]{0:T(1024)(128)(4,1)}), s8[3145728]{0:T(1024)(128)(4,1)S(1)}, s32[]{:S(2)}) async-start(s8[7340032]{0:T(1024)(128)(4,1)} %bitcast.13), calls=%async_computation.3 | async-start | bytes 6291456
  5.5 75.0 %copy-start = (bf16[1,7168,512]{2,1,0:T(8,128)(2,1)S(1)}, bf16[1,7168,512]{2,1,0:T(8,128)(2,1)}, u32[]{:S(2)}) copy-start(bf16[1,7168,512]{2,1,0:T(8,128)(2,1)} %param.14) | copy-start | bytes 22020100
  80.4 9.0 %collective-permute-start = (bf16[768,3584]{1,0:T(8,128)(2,1)S(1)}, bf16[768,3584]{1,0:T(8,128)(2,1)S(1)}, u32[]{:S(2)}, u32[]{:S(2)}) collective-permute-start(bf16[768,3584]{1,0:T(8,128)(2,1)S(1)} %bitcast.23), channel_id=1, source_target_pairs={{0,32},{32,0},{64,96},{96,64},{1,33},{33,1},{65,97},{97,65},{2,34}... | collective-permute-start | bytes 16515080 | tf_op jit(solution)/shard_map/ppermute | solution.py:42
  99.9 5.5 %collective-permute-start.1 = (bf16[768,1792]{1,0:T(8,128)(2,1)S(1)}, bf16[768,1792]{1,0:T(8,128)(2,1)S(1)}, u32[]{:S(2)}, u32[]{:S(2)}) collective-permute-start(bf16[768,1792]{1,0:T(8,128)(2,1)S(1)} %get-tuple-element.24), channel_id=1, source_target_pairs={{0,32},{32,0},{64,96},{96,64},{1,33},{33,1},{65,97},{97,65},{2,34}... | collective-permute-start | bytes 8257544 | tf_op jit(solution)/shard_map/ppermute | solution.py:42
  146.5 3.9 %copy-start.1 = (bf16[128,7168]{1,0:T(8,128)(2,1)S(1)}, bf16[128,7168]{1,0:T(8,128)(2,1)}, u32[]{:S(2)}) copy-start(bf16[128,7168]{1,0:T(8,128)(2,1)} %tokens.3) | copy-start | bytes 5505028
  146.5 3.9 %copy-start.3 = (f32[7168]{0:T(1024)S(1)}, f32[7168]{0:T(1024)}, u32[]{:S(2)}) copy-start(f32[7168]{0:T(1024)} %param.10) | copy-start | bytes 86020
  146.5 13.8 %collective-permute-start.2 = (bf16[128,1792]{1,0:T(8,128)(2,1)S(1)}, bf16[128,1792]{1,0:T(8,128)(2,1)S(1)}, u32[]{:S(2)}, u32[]{:S(2)}) collective-permute-start(bf16[128,1792]{1,0:T(8,128)(2,1)S(1)} %token_sums.3.sent), channel_id=1, source_target_pairs={{0,64},{64,0},{32,96},{96,32},{1,65},{65,1},{33,97},{97,33},{2,66}... | collective-permute-start | bytes 1376264 | tf_op jit(solution)/shard_map/ppermute | solution.py:46
  150.4 9.9 %copy-start.2 = (bf16[128,7168]{1,0:T(8,128)(2,1)S(1)}, bf16[128,7168]{1,0:T(8,128)(2,1)}, u32[]{:S(2)}) copy-start(bf16[128,7168]{1,0:T(8,128)(2,1)} %cotangent.3) | copy-start | bytes 5505028
  151.4 1.3 collective-permute-start.3
  152.7 7.6 %collective-permute-start.4 = (f32[128,128]{1,0:T(8,128)S(1)}, f32[128,128]{1,0:T(8,128)S(1)}, u32[]{:S(2)}, u32[]{:S(2)}) collective-permute-start(f32[128,128]{1,0:T(8,128)S(1)} %add.4.own_product), channel_id=1, source_target_pairs={{0,64},{64,0},{32,96},{96,32},{1,65},{65,1},{33,97},{97,33},{2,66}... | collective-permute-start | bytes 196616 | tf_op jit(solution)/shard_map/ppermute | solution.py:46

commit v9 on v8

--- a/solution.py
+++ b/solution.py
@@ -342,10 +342,17 @@
     )(place, gather, rows)
 
 
+def diagonal(count):
+    shape = (count, count)
+    return lax.broadcasted_iota(jnp.int32, shape, 0) == lax.broadcasted_iota(jnp.int32, shape, 1)
+
+
 def product_kernel(place, kept, sent, own_tokens, other_tokens, own_gain, other_gain, product):
     part = kept[...] * (own_tokens[...].astype(F32) * own_gain[...])
     part = part + sent[...].astype(F32) * (other_tokens[...].astype(F32) * other_gain[...])
-    product[...] = jnp.broadcast_to(jnp.sum(part, axis=1, keepdims=True), product.shape)
+    column = jnp.sum(part, axis=1, keepdims=True)
+    row = jnp.sum(jnp.where(diagonal(part.shape[0]), column, 0.0), axis=0, keepdims=True)
+    product[...] = jnp.broadcast_to(row, product.shape)
 
 
 def row_products(place, kept, sent, tokens, gain):
@@ -360,12 +367,12 @@
 
     return pl.pallas_call(
         product_kernel,
-        out_shape=jax.ShapeDtypeStruct((count, LANES), F32),
+        out_shape=jax.ShapeDtypeStruct((8, count), F32),
         grid_spec=grid_of(
             (1,),
             [whole(kept.shape), whole(sent.shape)]
             + [quarter(count, False), quarter(count, True), quarter(1, False), quarter(1, True)],
-            whole((count, LANES)),
+            whole((8, count)),
         ),
         compiler_params=params(16),
         name="row_products",
@@ -374,7 +381,8 @@
 
 def final_kernel(width, place, kept, arrived, own_product, other_product, tokens, cotangent, gain, inverse, out):
     scale = inverse[...]
-    row_product = own_product[:, :1] + other_product[:, :1]
+    row = own_product[:1, :] + other_product[:1, :]
+    row_product = jnp.sum(jnp.where(diagonal(out.shape[0]), row, 0.0), axis=1, keepdims=True)
     grad = kept[...] + arrived[...].astype(F32)
     value = cotangent[...].astype(F32) + scale * gain[...] * grad
     out[...] = (value - tokens[...].astype(F32) * (scale * scale * scale * row_product / width)).astype(BF16)
@@ -421,9 +429,9 @@
     )
     rows, ids = lax.optimization_barrier((exchange(rows), ids))
     accs = project(place, rows, weights)
-    theirs, *grads = expert(place, core_swap(rows), weights, accs)
+    swapped, gather = lax.optimization_barrier((core_swap(rows), gather_matrix(ids, capacity, experts)))
+    theirs, *grads = expert(place, swapped, weights, accs)
     back = merge(mine_rows(place, grads, weights), core_swap(theirs))
-    back, gather = lax.optimization_barrier((back, gather_matrix(ids, capacity, experts)))
     back = exchange(back)
     sent = token_sums(place, gather, back, True, BF16)
     kept = token_sums(place, gather, back, False, F32)

time: 162 us -> 160 us (0.988)
  transfers between devices with their start and end apart: 5 -> 5, of which waited for: 3 -> 4; matrix products, arithmetic and copies ran while one was open for 0% -> 0% of each run, Pallas kernels for 9% -> 9%
where the time goes in v9:
time: 160 us
  blocking collectives  114 us (71%)
  Pallas kernels  33.2 us (21%)
  waiting for transfers between devices  8.58 us (5%)
  starting transfers between devices  4.08 us (3%)
    all_to_all x2, blocking collectives, exchange(): lax.all_to_all(shaped, 'expert', split_axis=0, concat_axis=0, tiled=True)  114 us
    pallas_call x1, Pallas kernels, expert(): pl.pallas_call(expert_kernel, out_shape=(jax.ShapeDtypeStruct((height, we...  10.4 us
    pallas_call x1, Pallas kernels, project(): pl.pallas_call(project_kernel, out_shape=(acc,) * 3, grid_spec=grid_of((1...  6.81 us
    pallas_call x1, Pallas kernels, make_message(): pl.pallas_call(functools.partial(message_kernel, capacity), out_shape=(ja...  5.39 us
    ppermute x2, waiting for transfers between devices, high_swap(): return lax.ppermute(array, 'pipe', HIGH_SWAP)  5.37 us
    pallas_call x1, Pallas kernels, mine_rows(): pl.pallas_call(mine_kernel, out_shape=jax.ShapeDtypeStruct((2 * grads[0]....  4.01 us
    ppermute x2, starting transfers between devices, high_swap(): return lax.ppermute(array, 'pipe', HIGH_SWAP)  3.6 us
    ppermute x3, waiting for transfers between devices, core_swap(): return lax.ppermute(array, 'pipe', CORE_SWAP)  3.21 us
  transfers between devices with their start and end apart: 5, of which 4 were waited for; matrix products, arithmetic and copies ran while one was open for 0% of the time, Pallas kernels for 9%

profile of v9, /device:TPU:0, one launch (start us, length us, event | category | flops | bytes accessed | tf_op | source)
XLA Modules:
  0.0 160.1 jit_solution(464242308604947272)
XLA Ops:
  0.0 0.1 pad_add_fusion.place
  0.1 5.4 %message.1 = (bf16[768,3584]{1,0:T(8,128)(2,1)S(1)}, f32[128,1]{1,0:T(8,128)S(1)}) custom-call(s32[3]{0:T(128)S(1)} %pad_add_fusion.place, bf16[128,7168]{1,0:T(8,128)(2,1)} %tokens.3, bf16[128,7168]{1,0:T(8,128)(2,1)} %cotangent.3, f32[1,7168]{1,0:T(1,128)} %bitcast.27, s32[2,128]{1,0:T(2,128)} %bitcast.33, f32[2,128]{1,0:T(2,128)} %bitcast.35), custom_call_target="tpu_custom_call" | custom-call | tf_op jit(solution)/shard_map/message/pallas_call | solution.py:111
  5.5 0.0 slice-start.1
  5.5 0.0 copy-start
  5.5 74.9 %all_to_all.10 = bf16[32,24,3584]{2,1,0:T(8,128)(2,1)S(1)} all-to-all(bf16[32,24,3584]{2,1,0:T(8,128)(2,1)S(1)} %bitcast.26), channel_id=1, replica_groups=mesh['pipe'=4,'expert'=32] {'expert'}, dimensions={0} | all-to-all | bytes 11010048 | tf_op jit(solution)/shard_map/all_to_all | solution.py:52
  80.4 1.0 gather_matrix.1.gather
  81.5 6.8 %project.1 = (f32[384,512]{1,0:T(8,128)S(1)}, f32[384,512]{1,0:T(8,128)S(1)}, f32[384,512]{1,0:T(8,128)S(1)}) custom-call(s32[3]{0:T(128)S(1)} %pad_add_fusion.place, bf16[768,3584]{1,0:T(8,128)(2,1)S(1)} %bitcast.24, bf16[7168,512]{1,0:T(8,128)(2,1)S(1)} %bitcast.15, bf16[7168,512]{1,0:T(8,128)(2,1)S(1)} %bitcast.18, bf16[512,7168]{1,0:T(8,128)(2,1)} %bitcast.31), custom_call_target="tpu_custom_call" | custom-call | tf_op jit(solution)/shard_map/project/pallas_call | solution.py:249
  88.4 1.1 collective-permute-done.rows
  89.5 10.4 %expert.1 = (bf16[768,1792]{1,0:T(8,128)(2,1)S(1)}, bf16[384,512]{1,0:T(8,128)(2,1)S(1)}, bf16[384,512]{1,0:T(8,128)(2,1)S(1)}) custom-call(s32[3]{0:T(128)S(1)} %pad_add_fusion.place, bf16[768,3584]{1,0:T(8,128)(2,1)S(1)} %collective-permute-done.rows, bf16[7168,512]{1,0:T(8,128)(2,1)S(1)} %bitcast.16, bf16[7168,512]{1,0:T(8,128)(2,1)S(1)} %bitcast.19, ...), custom_call_target="tpu_custom_call" | custom-call | tf_op jit(solution)/shard_map/expert/pallas_call | solution.py:279
  99.9 0.4 collective-permute-start.1
  100.3 4.0 %mine_rows.1.mine = bf16[768,1792]{1,0:T(8,128)(2,1)S(1)} custom-call(s32[3]{0:T(128)S(1)} %pad_add_fusion.place, bf16[384,512]{1,0:T(8,128)(2,1)S(1)} %get-tuple-element.25.grad_gate, bf16[384,512]{1,0:T(8,128)(2,1)S(1)} %get-tuple-element.26.grad_up, bf16[7168,512]{1,0:T(8,128)(2,1)S(1)} %bitcast.17, bf16[7168,512]{1,0:T(8,128)(2,1)S(1)} %bitcast.20), custom_call_target="tpu_custom_call" | custom-call | tf_op jit(solution)/shard_map/mine_rows/pallas_call | solution.py:300
  104.4 0.9 collective-permute-done.1.other
  105.3 0.7 merge.1
  106.0 39.0 %all_to_all.11 = bf16[32,24,1792]{2,1,0:T(8,128)(2,1)S(1)} all-to-all(bf16[32,24,1792]{2,1,0:T(8,128)(2,1)S(1)} %bitcast.25), channel_id=1, replica_groups=mesh['pipe'=4,'expert'=32] {'expert'}, dimensions={0} | all-to-all | bytes 5505024 | tf_op jit(solution)/shard_map/all_to_all | solution.py:52
  145.0 1.1 token_sums.3.sent
  146.1 0.0 copy-start.1
  146.1 2.8 %collective-permute-start.2 = (bf16[128,1792]{1,0:T(8,128)(2,1)S(1)}, bf16[128,1792]{1,0:T(8,128)(2,1)S(1)}, u32[]{:S(2)}, u32[]{:S(2)}) collective-permute-start(bf16[128,1792]{1,0:T(8,128)(2,1)S(1)} %token_sums.3.sent), channel_id=1, source_target_pairs={{0,64},{64,0},{32,96},{96,32},{1,65},{65,1},{33,97},{97,33},{2,66}... | collective-permute-start | bytes 1376264 | tf_op jit(solution)/shard_map/ppermute | solution.py:46
  149.0 1.1 token_sums.2.kept
  150.1 0.9 row_products.1
  151.0 0.0 collective-permute-start.3
  151.1 1.2 collective-permute-done.3
  152.2 0.8 collective-permute-start.4
  153.0 5.4 %collective-permute-done.4.other_product = f32[8,128]{1,0:T(8,128)S(1)} collective-permute-done((f32[8,128]{1,0:T(8,128)S(1)}, f32[8,128]{1,0:T(8,128)S(1)}, u32[]{:S(2)}, u32[]{:S(2)}) %collective-permute-start.4) | collective-permute-done | bytes 4128 | tf_op jit(solution)/shard_map/ppermute | solution.py:46
  158.4 1.7 %final.1 = bf16[128,1792]{1,0:T(8,128)(2,1)} custom-call(s32[3]{0:T(128)S(1)} %pad_add_fusion.place, f32[128,1792]{1,0:T(8,128)S(1)} %token_sums.2.kept, bf16[128,1792]{1,0:T(8,128)(2,1)S(1)} %collective-permute-done.2.arrived, f32[8,128]{1,0:T(8,128)S(1)} %add.4.own_product, f32[8,128]{1,0:T(8,128)S(1)} %collective-permute-done.4.other_product, ...), custom_call_target="tpu_custom_call" | custom-call | tf_op jit(solution)/shard_map/final/pallas_call | solution.py:395
  (13 shorter events, 0.0 us)
Async XLA Ops:
  0.1 81.4 %slice-start = ((s8[7340032]{0:T(1024)(128)(4,1)}), s8[4194304]{0:T(1024)(128)(4,1)S(1)}, s32[]{:S(2)}) async-start(s8[7340032]{0:T(1024)(128)(4,1)} %bitcast.13), calls=%async_computation.2 | async-start | bytes 8388608
  5.5 76.0 %slice-start.1 = ((s8[7340032]{0:T(1024)(128)(4,1)}), s8[3145728]{0:T(1024)(128)(4,1)S(1)}, s32[]{:S(2)}) async-start(s8[7340032]{0:T(1024)(128)(4,1)} %bitcast.13), calls=%async_computation.3 | async-start | bytes 6291456
  5.5 76.0 %copy-start = (bf16[1,7168,512]{2,1,0:T(8,128)(2,1)S(1)}, bf16[1,7168,512]{2,1,0:T(8,128)(2,1)}, u32[]{:S(2)}) copy-start(bf16[1,7168,512]{2,1,0:T(8,128)(2,1)} %param.14) | copy-start | bytes 22020100
  80.4 9.0 %collective-permute-start = (bf16[768,3584]{1,0:T(8,128)(2,1)S(1)}, bf16[768,3584]{1,0:T(8,128)(2,1)S(1)}, u32[]{:S(2)}, u32[]{:S(2)}) collective-permute-start(bf16[768,3584]{1,0:T(8,128)(2,1)S(1)} %bitcast.23), channel_id=1, source_target_pairs={{0,32},{32,0},{64,96},{96,64},{1,33},{33,1},{65,97},{97,65},{2,34}... | collective-permute-start | bytes 16515080 | tf_op jit(solution)/shard_map/ppermute | solution.py:42
  99.9 5.4 %collective-permute-start.1 = (bf16[768,1792]{1,0:T(8,128)(2,1)S(1)}, bf16[768,1792]{1,0:T(8,128)(2,1)S(1)}, u32[]{:S(2)}, u32[]{:S(2)}) collective-permute-start(bf16[768,1792]{1,0:T(8,128)(2,1)S(1)} %get-tuple-element.27), channel_id=1, source_target_pairs={{0,32},{32,0},{64,96},{96,64},{1,33},{33,1},{65,97},{97,65},{2,34}... | collective-permute-start | bytes 8257544 | tf_op jit(solution)/shard_map/ppermute | solution.py:42
  146.1 3.9 %copy-start.1 = (bf16[128,7168]{1,0:T(8,128)(2,1)S(1)}, bf16[128,7168]{1,0:T(8,128)(2,1)}, u32[]{:S(2)}) copy-start(bf16[128,7168]{1,0:T(8,128)(2,1)} %tokens.3) | copy-start | bytes 5505028
  146.1 3.9 %copy-start.3 = (f32[7168]{0:T(1024)S(1)}, f32[7168]{0:T(1024)}, u32[]{:S(2)}) copy-start(f32[7168]{0:T(1024)} %param.10) | copy-start | bytes 86020
  146.1 12.2 %collective-permute-start.2 = (bf16[128,1792]{1,0:T(8,128)(2,1)S(1)}, bf16[128,1792]{1,0:T(8,128)(2,1)S(1)}, u32[]{:S(2)}, u32[]{:S(2)}) collective-permute-start(bf16[128,1792]{1,0:T(8,128)(2,1)S(1)} %token_sums.3.sent), channel_id=1, source_target_pairs={{0,64},{64,0},{32,96},{96,32},{1,65},{65,1},{33,97},{97,33},{2,66}... | collective-permute-start | bytes 1376264 | tf_op jit(solution)/shard_map/ppermute | solution.py:46
  150.1 8.3 %copy-start.2 = (bf16[128,7168]{1,0:T(8,128)(2,1)S(1)}, bf16[128,7168]{1,0:T(8,128)(2,1)}, u32[]{:S(2)}) copy-start(bf16[128,7168]{1,0:T(8,128)(2,1)} %cotangent.3) | copy-start | bytes 5505028
  151.0 1.2 collective-permute-start.3
  152.2 6.2 %collective-permute-start.4 = (f32[8,128]{1,0:T(8,128)S(1)}, f32[8,128]{1,0:T(8,128)S(1)}, u32[]{:S(2)}, u32[]{:S(2)}) collective-permute-start(f32[8,128]{1,0:T(8,128)S(1)} %add.4.own_product), channel_id=1, source_target_pairs={{0,64},{64,0},{32,96},{96,32},{1,65},{65,1},{33,97},{97,33},{2,66}... | collective-permute-start | bytes 12296 | tf_op jit(solution)/shard_map/ppermute | solution.py:46

commit v10 on v9

--- a/solution.py
+++ b/solution.py
@@ -52,17 +52,24 @@
     return lax.all_to_all(shaped, "expert", split_axis=0, concat_axis=0, tiled=True).reshape(rows.shape)
 
 
-def message_kernel(capacity, place, tokens, cotangent, gain, ids, weights, rows, inverse, tokens_in, cotangent_in, select, factors, sems):
+def message_kernel(capacity, place, tokens, cotangent, all_gain, all_ids, all_weights, rows, inverse, tokens_in, cotangent_in, gain, ids, weights, select, factors, sems):
     top, count = ids.shape
     half = rows.shape[1]
     start = place[0] * half
     own_half = pl.ds(pl.multiple_of(start, half), half)
+    small = (
+        pltpu.make_async_copy(all_ids, ids, sems.at[2]),
+        pltpu.make_async_copy(all_weights, weights, sems.at[3]),
+        pltpu.make_async_copy(all_gain, gain, sems.at[4]),
+    )
     copies = (
         pltpu.make_async_copy(tokens, tokens_in, sems.at[0]),
         pltpu.make_async_copy(cotangent.at[:, own_half], cotangent_in, sems.at[1]),
     )
-    for copy in copies:
+    for copy in small + copies:
         copy.start()
+    for copy in small:
+        copy.wait()
     height = select.shape[0]
     experts = height // (2 * capacity)
     expert_of = lax.broadcasted_iota(jnp.int32, (experts, count), 0)
@@ -113,14 +120,17 @@
         out_shape=(jax.ShapeDtypeStruct((height, half), BF16), jax.ShapeDtypeStruct((count, 1), F32)),
         grid_spec=grid_of(
             (1,),
-            [any_space, any_space, whole(gain.shape), whole(ids.shape), whole(weights.shape)],
-            (resident, whole((count, 1))),
+            [any_space] * 5,
+            (resident, resident),
             [
                 pltpu.VMEM((count, width), BF16),
                 pltpu.VMEM((count, half), BF16),
+                pltpu.VMEM(gain.shape, F32),
+                pltpu.VMEM(ids.shape, jnp.int32),
+                pltpu.VMEM(weights.shape, F32),
                 pltpu.VMEM((height, 2 * count), BF16),
                 pltpu.VMEM((height, LANES), F32),
-                pltpu.SemaphoreType.DMA((2,)),
+                pltpu.SemaphoreType.DMA((5,)),
             ],
         ),
         compiler_params=params(24),
@@ -324,19 +334,21 @@
     )(mine, other)
 
 
-def sums_kernel(place, gather, rows, out):
-    out[...] = jnp.dot(gather[...], rows[...], preferred_element_type=F32).astype(out.dtype)
+def sums_kernel(other, place, gather, rows, out):
+    count = out.shape[0]
+    high = 1 - place[1] if other else place[1]
+    mine = pl.ds(pl.multiple_of(high * count, count), count)
+    out[...] = jnp.dot(gather[mine, :], rows[...], preferred_element_type=F32).astype(out.dtype)
 
 
 def token_sums(place, gather, rows, other, kind):
     count = gather.shape[0] // 2
-    height, columns = rows.shape
-    resident = pl.BlockSpec(memory_space=pltpu.VMEM)
-    mine = pl.BlockSpec((count, height), lambda i, place: (1 - place[1] if other else place[1], 0))
-    return pl.pallas_call(
-        sums_kernel,
+    columns = rows.shape[1]
+    resident = pl.BlockSpec(memory_space=pltpu.VMEM)
+    return pl.pallas_call(
+        functools.partial(sums_kernel, other),
         out_shape=jax.ShapeDtypeStruct((count, columns), kind),
-        grid_spec=grid_of((1,), [mine, resident], resident),
+        grid_spec=grid_of((1,), [resident, resident], resident),
         compiler_params=params(16),
         name="token_sums",
     )(place, gather, rows)
@@ -379,31 +391,28 @@
     )(place, kept, sent, tokens, tokens, gain, gain)
 
 
-def final_kernel(width, place, kept, arrived, own_product, other_product, tokens, cotangent, gain, inverse, out):
+def final_kernel(place, kept, arrived, own_product, other_product, tokens, cotangent, gain, inverse, out):
+    count, columns = out.shape
+    own = pl.ds(pl.multiple_of(place[2] * columns, LANES), columns)
     scale = inverse[...]
     row = own_product[:1, :] + other_product[:1, :]
-    row_product = jnp.sum(jnp.where(diagonal(out.shape[0]), row, 0.0), axis=1, keepdims=True)
+    row_product = jnp.sum(jnp.where(diagonal(count), row, 0.0), axis=1, keepdims=True)
     grad = kept[...] + arrived[...].astype(F32)
-    value = cotangent[...].astype(F32) + scale * gain[...] * grad
-    out[...] = (value - tokens[...].astype(F32) * (scale * scale * scale * row_product / width)).astype(BF16)
-
-
-def final(place, kept, arrived, own_product, other_product, tokens, cotangent, gain, inverse):
-    count, width = tokens.shape
-    columns = width // 4
-    quarter = lambda height: pl.BlockSpec((height, columns), lambda i, place: (0, place[2]))
-    return pl.pallas_call(
-        functools.partial(final_kernel, width),
+    value = cotangent[:, own].astype(F32) + scale * gain[:, own] * grad
+    share = scale * scale * scale * row_product / tokens.shape[1]
+    out[...] = (value - tokens[:, own].astype(F32) * share).astype(BF16)
+
+
+def final(place, *arrays):
+    count, columns = arrays[0].shape
+    resident = pl.BlockSpec(memory_space=pltpu.VMEM)
+    return pl.pallas_call(
+        final_kernel,
         out_shape=jax.ShapeDtypeStruct((count, columns), BF16),
-        grid_spec=grid_of(
-            (1,),
-            [whole(array.shape) for array in (kept, arrived, own_product, other_product)]
-            + [quarter(count), quarter(count), quarter(1), whole(inverse.shape)],
-            whole((count, columns)),
-        ),
+        grid_spec=grid_of((1,), [resident] * len(arrays), whole((count, columns))),
         compiler_params=params(16),
         name="final",
-    )(place, kept, arrived, own_product, other_product, tokens, cotangent, gain, inverse)
+    )(place, *arrays)
 
 
 def body(tokens, cotangent, norm_gain, expert_ids, gate_weights, w_gate, w_up, w_down):

time: 160 us -> 160 us (level)
  no operation moved by 1% of the time
where the time goes in v10:
time: 160 us; the launch traced here: 159 us
  blocking collectives  114 us (71%)
  Pallas kernels  32.5 us (20%)
  waiting for transfers between devices  8.57 us (5%)
  starting transfers between devices  4.09 us (3%)
    all_to_all x2, blocking collectives, exchange(): lax.all_to_all(shaped, 'expert', split_axis=0, concat_axis=0, tiled=True)  114 us
    pallas_call x1, Pallas kernels, expert(): pl.pallas_call(expert_kernel, out_shape=(jax.ShapeDtypeStruct((height, we...  10.4 us
    pallas_call x1, Pallas kernels, project(): pl.pallas_call(project_kernel, out_shape=(acc,) * 3, grid_spec=grid_of((1...  6.82 us
    ppermute x2, waiting for transfers between devices, high_swap(): return lax.ppermute(array, 'pipe', HIGH_SWAP)  5.38 us
    pallas_call x1, Pallas kernels, make_message(): pl.pallas_call(functools.partial(message_kernel, capacity), out_shape=(ja...  4.7 us
    pallas_call x1, Pallas kernels, mine_rows(): pl.pallas_call(mine_kernel, out_shape=jax.ShapeDtypeStruct((2 * grads[0]....  4.02 us
    ppermute x2, starting transfers between devices, high_swap(): return lax.ppermute(array, 'pipe', HIGH_SWAP)  3.6 us
  transfers between devices with their start and end apart: 5, of which 4 were waited for; matrix products, arithmetic and copies ran while one was open for 0% of the time, Pallas kernels for 9%

profile of v10, /device:TPU:0, one launch (start us, length us, event | category | flops | bytes accessed | tf_op | source)
XLA Modules:
  0.0 159.4 jit_solution(6786360239306797018)
XLA Ops:
  0.0 0.1 pad_add_fusion.place
  0.1 4.7 %message.1 = (bf16[768,3584]{1,0:T(8,128)(2,1)S(1)}, f32[128,1]{1,0:T(8,128)S(1)}) custom-call(s32[3]{0:T(128)S(1)} %pad_add_fusion.place, bf16[128,7168]{1,0:T(8,128)(2,1)} %tokens.3, bf16[128,7168]{1,0:T(8,128)(2,1)} %cotangent.3, f32[1,7168]{1,0:T(1,128)} %bitcast.27, s32[2,128]{1,0:T(2,128)} %bitcast.33, f32[2,128]{1,0:T(2,128)} %bitcast.35), custom_call_target="tpu_custom_call" | custom-call | tf_op jit(solution)/shard_map/message/pallas_call | solution.py:118
  4.8 0.0 slice-start.1
  4.8 0.0 copy-start
  4.8 74.9 %all_to_all.10 = bf16[32,24,3584]{2,1,0:T(8,128)(2,1)S(1)} all-to-all(bf16[32,24,3584]{2,1,0:T(8,128)(2,1)S(1)} %bitcast.26), channel_id=1, replica_groups=mesh['pipe'=4,'expert'=32] {'expert'}, dimensions={0} | all-to-all | bytes 11010048 | tf_op jit(solution)/shard_map/all_to_all | solution.py:52
  79.8 1.0 gather_matrix.1.gather
  80.8 6.8 %project.1 = (f32[384,512]{1,0:T(8,128)S(1)}, f32[384,512]{1,0:T(8,128)S(1)}, f32[384,512]{1,0:T(8,128)S(1)}) custom-call(s32[3]{0:T(128)S(1)} %pad_add_fusion.place, bf16[768,3584]{1,0:T(8,128)(2,1)S(1)} %bitcast.24, bf16[7168,512]{1,0:T(8,128)(2,1)S(1)} %bitcast.15, bf16[7168,512]{1,0:T(8,128)(2,1)S(1)} %bitcast.18, bf16[512,7168]{1,0:T(8,128)(2,1)} %bitcast.31), custom_call_target="tpu_custom_call" | custom-call | tf_op jit(solution)/shard_map/project/pallas_call | solution.py:259
  87.7 1.1 collective-permute-done.rows
  88.8 10.4 %expert.1 = (bf16[768,1792]{1,0:T(8,128)(2,1)S(1)}, bf16[384,512]{1,0:T(8,128)(2,1)S(1)}, bf16[384,512]{1,0:T(8,128)(2,1)S(1)}) custom-call(s32[3]{0:T(128)S(1)} %pad_add_fusion.place, bf16[768,3584]{1,0:T(8,128)(2,1)S(1)} %collective-permute-done.rows, bf16[7168,512]{1,0:T(8,128)(2,1)S(1)} %bitcast.16, bf16[7168,512]{1,0:T(8,128)(2,1)S(1)} %bitcast.19, ...), custom_call_target="tpu_custom_call" | custom-call | tf_op jit(solution)/shard_map/expert/pallas_call | solution.py:289
  99.2 0.4 collective-permute-start.1
  99.7 4.0 %mine_rows.1.mine = bf16[768,1792]{1,0:T(8,128)(2,1)S(1)} custom-call(s32[3]{0:T(128)S(1)} %pad_add_fusion.place, bf16[384,512]{1,0:T(8,128)(2,1)S(1)} %get-tuple-element.25.grad_gate, bf16[384,512]{1,0:T(8,128)(2,1)S(1)} %get-tuple-element.26.grad_up, bf16[7168,512]{1,0:T(8,128)(2,1)S(1)} %bitcast.17, bf16[7168,512]{1,0:T(8,128)(2,1)S(1)} %bitcast.20), custom_call_target="tpu_custom_call" | custom-call | tf_op jit(solution)/shard_map/mine_rows/pallas_call | solution.py:310
  103.7 0.9 collective-permute-done.1.other
  104.6 0.7 merge.1
  105.3 39.0 %all_to_all.11 = bf16[32,24,1792]{2,1,0:T(8,128)(2,1)S(1)} all-to-all(bf16[32,24,1792]{2,1,0:T(8,128)(2,1)S(1)} %bitcast.25), channel_id=1, replica_groups=mesh['pipe'=4,'expert'=32] {'expert'}, dimensions={0} | all-to-all | bytes 5505024 | tf_op jit(solution)/shard_map/all_to_all | solution.py:52
  144.3 1.1 token_sums.3.sent
  145.4 0.0 copy-start.1
  145.5 2.8 %collective-permute-start.2 = (bf16[128,1792]{1,0:T(8,128)(2,1)S(1)}, bf16[128,1792]{1,0:T(8,128)(2,1)S(1)}, u32[]{:S(2)}, u32[]{:S(2)}) collective-permute-start(bf16[128,1792]{1,0:T(8,128)(2,1)S(1)} %token_sums.3.sent), channel_id=1, source_target_pairs={{0,64},{64,0},{32,96},{96,32},{1,65},{65,1},{33,97},{97,33},{2,66}... | collective-permute-start | bytes 1376264 | tf_op jit(solution)/shard_map/ppermute | solution.py:46
  148.3 1.1 token_sums.2.kept
  149.4 0.9 row_products.1
  150.3 0.0 collective-permute-start.3
  150.4 1.2 collective-permute-done.3
  151.5 0.8 collective-permute-start.4
  152.3 5.4 %collective-permute-done.4.other_product = f32[8,128]{1,0:T(8,128)S(1)} collective-permute-done((f32[8,128]{1,0:T(8,128)S(1)}, f32[8,128]{1,0:T(8,128)S(1)}, u32[]{:S(2)}, u32[]{:S(2)}) %collective-permute-start.4) | collective-permute-done | bytes 4128 | tf_op jit(solution)/shard_map/ppermute | solution.py:46
  157.7 1.7 %final.1 = bf16[128,1792]{1,0:T(8,128)(2,1)} custom-call(s32[3]{0:T(128)S(1)} %pad_add_fusion.place, f32[128,1792]{1,0:T(8,128)S(1)} %token_sums.2.kept, bf16[128,1792]{1,0:T(8,128)(2,1)S(1)} %collective-permute-done.2.arrived, f32[8,128]{1,0:T(8,128)S(1)} %add.4.own_product, f32[8,128]{1,0:T(8,128)S(1)} %collective-permute-done.4.other_product, ...), custom_call_target="tpu_custom_call" | custom-call | tf_op jit(solution)/shard_map/final/pallas_call | solution.py:409
  (13 shorter events, 0.0 us)
Async XLA Ops:
  0.1 80.7 %slice-start = ((s8[7340032]{0:T(1024)(128)(4,1)}), s8[4194304]{0:T(1024)(128)(4,1)S(1)}, s32[]{:S(2)}) async-start(s8[7340032]{0:T(1024)(128)(4,1)} %bitcast.13), calls=%async_computation.2 | async-start | bytes 8388608
  4.8 76.0 %slice-start.1 = ((s8[7340032]{0:T(1024)(128)(4,1)}), s8[3145728]{0:T(1024)(128)(4,1)S(1)}, s32[]{:S(2)}) async-start(s8[7340032]{0:T(1024)(128)(4,1)} %bitcast.13), calls=%async_computation.3 | async-start | bytes 6291456
  4.8 76.0 %copy-start = (bf16[1,7168,512]{2,1,0:T(8,128)(2,1)S(1)}, bf16[1,7168,512]{2,1,0:T(8,128)(2,1)}, u32[]{:S(2)}) copy-start(bf16[1,7168,512]{2,1,0:T(8,128)(2,1)} %param.14) | copy-start | bytes 22020100
  79.8 9.0 %collective-permute-start = (bf16[768,3584]{1,0:T(8,128)(2,1)S(1)}, bf16[768,3584]{1,0:T(8,128)(2,1)S(1)}, u32[]{:S(2)}, u32[]{:S(2)}) collective-permute-start(bf16[768,3584]{1,0:T(8,128)(2,1)S(1)} %bitcast.23), channel_id=1, source_target_pairs={{0,32},{32,0},{64,96},{96,64},{1,33},{33,1},{65,97},{97,65},{2,34}... | collective-permute-start | bytes 16515080 | tf_op jit(solution)/shard_map/ppermute | solution.py:42
  99.2 5.4 %collective-permute-start.1 = (bf16[768,1792]{1,0:T(8,128)(2,1)S(1)}, bf16[768,1792]{1,0:T(8,128)(2,1)S(1)}, u32[]{:S(2)}, u32[]{:S(2)}) collective-permute-start(bf16[768,1792]{1,0:T(8,128)(2,1)S(1)} %get-tuple-element.27), channel_id=1, source_target_pairs={{0,32},{32,0},{64,96},{96,64},{1,33},{33,1},{65,97},{97,65},{2,34}... | collective-permute-start | bytes 8257544 | tf_op jit(solution)/shard_map/ppermute | solution.py:42
  145.4 3.9 %copy-start.1 = (bf16[128,7168]{1,0:T(8,128)(2,1)S(1)}, bf16[128,7168]{1,0:T(8,128)(2,1)}, u32[]{:S(2)}) copy-start(bf16[128,7168]{1,0:T(8,128)(2,1)} %tokens.3) | copy-start | bytes 5505028
  145.4 3.9 %copy-start.3 = (f32[7168]{0:T(1024)S(1)}, f32[7168]{0:T(1024)}, u32[]{:S(2)}) copy-start(f32[7168]{0:T(1024)} %param.10) | copy-start | bytes 86020
  145.5 12.3 %collective-permute-start.2 = (bf16[128,1792]{1,0:T(8,128)(2,1)S(1)}, bf16[128,1792]{1,0:T(8,128)(2,1)S(1)}, u32[]{:S(2)}, u32[]{:S(2)}) collective-permute-start(bf16[128,1792]{1,0:T(8,128)(2,1)S(1)} %token_sums.3.sent), channel_id=1, source_target_pairs={{0,64},{64,0},{32,96},{96,32},{1,65},{65,1},{33,97},{97,33},{2,66}... | collective-permute-start | bytes 1376264 | tf_op jit(solution)/shard_map/ppermute | solution.py:46
  149.4 8.3 %copy-start.2 = (bf16[128,7168]{1,0:T(8,128)(2,1)S(1)}, bf16[128,7168]{1,0:T(8,128)(2,1)}, u32[]{:S(2)}) copy-start(bf16[128,7168]{1,0:T(8,128)(2,1)} %cotangent.3) | copy-start | bytes 5505028
  150.3 1.2 collective-permute-start.3
  151.5 6.2 %collective-permute-start.4 = (f32[8,128]{1,0:T(8,128)S(1)}, f32[8,128]{1,0:T(8,128)S(1)}, u32[]{:S(2)}, u32[]{:S(2)}) collective-permute-start(f32[8,128]{1,0:T(8,128)S(1)} %add.4.own_product), channel_id=1, source_target_pairs={{0,64},{64,0},{32,96},{96,32},{1,65},{65,1},{33,97},{97,33},{2,66}... | collective-permute-start | bytes 12296 | tf_op jit(solution)/shard_map/ppermute | solution.py:46

commit v11 on v10

--- a/solution.py
+++ b/solution.py
@@ -321,14 +321,12 @@
 
 
 def merge(mine, other):
-    rows, columns = mine.shape
-    spec = pl.BlockSpec((rows // 4, columns), lambda i: (i, 0))
+    resident = pl.BlockSpec(memory_space=pltpu.VMEM)
     return pl.pallas_call(
         merge_kernel,
-        out_shape=jax.ShapeDtypeStruct((rows, columns), BF16),
-        grid=(4,),
-        in_specs=[spec, spec],
-        out_specs=spec,
+        out_shape=jax.ShapeDtypeStruct(mine.shape, BF16),
+        in_specs=[resident, resident],
+        out_specs=resident,
         compiler_params=params(12),
         name="merge",
     )(mine, other)
@@ -391,16 +389,24 @@
     )(place, kept, sent, tokens, tokens, gain, gain)
 
 
-def final_kernel(place, kept, arrived, own_product, other_product, tokens, cotangent, gain, inverse, out):
+def final_kernel(place, kept, arrived, own_product, other_product, tokens, cotangent, gain, inverse, out, result, sems):
     count, columns = out.shape
-    own = pl.ds(pl.multiple_of(place[2] * columns, LANES), columns)
+    half = columns // 2
     scale = inverse[...]
     row = own_product[:1, :] + other_product[:1, :]
     row_product = jnp.sum(jnp.where(diagonal(count), row, 0.0), axis=1, keepdims=True)
-    grad = kept[...] + arrived[...].astype(F32)
-    value = cotangent[:, own].astype(F32) + scale * gain[:, own] * grad
     share = scale * scale * scale * row_product / tokens.shape[1]
-    out[...] = (value - tokens[:, own].astype(F32) * share).astype(BF16)
+    copies = []
+    for number in range(2):
+        part = slice(number * half, (number + 1) * half)
+        own = pl.ds(pl.multiple_of(place[2] * columns + number * half, LANES), half)
+        grad = kept[:, part] + arrived[:, part].astype(F32)
+        value = cotangent[:, own].astype(F32) + scale * gain[:, own] * grad
+        result[:, part] = (value - tokens[:, own].astype(F32) * share).astype(BF16)
+        copies.append(pltpu.make_async_copy(result.at[:, part], out.at[:, part], sems.at[number]))
+        copies[number].start()
+    for copy in copies:
+        copy.wait()
 
 
 def final(place, *arrays):
@@ -409,7 +415,12 @@
     return pl.pallas_call(
         final_kernel,
         out_shape=jax.ShapeDtypeStruct((count, columns), BF16),
-        grid_spec=grid_of((1,), [resident] * len(arrays), whole((count, columns))),
+        grid_spec=grid_of(
+            (1,),
+            [resident] * len(arrays),
+            pl.BlockSpec(memory_space=pl.ANY),
+            [pltpu.VMEM((count, columns), BF16), pltpu.SemaphoreType.DMA((2,))],
+        ),
         compiler_params=params(16),
         name="final",
     )(place, *arrays)

time: 160 us -> 160 us (level)
  no operation moved by 1% of the time
where the time goes in v11:
time: 160 us
  blocking collectives  114 us (71%)
  Pallas kernels  32.5 us (20%)
  waiting for transfers between devices  8.58 us (5%)
  starting transfers between devices  4.08 us (3%)
    all_to_all x2, blocking collectives, exchange(): lax.all_to_all(shaped, 'expert', split_axis=0, concat_axis=0, tiled=True)  114 us
    pallas_call x1, Pallas kernels, expert(): pl.pallas_call(expert_kernel, out_shape=(jax.ShapeDtypeStruct((height, we...  10.4 us
    pallas_call x1, Pallas kernels, project(): pl.pallas_call(project_kernel, out_shape=(acc,) * 3, grid_spec=grid_of((1...  6.82 us
    ppermute x2, waiting for transfers between devices, high_swap(): return lax.ppermute(array, 'pipe', HIGH_SWAP)  5.38 us
    pallas_call x1, Pallas kernels, make_message(): pl.pallas_call(functools.partial(message_kernel, capacity), out_shape=(ja...  4.7 us
    pallas_call x1, Pallas kernels, mine_rows(): pl.pallas_call(mine_kernel, out_shape=jax.ShapeDtypeStruct((2 * grads[0]....  4.02 us
    ppermute x2, starting transfers between devices, high_swap(): return lax.ppermute(array, 'pipe', HIGH_SWAP)  3.6 us
  transfers between devices with their start and end apart: 5, of which 4 were waited for; matrix products, arithmetic and copies ran while one was open for 0% of the time, Pallas kernels for 9%

profile of v11, /device:TPU:0, one launch (start us, length us, event | category | flops | bytes accessed | tf_op | source)
XLA Modules:
  0.0 159.6 jit_solution(15205147850119779940)
XLA Ops:
  0.0 0.1 pad_add_fusion.place
  0.1 4.7 %message.1 = (bf16[768,3584]{1,0:T(8,128)(2,1)S(1)}, f32[128,1]{1,0:T(8,128)S(1)}) custom-call(s32[3]{0:T(128)S(1)} %pad_add_fusion.place, bf16[128,7168]{1,0:T(8,128)(2,1)} %tokens.3, bf16[128,7168]{1,0:T(8,128)(2,1)} %cotangent.3, f32[1,7168]{1,0:T(1,128)} %bitcast.27, s32[2,128]{1,0:T(2,128)} %bitcast.33, f32[2,128]{1,0:T(2,128)} %bitcast.35), custom_call_target="tpu_custom_call" | custom-call | tf_op jit(solution)/shard_map/message/pallas_call | solution.py:118
  4.8 0.0 slice-start.1
  4.8 0.0 copy-start
  4.8 74.9 %all_to_all.10 = bf16[32,24,3584]{2,1,0:T(8,128)(2,1)S(1)} all-to-all(bf16[32,24,3584]{2,1,0:T(8,128)(2,1)S(1)} %bitcast.26), channel_id=1, replica_groups=mesh['pipe'=4,'expert'=32] {'expert'}, dimensions={0} | all-to-all | bytes 11010048 | tf_op jit(solution)/shard_map/all_to_all | solution.py:52
  79.8 1.0 gather_matrix.1.gather
  80.8 6.8 %project.1 = (f32[384,512]{1,0:T(8,128)S(1)}, f32[384,512]{1,0:T(8,128)S(1)}, f32[384,512]{1,0:T(8,128)S(1)}) custom-call(s32[3]{0:T(128)S(1)} %pad_add_fusion.place, bf16[768,3584]{1,0:T(8,128)(2,1)S(1)} %bitcast.24, bf16[7168,512]{1,0:T(8,128)(2,1)S(1)} %bitcast.15, bf16[7168,512]{1,0:T(8,128)(2,1)S(1)} %bitcast.18, bf16[512,7168]{1,0:T(8,128)(2,1)} %bitcast.31), custom_call_target="tpu_custom_call" | custom-call | tf_op jit(solution)/shard_map/project/pallas_call | solution.py:259
  87.7 1.1 collective-permute-done.rows
  88.8 10.4 %expert.1 = (bf16[768,1792]{1,0:T(8,128)(2,1)S(1)}, bf16[384,512]{1,0:T(8,128)(2,1)S(1)}, bf16[384,512]{1,0:T(8,128)(2,1)S(1)}) custom-call(s32[3]{0:T(128)S(1)} %pad_add_fusion.place, bf16[768,3584]{1,0:T(8,128)(2,1)S(1)} %collective-permute-done.rows, bf16[7168,512]{1,0:T(8,128)(2,1)S(1)} %bitcast.16, bf16[7168,512]{1,0:T(8,128)(2,1)S(1)} %bitcast.19, ...), custom_call_target="tpu_custom_call" | custom-call | tf_op jit(solution)/shard_map/expert/pallas_call | solution.py:289
  99.2 0.4 collective-permute-start.1
  99.7 4.0 %mine_rows.1.mine = bf16[768,1792]{1,0:T(8,128)(2,1)S(1)} custom-call(s32[3]{0:T(128)S(1)} %pad_add_fusion.place, bf16[384,512]{1,0:T(8,128)(2,1)S(1)} %get-tuple-element.25.grad_gate, bf16[384,512]{1,0:T(8,128)(2,1)S(1)} %get-tuple-element.26.grad_up, bf16[7168,512]{1,0:T(8,128)(2,1)S(1)} %bitcast.17, bf16[7168,512]{1,0:T(8,128)(2,1)S(1)} %bitcast.20), custom_call_target="tpu_custom_call" | custom-call | tf_op jit(solution)/shard_map/mine_rows/pallas_call | solution.py:310
  103.7 0.9 collective-permute-done.1.other
  104.6 0.6 merge.1
  105.2 39.0 %all_to_all.11 = bf16[32,24,1792]{2,1,0:T(8,128)(2,1)S(1)} all-to-all(bf16[32,24,1792]{2,1,0:T(8,128)(2,1)S(1)} %bitcast.25), channel_id=1, replica_groups=mesh['pipe'=4,'expert'=32] {'expert'}, dimensions={0} | all-to-all | bytes 5505024 | tf_op jit(solution)/shard_map/all_to_all | solution.py:52
  144.3 1.1 token_sums.3.sent
  145.4 0.0 copy-start.3
  145.4 2.8 %collective-permute-start.2 = (bf16[128,1792]{1,0:T(8,128)(2,1)S(1)}, bf16[128,1792]{1,0:T(8,128)(2,1)S(1)}, u32[]{:S(2)}, u32[]{:S(2)}) collective-permute-start(bf16[128,1792]{1,0:T(8,128)(2,1)S(1)} %token_sums.3.sent), channel_id=1, source_target_pairs={{0,64},{64,0},{32,96},{96,32},{1,65},{65,1},{33,97},{97,33},{2,66}... | collective-permute-start | bytes 1376264 | tf_op jit(solution)/shard_map/ppermute | solution.py:46
  148.2 1.1 token_sums.2.kept
  149.3 0.9 row_products.1
  150.3 0.0 collective-permute-start.3
  150.3 1.2 collective-permute-done.3
  151.5 0.8 collective-permute-start.4
  152.3 5.4 %collective-permute-done.4.other_product = f32[8,128]{1,0:T(8,128)S(1)} collective-permute-done((f32[8,128]{1,0:T(8,128)S(1)}, f32[8,128]{1,0:T(8,128)S(1)}, u32[]{:S(2)}, u32[]{:S(2)}) %collective-permute-start.4) | collective-permute-done | bytes 4128 | tf_op jit(solution)/shard_map/ppermute | solution.py:46
  157.7 1.7 %final.1 = bf16[128,1792]{1,0:T(8,128)(2,1)} custom-call(s32[3]{0:T(128)S(1)} %pad_add_fusion.place, f32[128,1792]{1,0:T(8,128)S(1)} %token_sums.2.kept, bf16[128,1792]{1,0:T(8,128)(2,1)S(1)} %collective-permute-done.2.arrived, f32[8,128]{1,0:T(8,128)S(1)} %add.4.own_product, f32[8,128]{1,0:T(8,128)S(1)} %collective-permute-done.4.other_product, ...), custom_call_target="tpu_custom_call" | custom-call | tf_op jit(solution)/shard_map/final/pallas_call | solution.py:415
  (13 shorter events, 0.0 us)
Async XLA Ops:
  0.1 80.7 %slice-start = ((s8[7340032]{0:T(1024)(128)(4,1)}), s8[4194304]{0:T(1024)(128)(4,1)S(1)}, s32[]{:S(2)}) async-start(s8[7340032]{0:T(1024)(128)(4,1)} %bitcast.13), calls=%async_computation.2 | async-start | bytes 8388608
  4.8 76.0 %slice-start.1 = ((s8[7340032]{0:T(1024)(128)(4,1)}), s8[3145728]{0:T(1024)(128)(4,1)S(1)}, s32[]{:S(2)}) async-start(s8[7340032]{0:T(1024)(128)(4,1)} %bitcast.13), calls=%async_computation.3 | async-start | bytes 6291456
  4.8 76.0 %copy-start = (bf16[1,7168,512]{2,1,0:T(8,128)(2,1)S(1)}, bf16[1,7168,512]{2,1,0:T(8,128)(2,1)}, u32[]{:S(2)}) copy-start(bf16[1,7168,512]{2,1,0:T(8,128)(2,1)} %param.14) | copy-start | bytes 22020100
  79.8 9.0 %collective-permute-start = (bf16[768,3584]{1,0:T(8,128)(2,1)S(1)}, bf16[768,3584]{1,0:T(8,128)(2,1)S(1)}, u32[]{:S(2)}, u32[]{:S(2)}) collective-permute-start(bf16[768,3584]{1,0:T(8,128)(2,1)S(1)} %bitcast.23), channel_id=1, source_target_pairs={{0,32},{32,0},{64,96},{96,64},{1,33},{33,1},{65,97},{97,65},{2,34}... | collective-permute-start | bytes 16515080 | tf_op jit(solution)/shard_map/ppermute | solution.py:42
  99.2 5.4 %collective-permute-start.1 = (bf16[768,1792]{1,0:T(8,128)(2,1)S(1)}, bf16[768,1792]{1,0:T(8,128)(2,1)S(1)}, u32[]{:S(2)}, u32[]{:S(2)}) collective-permute-start(bf16[768,1792]{1,0:T(8,128)(2,1)S(1)} %get-tuple-element.27), channel_id=1, source_target_pairs={{0,32},{32,0},{64,96},{96,64},{1,33},{33,1},{65,97},{97,65},{2,34}... | collective-permute-start | bytes 8257544 | tf_op jit(solution)/shard_map/ppermute | solution.py:42
  145.4 3.9 %copy-start.1 = (bf16[128,7168]{1,0:T(8,128)(2,1)S(1)}, bf16[128,7168]{1,0:T(8,128)(2,1)}, u32[]{:S(2)}) copy-start(bf16[128,7168]{1,0:T(8,128)(2,1)} %tokens.3) | copy-start | bytes 5505028
  145.4 3.9 %copy-start.3 = (f32[7168]{0:T(1024)S(1)}, f32[7168]{0:T(1024)}, u32[]{:S(2)}) copy-start(f32[7168]{0:T(1024)} %param.10) | copy-start | bytes 86020
  145.4 12.3 %collective-permute-start.2 = (bf16[128,1792]{1,0:T(8,128)(2,1)S(1)}, bf16[128,1792]{1,0:T(8,128)(2,1)S(1)}, u32[]{:S(2)}, u32[]{:S(2)}) collective-permute-start(bf16[128,1792]{1,0:T(8,128)(2,1)S(1)} %token_sums.3.sent), channel_id=1, source_target_pairs={{0,64},{64,0},{32,96},{96,32},{1,65},{65,1},{33,97},{97,33},{2,66}... | collective-permute-start | bytes 1376264 | tf_op jit(solution)/shard_map/ppermute | solution.py:46
  149.3 8.4 %copy-start.2 = (bf16[128,7168]{1,0:T(8,128)(2,1)S(1)}, bf16[128,7168]{1,0:T(8,128)(2,1)}, u32[]{:S(2)}) copy-start(bf16[128,7168]{1,0:T(8,128)(2,1)} %cotangent.3) | copy-start | bytes 5505028
  150.3 1.2 collective-permute-start.3
  151.5 6.2 %collective-permute-start.4 = (f32[8,128]{1,0:T(8,128)S(1)}, f32[8,128]{1,0:T(8,128)S(1)}, u32[]{:S(2)}, u32[]{:S(2)}) collective-permute-start(f32[8,128]{1,0:T(8,128)S(1)} %add.4.own_product), channel_id=1, source_target_pairs={{0,64},{64,0},{32,96},{96,32},{1,65},{65,1},{33,97},{97,33},{2,66}... | collective-permute-start | bytes 12296 | tf_op jit(solution)/shard_map/ppermute | solution.py:46
